TPU v7x, 32 devices: a whole 2x2x4 slice. The times are simulated.
32 devices in a mesh: stations: 4 (over z), tm: 8 (over y, x, core).
Axes of the slice: x: 2, y: 2, z: 4, core: 2. Of those that a mesh axis runs over, the one named last changes fastest.
Arguments:
- patch_embedding_tensor: bfloat16 [16, 1024, 512], P('stations', 'tm'), may hold values from -6 to 6
- qkv_projector_matrix: bfloat16 [512, 1536], replicated, may hold values from -0.25 to 0.25
- closing_projector_matrix: bfloat16 [1024, 512], replicated, may hold values from -0.1875 to 0.1875
- logit_sharpness: float32 [8], replicated, may hold values from 0.5 to 2
- adjacent_group_table: int32 [16, 8], P('stations'), may hold values from 0 to 15, as said below
- adjacent_valid_tally: int32 [16], P('stations'), may hold values from 1 to 8
Outputs:
- encoded: bfloat16 [16, 1024, 512], P('stations', 'tm')
Inputs may be any that keep to these rules, and one draw needn't show every extreme that they name: `adjacent_group_table`: slot 0 of row g names g itself; every entry of row g lies within 4 of g.
All inputs are finite; a program needn't handle non-finite values.
Results may differ from a plain program's by a relative error of at most 0.0062.
Values may be sent and summed in bfloat16 or wider, within the bound.
No kernel may reach another device: no remote copies, remote signals or barrier semaphores. Data moves between devices by JAX's collectives and lax.ppermute only.
A program may use at most 128 MiB of HBM per device.

v0:
```python
import math

import jax
import jax.numpy as jnp
from jax import lax
from jax.sharding import PartitionSpec as P

NEAR = 4


def entering(value, axis, join, neutral):
    count, mine = (lax.axis_size(axis), lax.axis_index(axis))
    pieces = lax.all_gather(value, axis)
    subtotal = jnp.full_like(value, 0) + jnp.asarray(neutral, value.dtype)

    def turn(position, subtotal):
        longer = join(subtotal, pieces[position])
        return jnp.where(position < mine, longer, subtotal)

    return lax.fori_loop(0, count - 1, turn, subtotal)


def with_halo(value, sides, width):
    for axis, dim in sides:
        size, length = (lax.axis_size(axis), value.shape[dim])
        up = [(i, (i + 1) % size) for i in range(size - 1)]
        down = [(j, i) for i, j in up]
        last = lax.slice_in_dim(value, length - width, length, axis=dim)
        initial = lax.slice_in_dim(value, 0, width, axis=dim)
        before = lax.ppermute(last, axis, up)
        after = lax.ppermute(initial, axis, down)
        value = jnp.concatenate([before, value, after], axis=dim)
    return value


def head_norm(values, epsilon):
    return values * lax.rsqrt(jnp.mean(values * values, axis=-1, keepdims=True) + epsilon)


def keys_values(normed, weight_cols, channel_tally):
    group_count, patch_count, model_width = normed.shape
    channel_breadth = model_width // channel_tally
    projected = jnp.dot(
        normed.reshape(-1, model_width), weight_cols, preferred_element_type=jnp.float32
    )
    projected = projected.reshape(group_count, patch_count, 2, channel_tally, channel_breadth)
    key_rows = head_norm(projected[:, :, 0], 1e-06).astype(jnp.bfloat16)
    value_rows = projected[:, :, 1].astype(jnp.bfloat16)
    return (key_rows, value_rows)


def add_states(earlier, later):
    return earlier + later


def per_device(
    patch_embedding_tensor,
    qkv_projector_matrix,
    closing_projector_matrix,
    logit_sharpness,
    adjacent_group_table,
    adjacent_valid_tally,
):
    group_count, patch_count, model_width = patch_embedding_tensor.shape
    channel_tally = logit_sharpness.shape[0]
    channel_breadth = model_width // channel_tally
    inputs_f = patch_embedding_tensor.astype(jnp.float32)
    normed = head_norm(inputs_f, 1e-06).astype(jnp.bfloat16)
    queries_f = jnp.dot(
        normed.reshape(-1, model_width),
        qkv_projector_matrix[:, :model_width],
        preferred_element_type=jnp.float32,
    )
    queries = head_norm(
        queries_f.reshape(group_count, patch_count, channel_tally, channel_breadth), 1e-06
    ).astype(jnp.bfloat16)
    key_rows, value_rows = keys_values(normed, qkv_projector_matrix[:, model_width:], channel_tally)
    scores_time = jnp.einsum(
        "gthd,gshd->ghts", queries, key_rows, preferred_element_type=jnp.float32
    )
    positions = jnp.arange(patch_count, dtype=jnp.int32)
    causal = positions[:, None] >= positions[None, :]
    scores_time = jnp.where(causal[None, None], scores_time, 0.0).astype(jnp.bfloat16)
    local_part = jnp.einsum(
        "ghts,gshd->gthd", scores_time, value_rows, preferred_element_type=jnp.float32
    )
    states = jnp.einsum("gthd,gthe->ghde", key_rows, value_rows, preferred_element_type=jnp.float32)
    carried = entering(states, "tm", add_states, jnp.zeros_like(states))
    prefix_states = carried.astype(jnp.bfloat16)
    linear_sum = local_part + jnp.einsum(
        "gthd,ghde->gthe", queries, prefix_states, preferred_element_type=jnp.float32
    )
    linear_out = head_norm(linear_sum, 1e-05).astype(jnp.bfloat16)
    beside_all = with_halo(normed, (("stations", 0),), NEAR)
    lower_keys, lower_values = keys_values(
        beside_all[:NEAR], qkv_projector_matrix[:, model_width:], channel_tally
    )
    upper_keys, upper_values = keys_values(
        beside_all[NEAR + group_count :], qkv_projector_matrix[:, model_width:], channel_tally
    )
    window_keys = jnp.concatenate([lower_keys, key_rows, upper_keys], axis=0)
    window_values = jnp.concatenate([lower_values, value_rows, upper_values], axis=0)
    first = lax.axis_index("stations") * group_count
    window_ids = first - NEAR + jnp.arange(group_count + 2 * NEAR, dtype=jnp.int32)
    live_slots = (
        jnp.arange(adjacent_group_table.shape[1], dtype=jnp.int32)[None, :]
        < adjacent_valid_tally[:, None]
    )
    matches = (adjacent_group_table[:, :, None] == window_ids[None, None, :]) & live_slots[
        :, :, None
    ]
    multiplicity = jnp.sum(matches.astype(jnp.int32), axis=1).astype(jnp.float32)
    affinity_logits = jnp.einsum(
        "gthd,nthd->ghnt", queries, window_keys, preferred_element_type=jnp.float32
    )
    affinity_logits = affinity_logits * (
        logit_sharpness[None, :, None, None] / math.sqrt(channel_breadth)
    )
    exponent = multiplicity[:, None, :, None] * jnp.exp(affinity_logits)
    weights = (exponent / jnp.sum(exponent, axis=2, keepdims=True)).astype(jnp.bfloat16)
    gathered = jnp.einsum(
        "ghnt,nthd->gthd", weights, window_values, preferred_element_type=jnp.float32
    ).astype(jnp.bfloat16)
    joined = jnp.concatenate(
        [
            linear_out.reshape(group_count, patch_count, model_width),
            gathered.reshape(group_count, patch_count, model_width),
        ],
        axis=2,
    )
    mixed = jnp.dot(
        joined.reshape(-1, 2 * model_width),
        closing_projector_matrix,
        preferred_element_type=jnp.float32,
    )
    return (inputs_f + mixed.reshape(group_count, patch_count, model_width)).astype(jnp.bfloat16)


def solution(mesh):
    return jax.shard_map(
        per_device,
        mesh=mesh,
        in_specs=(P("stations", "tm", None), P(), P(), P(), P("stations", None), P("stations")),
        out_specs=P("stations", "tm", None),
        check_vma=False,
    )
```

profile of v0, /device:TPU:0, one launch (start us, length us, event | category | flops | bytes accessed | tf_op | source)
XLA Modules:
  0.0 100.3 jit_solution(47706209849533685)
XLA Ops:
  9.7 2.0 %fusion.6 = bf16[4,128,512]{2,1,0:T(8,128)(2,1)} fusion(bf16[4,128,512]{2,1,0:T(8,128)(2,1)} %param.8, f32[4,128]{1,0:T(4,128)S(1)} %add_rsqrt_fusion.5), kind=kLoop, calls=%fused_computation.16 | loop fusion | flops 786432 | bytes 1050624 | tf_op jit(solution)/shard_map/convert_element_type | solution.py:68
  11.7 1.8 %fusion.24 = f32[4,128,2,8,64]{1,4,3,2,0:T(8,128)S(1)} fusion(bf16[2,8,64,512,1]{3,2,1,0,4:T(8,128)(2,1)S(1)} %bitcast.89, bf16[4,128,512]{2,1,0:T(8,128)(2,1)} %fusion.6), kind=kOutput, calls=%fused_computation.51 | convolution fusion | flops 536870912 | bytes 3670016 | tf_op jit(solution)/shard_map/dot_general | solution.py:43
  18.4 6.4 %collective-permute-start = (bf16[4,128,512]{2,1,0:T(8,128)(2,1)}, bf16[4,128,512]{2,1,0:T(8,128)(2,1)}, u32[]{:S(2)}, u32[]{:S(2)}) collective-permute-start(bf16[4,128,512]{2,1,0:T(8,128)(2,1)} %fusion.6), channel_id=1, source_target_pairs={{0,8},{8,16},{16,24},{1,9},{9,17},{17,25},{2,10},{10,18},{18,26},{... | collective-permute-start | bytes 1572872 | tf_op jit(solution)/shard_map/ppermute | solution.py:30
  26.2 1.6 %multiply_reduce_fusion.4 = (f32[4,128,8]{1,2,0:T(8,128)S(1)}, f32[4,128,8,64]{1,3,2,0:T(8,128)S(1)}) fusion(bf16[8,64,512,1]{2,1,0,3:T(8,128)(2,1)S(1)} %bitcast.95, bf16[4,128,512]{2,1,0:T(8,128)(2,1)} %fusion.6), kind=kOutput, calls=%fused_computation.39 | convolution fusion | flops 268955648 | bytes 2113536 | tf_op jit(solution)/shard_map/dot_general | solution.py:69
  28.8 2.4 %copy.55 = bf16[4,128,8,64]{3,0,1,2:T(4,128)(2,1)} copy(bf16[4,128,8,64]{1,3,2,0:T(8,128)(2,1)} %multiply_convert_fusion.4) | data formatting | bytes 1048576 | tf_op jit(solution)/shard_map/convert_element_type | solution.py:76
  32.5 1.7 %collective-permute-done.1 = bf16[4,128,512]{2,1,0:T(8,128)(2,1)} collective-permute-done((bf16[4,128,512]{2,1,0:T(8,128)(2,1)}, bf16[4,128,512]{2,1,0:T(8,128)(2,1)}, u32[]{:S(2)}, u32[]{:S(2)}) %collective-permute-start.1) | collective-permute-done | bytes 524320 | tf_op jit(solution)/shard_map/ppermute | solution.py:31
  34.2 1.8 %fusion.18 = f32[4,128,2,8,64]{1,4,3,0,2:T(8,128)S(1)} fusion(bf16[2,8,64,512,1]{3,2,1,4,0:T(8,128)(2,1)S(1)} %bitcast.90, bf16[4,128,512]{2,1,0:T(8,128)(2,1)} %collective-permute-done.1), kind=kOutput, calls=%fused_computation.45 | convolution fusion | flops 536870912 | bytes 3670016 | tf_op jit(solution)/shard_map/dot_general | solution.py:43
  36.1 2.2 %fusion.20 = f32[4,128,2,8,64]{1,4,3,0,2:T(8,128)S(1)} fusion(bf16[2,8,64,512,1]{3,2,1,4,0:T(8,128)(2,1)S(1)} %bitcast.91, bf16[4,128,512]{2,1,0:T(8,128)(2,1)} %collective-permute-done), kind=kOutput, calls=%fused_computation.47 | convolution fusion | flops 536870912 | bytes 3670016 | tf_op jit(solution)/shard_map/dot_general | solution.py:43
  41.1 7.4 %copy.56 = bf16[12,128,8,64]{3,0,2,1:T(8,128)(2,1)} copy(bf16[12,128,8,64]{1,3,2,0:T(8,128)(2,1)} %pad_maximum_fusion) | data formatting | bytes 3145728 | tf_op jit(solution)/shard_map/concatenate | solution.py:102
  48.5 1.6 %multiply_reduce_fusion = f32[4,128,8]{1,2,0:T(8,128)S(1)} fusion(f32[4,128,2,8,64]{1,4,3,0,2:T(8,128)} %copy-done.2), kind=kLoop, calls=%fused_computation.30 | loop fusion | flops 520192 | bytes 1064960 | tf_op jit(solution)/shard_map/reduce_sum | solution.py:37
  54.4 5.6 %copy.54 = bf16[12,128,8,64]{3,0,1,2:T(8,128)(2,1)} copy(bf16[12,128,8,64]{1,3,2,0:T(8,128)(2,1)} %pad_maximum_fusion.1) | data formatting | bytes 3145728 | tf_op jit(solution)/shard_map/concatenate | solution.py:101
  59.9 6.7 %divide_convert_fusion = bf16[4,8,12,128]{2,0,3,1:T(4,128)(2,1)} fusion(bf16[12,128,8,64]{3,0,1,2:T(8,128)(2,1)} %copy.54, bf16[4,128,8,64]{3,0,1,2:T(4,128)(2,1)} %copy.55, f32[8]{0:T(128)S(1)} %broadcast_multiply_fusion, f32[4,12]{1,0:T(4,128)S(1)} %convert_element_type.72), kind=kOutput, calls=%fused_computation.3 | convolution fusion | flops 6492171 | bytes 2195680 | tf_op jit(solution)/shard_map/div | solution.py:120
  66.6 4.9 %fusion.3 = bf16[4,128,8,64]{3,0,2,1:T(4,128)(2,1)} fusion(bf16[12,128,8,64]{3,0,2,1:T(8,128)(2,1)} %copy.56, bf16[4,8,12,128]{2,0,3,1:T(4,128)(2,1)} %divide_convert_fusion), kind=kOutput, calls=%fused_computation.13 | convolution fusion | flops 6553600 | bytes 2195456 | tf_op jit(solution)/shard_map/ghnt,nthd->gthd/dot_general | solution.py:121
  71.5 1.9 %copy.58 = bf16[4,128,8,64]{1,3,2,0:T(8,128)(2,1)S(1)} copy(bf16[4,128,8,64]{3,0,2,1:T(4,128)(2,1)} %fusion.3) | data formatting | bytes 1048576 | tf_op jit(solution)/shard_map/convert_element_type | solution.py:123
  74.5 11.3 %while.14 = (s32[]{:T(128)}, f32[4,8,64,64]{3,2,1,0:T(8,128)S(1)}, s32[]{:T(128)}, f32[8,4,8,64,64]{4,3,2,1,0:T(8,128)}, s32[]{:T(128)}, /*index=5*/s32[]{:T(128)}) while((s32[]{:T(128)}, f32[4,8,64,64]{3,2,1,0:T(8,128)S(1)}, s32[]{:T(128)}, f32[8,4,8,64,64]{4,3,2,1,0:T(8,128)}, s32[]{:T(128)}, /*index=5*/s32[]{:T(128)}) %tuple.39), condition=%wide.region_4.5_spmd.clone, body=%wide.region_3.4_spmd.clone.sunk | while | flops 393220 | bytes 1572965 | solution.py:20
  74.5 1.6 %add_select_fusion.2 = f32[4,8,64,64]{3,2,1,0:T(8,128)S(1)} fusion(f32[4,8,64,64]{3,2,1,0:T(8,128)S(1)} %get-tuple-element.144, f32[8,4,8,64,64]{4,3,2,1,0:T(8,128)} %get-tuple-element.152, s32[]{:T(128)S(6)} %copy.73, pred[]{:T(512)S(6)} %compare.3, pred[]{:T(512)S(6)} %lt.44), kind=kLoop, calls=%fused_computation.clone.1 | loop fusion | flops 393216 | bytes 1572870 | tf_op jit(solution)/shard_map/while/body/eval_jaxpr/jit(_where)/select_n | solution.py:18
  76.1 1.6 %add_select_fusion.2 = f32[4,8,64,64]{3,2,1,0:T(8,128)S(1)} fusion(f32[4,8,64,64]{3,2,1,0:T(8,128)S(1)} %get-tuple-element.144, f32[8,4,8,64,64]{4,3,2,1,0:T(8,128)} %get-tuple-element.152, s32[]{:T(128)S(6)} %copy.73, pred[]{:T(512)S(6)} %compare.3, pred[]{:T(512)S(6)} %lt.44), kind=kLoop, calls=%fused_computation.clone.1 | loop fusion | flops 393216 | bytes 1572870 | tf_op jit(solution)/shard_map/while/body/eval_jaxpr/jit(_where)/select_n | solution.py:18
  77.7 1.6 %add_select_fusion.2 = f32[4,8,64,64]{3,2,1,0:T(8,128)S(1)} fusion(f32[4,8,64,64]{3,2,1,0:T(8,128)S(1)} %get-tuple-element.144, f32[8,4,8,64,64]{4,3,2,1,0:T(8,128)} %get-tuple-element.152, s32[]{:T(128)S(6)} %copy.73, pred[]{:T(512)S(6)} %compare.3, pred[]{:T(512)S(6)} %lt.44), kind=kLoop, calls=%fused_computation.clone.1 | loop fusion | flops 393216 | bytes 1572870 | tf_op jit(solution)/shard_map/while/body/eval_jaxpr/jit(_where)/select_n | solution.py:18
  79.4 1.6 %add_select_fusion.2 = f32[4,8,64,64]{3,2,1,0:T(8,128)S(1)} fusion(f32[4,8,64,64]{3,2,1,0:T(8,128)S(1)} %get-tuple-element.144, f32[8,4,8,64,64]{4,3,2,1,0:T(8,128)} %get-tuple-element.152, s32[]{:T(128)S(6)} %copy.73, pred[]{:T(512)S(6)} %compare.3, pred[]{:T(512)S(6)} %lt.44), kind=kLoop, calls=%fused_computation.clone.1 | loop fusion | flops 393216 | bytes 1572870 | tf_op jit(solution)/shard_map/while/body/eval_jaxpr/jit(_where)/select_n | solution.py:18
  81.0 1.6 %add_select_fusion.2 = f32[4,8,64,64]{3,2,1,0:T(8,128)S(1)} fusion(f32[4,8,64,64]{3,2,1,0:T(8,128)S(1)} %get-tuple-element.144, f32[8,4,8,64,64]{4,3,2,1,0:T(8,128)} %get-tuple-element.152, s32[]{:T(128)S(6)} %copy.73, pred[]{:T(512)S(6)} %compare.3, pred[]{:T(512)S(6)} %lt.44), kind=kLoop, calls=%fused_computation.clone.1 | loop fusion | flops 393216 | bytes 1572870 | tf_op jit(solution)/shard_map/while/body/eval_jaxpr/jit(_where)/select_n | solution.py:18
  82.6 1.6 %add_select_fusion.2 = f32[4,8,64,64]{3,2,1,0:T(8,128)S(1)} fusion(f32[4,8,64,64]{3,2,1,0:T(8,128)S(1)} %get-tuple-element.144, f32[8,4,8,64,64]{4,3,2,1,0:T(8,128)} %get-tuple-element.152, s32[]{:T(128)S(6)} %copy.73, pred[]{:T(512)S(6)} %compare.3, pred[]{:T(512)S(6)} %lt.44), kind=kLoop, calls=%fused_computation.clone.1 | loop fusion | flops 393216 | bytes 1572870 | tf_op jit(solution)/shard_map/while/body/eval_jaxpr/jit(_where)/select_n | solution.py:18
  84.2 1.6 %add_select_fusion.2 = f32[4,8,64,64]{3,2,1,0:T(8,128)S(1)} fusion(f32[4,8,64,64]{3,2,1,0:T(8,128)S(1)} %get-tuple-element.144, f32[8,4,8,64,64]{4,3,2,1,0:T(8,128)} %get-tuple-element.152, s32[]{:T(128)S(6)} %copy.73, pred[]{:T(512)S(6)} %compare.3, pred[]{:T(512)S(6)} %lt.44), kind=kLoop, calls=%fused_computation.clone.1 | loop fusion | flops 393216 | bytes 1572870 | tf_op jit(solution)/shard_map/while/body/eval_jaxpr/jit(_where)/select_n | solution.py:18
  87.2 2.7 %multiply_reduce_fusion.2 = (f32[4,128,8]{1,2,0:T(8,128)S(1)}, f32[4,128,8,64]{1,3,2,0:T(8,128)S(1)}) fusion(f32[4,8,64,128]{3,2,1,0:T(8,128)} %fusion.26, bf16[4,128,8,64]{1,3,2,0:T(8,128)(2,1)S(1)} %copy-done.5, bf16[4,128,8,64]{1,3,2,0:T(8,128)(2,1)S(1)} %copy-done.7, pred[128,128]{1,0:T(8,128)(4,1)S(1)} %iota_compare_fusion, ...), kind=kOutput, calls=%fused_computation.34 | convolution fusion | flops 136048640 | bytes 3702784 | tf_op jit(solution)/shard_map/ghts,gshd->gthd/dot_general | solution.py:84
  90.9 2.5 %fusion.4 = bf16[4,128,512]{2,1,0:T(8,128)(2,1)} fusion(bf16[4,128,512]{2,1,0:T(8,128)(2,1)S(1)} %copy-done.8, bf16[4,128,512]{2,1,0:T(8,128)(2,1)} %copy.60, bf16[4,128,512]{2,1,0:T(8,128)(2,1)S(1)} %copy.59, bf16[1024,512]{1,0:T(8,128)(2,1)S(1)} %copy-done), kind=kOutput, calls=%fused_computation.14 | convolution fusion | flops 539754496 | bytes 3145728 | tf_op jit(solution)/shard_map/dot_general | solution.py:131
  (63 shorter events, 22.2 us)
Async XLA Ops:
  6.5 83.8 %copy-start = (bf16[1024,512]{1,0:T(8,128)(2,1)S(1)}, bf16[1024,512]{1,0:T(8,128)(2,1)}, u32[]{:S(2)}) copy-start(bf16[1024,512]{1,0:T(8,128)(2,1)} %param.10) | copy-start | bytes 3145732
  6.5 67.9 %all-gather.3.cloned.1.call-start = ((), (), s32[]{:S(2)}) async-start(), calls=%async_computation | async-start | bytes 9437184 | tf_op jit(solution)/shard_map/all_gather | solution.py:13
  13.5 1.4 %copy-start.1 = (f32[4,128,2,8,64]{1,4,3,2,0:T(8,128)}, f32[4,128,2,8,64]{1,4,3,2,0:T(8,128)S(1)}, u32[]{:S(2)}) copy-start(f32[4,128,2,8,64]{1,4,3,2,0:T(8,128)S(1)} %fusion.24) | copy-start | bytes 6291460
  14.9 0.8 copy-start.6
  17.0 9.0 %copy-start.10 = (s32[4]{0:T(128)S(1)}, s32[4]{0:T(128)}, u32[]{:S(2)}) copy-start(s32[4]{0:T(128)} %param.13) | copy-start | bytes 52
  17.0 9.1 %copy-start.9 = (s32[4,8]{1,0:T(4,128)S(1)}, s32[4,8]{1,0:T(4,128)}, u32[]{:S(2)}) copy-start(s32[4,8]{1,0:T(4,128)} %param.12) | copy-start | bytes 388
  17.1 17.2 %collective-permute-start.1 = (bf16[4,128,512]{2,1,0:T(8,128)(2,1)}, bf16[4,128,512]{2,1,0:T(8,128)(2,1)}, u32[]{:S(2)}, u32[]{:S(2)}) collective-permute-start(bf16[4,128,512]{2,1,0:T(8,128)(2,1)} %fusion.6), channel_id=1, source_target_pairs={{8,0},{16,8},{24,16},{9,1},{17,9},{25,17},{10,2},{18,10},{26,18},{... | collective-permute-start | bytes 1572872 | tf_op jit(solution)/shard_map/ppermute | solution.py:31
  18.4 17.7 %collective-permute-start = (bf16[4,128,512]{2,1,0:T(8,128)(2,1)}, bf16[4,128,512]{2,1,0:T(8,128)(2,1)}, u32[]{:S(2)}, u32[]{:S(2)}) collective-permute-start(bf16[4,128,512]{2,1,0:T(8,128)(2,1)} %fusion.6), channel_id=1, source_target_pairs={{0,8},{8,16},{16,24},{1,9},{9,17},{17,25},{2,10},{10,18},{18,26},{... | collective-permute-start | bytes 1572872 | tf_op jit(solution)/shard_map/ppermute | solution.py:30
  27.8 3.4 %copy-start.11 = (f32[8]{0:T(128)S(1)}, f32[8]{0:T(128)}, u32[]{:S(2)}) copy-start(f32[8]{0:T(128)} %param.11) | copy-start | bytes 100
  36.0 2.3 %copy-start.2 = (f32[4,128,2,8,64]{1,4,3,0,2:T(8,128)}, f32[4,128,2,8,64]{1,4,3,0,2:T(8,128)S(1)}, u32[]{:S(2)}) copy-start(f32[4,128,2,8,64]{1,4,3,0,2:T(8,128)S(1)} %fusion.18) | copy-start | bytes 6291460
  38.3 1.3 %copy-start.4 = (f32[4,128,2,8,64]{1,4,3,0,2:T(8,128)}, f32[4,128,2,8,64]{1,4,3,0,2:T(8,128)S(1)}, u32[]{:S(2)}) copy-start(f32[4,128,2,8,64]{1,4,3,0,2:T(8,128)S(1)} %fusion.20) | copy-start | bytes 6291460
  48.5 3.0 %copy-start.3 = (f32[4,128,2,8,64]{1,4,3,0,2:T(8,128)S(1)}, f32[4,128,2,8,64]{1,4,3,0,2:T(8,128)}, u32[]{:S(2)}) copy-start(f32[4,128,2,8,64]{1,4,3,0,2:T(8,128)} %copy-done.2) | copy-start | bytes 6291460
  50.1 2.9 %copy-start.7 = (bf16[4,128,8,64]{1,3,2,0:T(8,128)(2,1)S(1)}, bf16[4,128,8,64]{1,3,2,0:T(8,128)(2,1)}, u32[]{:S(2)}) copy-start(bf16[4,128,8,64]{1,3,2,0:T(8,128)(2,1)} %copy-done.6) | copy-start | bytes 1572868
  74.5 11.4 %copy-start.5 = (bf16[4,128,8,64]{1,3,2,0:T(8,128)(2,1)S(1)}, bf16[4,128,8,64]{1,3,2,0:T(8,128)(2,1)}, u32[]{:S(2)}) copy-start(bf16[4,128,8,64]{1,3,2,0:T(8,128)(2,1)} %multiply_convert_fusion.4) | copy-start | bytes 1572868
  89.9 1.0 %copy-start.8 = (bf16[4,128,512]{2,1,0:T(8,128)(2,1)S(1)}, bf16[4,128,512]{2,1,0:T(8,128)(2,1)}, u32[]{:S(2)}) copy-start(bf16[4,128,512]{2,1,0:T(8,128)(2,1)} %param.8) | copy-start | bytes 1572868
Sparse Core Ops, SparseCore 0:
  17.2 57.0 all-gather.2
where the time goes:
time: 101 us; the launch traced here: 100 us
  local copies, waits for them, and re-layouts  27.1 us (27%)
  matrix products  26.8 us (27%)
  other arithmetic  23.1 us (23%)
  between operations  13.7 us (14%)
  starting transfers between devices  7.65 us (8%)
  waiting for transfers between devices  1.75 us (2%)
    select_n x7, other arithmetic, turn(): return jnp.where(position < mine, longer, subtotal)  11.2 us
    concatenate x1, local copies, waits for them, and re-layouts, per_device(): jnp.concatenate([lower_values, value_rows, upper_values], axis=0)  7.43 us
    div x1, matrix products, per_device(): exponent / jnp.sum(exponent, axis=2, keepdims=True)  6.66 us
    ppermute x1, starting transfers between devices, with_halo(): before = lax.ppermute(last, axis, up)  6.35 us
    dot_general x3, matrix products, keys_values(): jnp.dot(normed.reshape(-1, model_width), weight_cols, preferred_element_t...  5.73 us
    concatenate x1, local copies, waits for them, and re-layouts, per_device(): window_keys = jnp.concatenate([lower_keys, key_rows, upper_keys], axis=0)  5.55 us
    dot_general x1, matrix products, per_device(): jnp.einsum('ghnt,nthd->gthd', weights, window_values, preferred_element_t...  4.9 us
    reduce_sum x4, other arithmetic, head_norm(): jnp.mean(values * values, axis=-1, keepdims=True) + epsilon  4.3 us
  transfers between devices with their start and end apart: 3, of which 1 were waited for; matrix products, arithmetic and copies ran while one was open for 46% of the time, Pallas kernels for 0%

commit v1 on v0

v1 whole, which is shorter than its diff:
```python
import functools
import math

import jax
import jax.numpy as jnp
from jax import lax
from jax.experimental import pallas as pl
from jax.experimental.pallas import tpu as pltpu
from jax.sharding import PartitionSpec as P

NEAR = 4
HALF = 256
T = 32
F32 = jnp.float32
BF16 = jnp.bfloat16
VMEM = pltpu.VMEM
SMEM = pltpu.SMEM


def dot(a, b):
    return jnp.dot(a, b, preferred_element_type=F32)


def dot_nt(a, b):
    return lax.dot_general(a, b, (((1,), (1,)), ((), ())), preferred_element_type=F32)


def dot_tn(a, b):
    return lax.dot_general(a, b, (((0,), (0,)), ((), ())), preferred_element_type=F32)


def row_norm(x):
    xf = x.astype(F32)
    return (xf * lax.rsqrt(jnp.mean(xf * xf, axis=-1, keepdims=True) + 1e-06)).astype(BF16)


def head_ids(shape, axis, breadth):
    return lax.broadcasted_iota(jnp.int32, shape, axis) // breadth


def mean_matrix(breadth):
    same = head_ids((HALF, HALF), 0, breadth) == head_ids((HALF, HALF), 1, breadth)
    return jnp.where(same, 1.0 / breadth, 0.0).astype(BF16)


def head_norm(values, means, epsilon):
    square = (values * values).astype(BF16)
    return (values * lax.rsqrt(dot(square, means) + epsilon)).astype(BF16)


def own_head(values, j, breadth):
    ids = head_ids(values.shape, 1, breadth)
    return jnp.where(ids == j, values, jnp.zeros_like(values))


def multiplicity_mask(table_ref, tally_ref, base):
    groups, slots = table_ref.shape
    wide = groups * T
    ids = base + lax.broadcasted_iota(jnp.int32, (8, wide), 1) // T
    rows = []
    for g in range(groups):
        total = jnp.zeros((8, wide), F32)
        for j in range(slots):
            total += jnp.where((ids == table_ref[g, j]) & (j < tally_ref[g]), 1.0, 0.0)
        rows.append(jnp.broadcast_to(total[:1], (T, wide)))
    full = jnp.concatenate(rows, axis=0)
    t_row = lax.broadcasted_iota(jnp.int32, (wide, wide), 0) % T
    t_col = lax.broadcasted_iota(jnp.int32, (wide, wide), 1) % T
    return jnp.where(t_row == t_col, full, 0.0)


def neighbour_chunk(q, k, v, mask, sharp, breadth):
    heads = HALF // breadth
    shares = []
    for j in range(heads):
        score = dot_nt(q, own_head(k, j, breadth))
        shares.append((jnp.exp2(score * sharp[j]) * mask).astype(BF16))
    share = jnp.concatenate(shares, axis=1)
    spread = jnp.concatenate([own_head(v, j, breadth) for j in range(heads)], axis=0)
    ones = jnp.concatenate([own_head(jnp.ones_like(v), j, breadth) for j in range(heads)], axis=0)
    return dot(share, spread), dot(share, ones)


def sharpness_of(sharp_ref, first, heads, breadth):
    scale = math.log2(math.e) / math.sqrt(breadth)
    return [sharp_ref[first + j] * scale for j in range(heads)]


def cut(ref, c, h):
    groups = ref.shape[0]
    return ref[:, c * T : (c + 1) * T, h * HALF : (h + 1) * HALF].reshape(groups * T, HALF)


def states_kernel(breadth, x_ref, w_ref, n_ref, k_ref, v_ref, keep_ref, give_ref):
    groups, patches, width = x_ref.shape
    core = lax.axis_index("tm") % 2
    means = mean_matrix(breadth)
    normed = row_norm(x_ref[...].reshape(groups * patches, width))
    n_ref[...] = normed.reshape(n_ref.shape)
    for h in range(width // HALF):
        at = slice(h * HALF, (h + 1) * HALF)
        k = head_norm(dot(normed, w_ref[:, width + h * HALF : width + (h + 1) * HALF]), means, 1e-06)
        v = dot(normed, w_ref[:, 2 * width + h * HALF : 2 * width + (h + 1) * HALF]).astype(BF16)
        k_ref[:, :, at] = k.reshape(groups, patches, HALF)
        v_ref[:, :, at] = v.reshape(groups, patches, HALF)
        states = []
        for g in range(groups):
            rows = slice(g * patches, (g + 1) * patches)
            full = dot_tn(k[rows], v[rows])
            state = jnp.zeros((breadth, HALF), F32)
            for j in range(HALF // breadth):
                state += own_head(full[j * breadth : (j + 1) * breadth], j, breadth)
            states.append(state)

        @pl.when(core == h)
        def _():
            for g in range(groups):
                keep_ref[g] = states[g]

        @pl.when(core != h)
        def _():
            for g in range(groups):
                give_ref[g] = states[g].astype(BF16)


def own_kernel(breadth, n_ref, w_ref, k_ref, v_ref, sharp_ref, table_ref, tally_ref, q_ref, lin_ref, num_ref, den_ref):
    groups, patches, width = n_ref.shape
    heads = HALF // breadth
    means = mean_matrix(breadth)
    normed = n_ref[...].reshape(groups * patches, width)
    causal = lax.broadcasted_iota(jnp.int32, (patches, patches), 0) >= lax.broadcasted_iota(jnp.int32, (patches, patches), 1)
    mask = multiplicity_mask(table_ref, tally_ref, lax.axis_index("stations") * groups)
    for h in range(width // HALF):
        at = slice(h * HALF, (h + 1) * HALF)
        q = head_norm(dot(normed, w_ref[:, at]), means, 1e-06)
        q_ref[:, :, at] = q.reshape(groups, patches, HALF)
        for g in range(groups):
            k, v = k_ref[g, :, at], v_ref[g, :, at]
            qg = q[g * patches : (g + 1) * patches]
            scores = [jnp.where(causal, dot_nt(qg, own_head(k, j, breadth)), 0.0).astype(BF16) for j in range(heads)]
            spread = jnp.concatenate([own_head(v, j, breadth) for j in range(heads)], axis=0)
            lin_ref[g, :, at] = dot(jnp.concatenate(scores, axis=1), spread)
        sharp = sharpness_of(sharp_ref, h * heads, heads, breadth)
        for c in range(patches // T):
            num, den = neighbour_chunk(cut(q_ref, c, h), cut(k_ref, c, h), cut(v_ref, c, h), mask, sharp, breadth)
            span = slice(c * T, (c + 1) * T)
            num_ref[:, span, at] = num.reshape(groups, T, HALF)
            den_ref[:, span, at] = den.reshape(groups, T, HALF)


def halo(breadth, base, x_ref, w_ref, q_ref, sharp_ref, table_ref, tally_ref, num_ref, den_ref, k_ref, v_ref, emit):
    groups, patches, width = x_ref.shape
    heads = HALF // breadth
    means = mean_matrix(breadth)
    normed = row_norm(x_ref[...].reshape(groups * patches, width))
    mask = multiplicity_mask(table_ref, tally_ref, base)
    for h in range(width // HALF):
        at = slice(h * HALF, (h + 1) * HALF)
        k = head_norm(dot(normed, w_ref[:, width + h * HALF : width + (h + 1) * HALF]), means, 1e-06)
        v = dot(normed, w_ref[:, 2 * width + h * HALF : 2 * width + (h + 1) * HALF]).astype(BF16)
        k_ref[...] = k.reshape(groups, patches, HALF)
        v_ref[...] = v.reshape(groups, patches, HALF)
        sharp = sharpness_of(sharp_ref, h * heads, heads, breadth)
        for c in range(patches // T):
            num, den = neighbour_chunk(cut(q_ref, c, h), cut(k_ref, c, 0), cut(v_ref, c, 0), mask, sharp, breadth)
            span = slice(c * T, (c + 1) * T)
            emit(span, at, num.reshape(groups, T, HALF) + num_ref[:, span, at], den.reshape(groups, T, HALF) + den_ref[:, span, at])


def even_kernel(breadth, x_ref, w_ref, q_ref, sharp_ref, table_ref, tally_ref, num_ref, den_ref, num_out, den_out, k_ref, v_ref):
    base = (lax.axis_index("stations") ^ 1) * x_ref.shape[0]

    def emit(span, at, num, den):
        num_out[:, span, at] = num
        den_out[:, span, at] = den

    halo(breadth, base, x_ref, w_ref, q_ref, sharp_ref, table_ref, tally_ref, num_ref, den_ref, k_ref, v_ref, emit)


def odd_kernel(breadth, x_ref, w_ref, q_ref, sharp_ref, table_ref, tally_ref, num_ref, den_ref, own_ref, close_ref, y_ref, k_ref, v_ref, gathered_ref):
    groups, patches, width = x_ref.shape
    station = lax.axis_index("stations")
    base = (station + 2 * (station % 2) - 1) * groups

    def emit(span, at, num, den):
        gathered_ref[:, span, at] = (num / den).astype(BF16)

    halo(breadth, base, x_ref, w_ref, q_ref, sharp_ref, table_ref, tally_ref, num_ref, den_ref, k_ref, v_ref, emit)
    mixed = dot(gathered_ref[...].reshape(groups * patches, width), close_ref[width:, :])
    y_ref[...] = own_ref[...].astype(F32) + mixed.reshape(groups, patches, width)


def closing_kernel(breadth, q_ref, lin_ref, mine_ref, other_ref, close_ref, y_ref, out_ref, normed_ref):
    groups, patches, width = q_ref.shape
    heads = HALF // breadth
    core = lax.axis_index("tm") % 2
    means = mean_matrix(breadth)
    same = head_ids((HALF, HALF), 0, breadth) == head_ids((HALF, HALF), 1, breadth)
    for h in range(width // HALF):
        at = slice(h * HALF, (h + 1) * HALF)
        for g in range(groups):
            state = jnp.where(core == h, mine_ref[g], other_ref[g].astype(F32))
            block = jnp.where(same, jnp.concatenate([state] * heads, axis=0), 0.0).astype(BF16)
            total = lin_ref[g, :, at] + dot(q_ref[g, :, at], block)
            normed_ref[g, :, at] = head_norm(total, means, 1e-05)
    mixed = dot(normed_ref[...].reshape(groups * patches, width), close_ref[:width, :])
    out_ref[...] = (y_ref[...] + mixed.reshape(groups, patches, width)).astype(BF16)


def call(kernel, breadth, outs, args, scratch=(), flops=10**9, name=None):
    def place(a):
        return pl.BlockSpec(memory_space=SMEM if a.size <= 64 else VMEM)

    return pl.pallas_call(
        functools.partial(kernel, breadth),
        out_shape=[jax.ShapeDtypeStruct(s, d) for s, d in outs],
        in_specs=[place(a) for a in args],
        out_specs=[pl.BlockSpec(memory_space=VMEM) for _ in outs],
        scratch_shapes=[pltpu.VMEM(s, d) for s, d in scratch],
        compiler_params=pltpu.CompilerParams(vmem_limit_bytes=24 * 2**20),
        cost_estimate=pl.CostEstimate(flops=flops, bytes_accessed=2**20, transcendentals=0),
        name=name,
    )(*args)


def swap_with(value, axis, partner):
    size = lax.axis_size(axis)
    pairs = [(i, partner(i)) for i in range(size) if 0 <= partner(i) < size]
    return lax.ppermute(value, axis, pairs)


def entering(keep, give):
    core, chip = lax.axis_index("tm") % 2, lax.axis_index("tm") // 2
    chips = lax.axis_size("tm") // 2
    got = swap_with(give, "tm", lambda i: i ^ 1)
    total = (keep + got.astype(F32)).astype(BF16)
    before = jnp.zeros_like(keep)
    for m in range(1, chips):
        piece = swap_with(total, "tm", lambda i: i ^ (2 * m))
        before += jnp.where((chip ^ m) < chip, piece.astype(F32), 0.0)
    send = (before + jnp.where(core == 0, keep, 0.0)).astype(BF16)
    mine = before + jnp.where(core == 0, 0.0, got.astype(F32))
    other = swap_with(send, "tm", lambda i: i ^ 1)
    return mine, other


def per_device(x, w, close, sharp, table, tally):
    groups, patches, width = x.shape
    breadth = width // sharp.shape[0]
    x_odd = swap_with(x, "stations", lambda i: i + 2 * (i % 2) - 1)
    x_even = swap_with(x, "stations", lambda i: i ^ 1)
    block = x.shape
    part = (groups, breadth, HALF)
    normed, k, v, keep, give = call(
        states_kernel, breadth, [(block, BF16)] * 3 + [(part, F32), (part, BF16)], (x, w), name="states"
    )
    mine, other = entering(keep, give)
    q, lin, num, den = call(
        own_kernel, breadth, [(block, BF16)] + [(block, F32)] * 3, (normed, w, k, v, sharp, table, tally), name="own"
    )
    half = [((groups, patches, HALF), BF16)] * 2
    num, den = call(
        even_kernel, breadth, [(block, F32)] * 2, (x_even, w, q, sharp, table, tally, num, den), half, name="even"
    )
    (y,) = call(
        odd_kernel,
        breadth,
        [(block, F32)],
        (x_odd, w, q, sharp, table, tally, num, den, x, close),
        half + [(block, BF16)],
        name="odd",
    )
    (out,) = call(
        closing_kernel, breadth, [(block, BF16)], (q, lin, mine, other, close, y), [(block, BF16)], name="closing"
    )
    return out


def solution(mesh):
    return jax.shard_map(
        per_device,
        mesh=mesh,
        in_specs=(P("stations", "tm", None), P(), P(), P(), P("stations", None), P("stations")),
        out_specs=P("stations", "tm", None),
        check_vma=False,
    )
```

time: 101 us -> 34.7 us (0.34)
  the two profiles are of different devices: /device:TPU:0 before, /device:TPU:9 now
where the time goes in v1:
time: 34.7 us; the launch traced here: 34.4 us
  Pallas kernels  18.1 us (52%)
  starting transfers between devices  9.28 us (27%)
  local copies, waits for them, and re-layouts  5.08 us (15%)
  other arithmetic  1.84 us (5%)
    pallas_call x5, Pallas kernels, call(): pl.pallas_call(functools.partial(kernel, breadth), out_shape=[jax.ShapeDt...  18.1 us
    ppermute x7, starting transfers between devices, swap_with(): return lax.ppermute(value, axis, pairs)  9.28 us
    unnamed x20, local copies, waits for them, and re-layouts  5.08 us
    convert_element_type x1, other arithmetic, entering(): send = (before + jnp.where(core == 0, keep, 0.0)).astype(BF16)  1.16 us
  transfers between devices with their start and end apart: 7, of which 0 were waited for; matrix products, arithmetic and copies ran while one was open for 5% of the time, Pallas kernels for 38%

profile of v1, /device:TPU:9, one launch (start us, length us, event | category | flops | bytes accessed | tf_op | source)
XLA Modules:
  0.0 34.4 jit_solution(17635369877916224996)
XLA Ops:
  0.0 1.4 %copy-done = bf16[512,1536]{1,0:T(8,128)(2,1)S(1)} copy-done((bf16[512,1536]{1,0:T(8,128)(2,1)S(1)}, bf16[512,1536]{1,0:T(8,128)(2,1)}, u32[]{:S(2)}) %copy-start) | copy-done | bytes 1572888
  1.4 3.3 %states.1 = (bf16[4,128,512]{2,1,0:T(8,128)(2,1)S(1)}, bf16[4,128,512]{2,1,0:T(8,128)(2,1)S(1)}, bf16[4,128,512]{2,1,0:T(8,128)(2,1)S(1)}, f32[4,64,256]{2,1,0:T(8,128)S(1)}, bf16[4,64,256]{2,1,0:T(8,128)(2,1)S(1)}) custom-call(bf16[4,128,512]{2,1,0:T(8,128)(2,1)} %own_ref.1, bf16[512,1536]{1,0:T(8,128)(2,1)S(1)} %copy-done), custom_call_target="tpu_custom_call" | custom-call | flops 1000000000 | bytes 1048576 | tf_op jit(solution)/shard_map/states/pallas_call | solution.py:214
  4.7 0.0 copy-start.6
  4.7 0.8 %copy-done.6 = bf16[4,128,512]{2,1,0:T(8,128)(2,1)} copy-done((bf16[4,128,512]{2,1,0:T(8,128)(2,1)}, bf16[4,128,512]{2,1,0:T(8,128)(2,1)S(1)}, u32[]{:S(2)}) %copy-start.6) | copy-done | bytes 524312
  5.5 0.8 %copy-done.8 = bf16[4,128,512]{2,1,0:T(8,128)(2,1)} copy-done((bf16[4,128,512]{2,1,0:T(8,128)(2,1)}, bf16[4,128,512]{2,1,0:T(8,128)(2,1)S(1)}, u32[]{:S(2)}) %copy-start.8) | copy-done | bytes 524312
  6.3 0.7 %collective-permute-start = (bf16[4,64,256]{2,1,0:T(8,128)(2,1)S(1)}, bf16[4,64,256]{2,1,0:T(8,128)(2,1)S(1)}, u32[]{:S(2)}, u32[]{:S(2)}) collective-permute-start(bf16[4,64,256]{2,1,0:T(8,128)(2,1)S(1)} %get-tuple-element.22), channel_id=1, source_target_pairs={{0,1},{1,0},{2,3},{3,2},{4,5},{5,4},{6,7},{7,6},{8,9},{9,8},{10,11... | collective-permute-start | bytes 393224 | tf_op jit(solution)/shard_map/ppermute | solution.py:229
  7.0 0.0 collective-permute-start.6
  7.0 4.5 %collective-permute-start.5 = (bf16[4,128,512]{2,1,0:T(8,128)(2,1)}, bf16[4,128,512]{2,1,0:T(8,128)(2,1)S(1)}, u32[]{:S(2)}, u32[]{:S(2)}) collective-permute-start(bf16[4,128,512]{2,1,0:T(8,128)(2,1)} %own_ref.1), channel_id=1, source_target_pairs={{8,16},{16,8},{9,17},{17,9},{10,18},{18,10},{11,19},{19,11},{12,20... | collective-permute-start | bytes 1572872 | tf_op jit(solution)/shard_map/ppermute | solution.py:229
  11.5 0.7 %fusion = bf16[4,64,256]{2,1,0:T(8,128)(2,1)} fusion(f32[4,64,256]{2,1,0:T(8,128)S(1)} %get-tuple-element.21, bf16[4,64,256]{2,1,0:T(8,128)(2,1)S(1)} %collective-permute-done), kind=kLoop, calls=%fused_computation.2 | loop fusion | flops 196608 | bytes 524288 | tf_op jit(solution)/shard_map/convert_element_type | solution.py:236
  12.2 1.2 %collective-permute-start.1 = (bf16[4,64,256]{2,1,0:T(8,128)(2,1)}, bf16[4,64,256]{2,1,0:T(8,128)(2,1)}, u32[]{:S(2)}, u32[]{:S(2)}) collective-permute-start(bf16[4,64,256]{2,1,0:T(8,128)(2,1)} %fusion), channel_id=1, source_target_pairs={{0,2},{1,3},{2,0},{3,1},{4,6},{5,7},{6,4},{7,5},{8,10},{9,11},{10,... | collective-permute-start | bytes 393224 | tf_op jit(solution)/shard_map/ppermute | solution.py:229
  13.4 1.2 %collective-permute-start.2 = (bf16[4,64,256]{2,1,0:T(8,128)(2,1)}, bf16[4,64,256]{2,1,0:T(8,128)(2,1)}, u32[]{:S(2)}, u32[]{:S(2)}) collective-permute-start(bf16[4,64,256]{2,1,0:T(8,128)(2,1)} %fusion), channel_id=1, source_target_pairs={{0,4},{1,5},{2,6},{3,7},{4,0},{5,1},{6,2},{7,3},{8,12},{9,13},{10,... | collective-permute-start | bytes 393224 | tf_op jit(solution)/shard_map/ppermute | solution.py:229
  14.6 0.2 collective-permute-start.3
  14.8 0.0 copy-start.7
  14.9 1.0 %copy-done.7 = bf16[4,128,512]{2,1,0:T(8,128)(2,1)S(1)} copy-done((bf16[4,128,512]{2,1,0:T(8,128)(2,1)S(1)}, bf16[4,128,512]{2,1,0:T(8,128)(2,1)}, u32[]{:S(2)}) %copy-start.7) | copy-done | bytes 524312
  15.9 1.0 %copy-done.9 = bf16[4,128,512]{2,1,0:T(8,128)(2,1)S(1)} copy-done((bf16[4,128,512]{2,1,0:T(8,128)(2,1)S(1)}, bf16[4,128,512]{2,1,0:T(8,128)(2,1)}, u32[]{:S(2)}) %copy-start.9) | copy-done | bytes 524312
  16.9 4.6 %own.1 = (bf16[4,128,512]{2,1,0:T(8,128)(2,1)S(1)}, f32[4,128,512]{2,1,0:T(8,128)S(1)}, f32[4,128,512]{2,1,0:T(8,128)S(1)}, f32[4,128,512]{2,1,0:T(8,128)S(1)}) custom-call(bf16[4,128,512]{2,1,0:T(8,128)(2,1)S(1)} %get-tuple-element.16.n_ref, bf16[512,1536]{1,0:T(8,128)(2,1)S(1)} %copy-done.1, bf16[4,128,512]{2,1,0:T(8,128)(2,1)S(1)} %copy-done.7, ...), custom_call_target="tpu_custom_call" | custom-call | flops 1000000000 | bytes 1048576 | tf_op jit(solution)/shard_map/own/pallas_call | solution.py:214
  21.6 0.0 collective-permute-done.1
  21.6 0.0 collective-permute-done.2
  21.6 1.2 %add_convert_fusion = (bf16[4,64,256]{2,1,0:T(8,128)(2,1)S(1)}, f32[4,64,256]{2,1,0:T(8,128)S(1)}) fusion(f32[4,64,256]{2,1,0:T(8,128)S(1)} %get-tuple-element.21, pred[]{:T(512)S(6)} %eq.6, bf16[4,64,256]{2,1,0:T(8,128)(2,1)} %collective-permute-done.3, pred[]{:T(512)S(6)} %lt.17, bf16[4,64,256]{2,1,0:T(8,128)(2,1)} %collective-permute-done.2, pred[]{:T(512)S(6)} %lt.16, ...), kind=kLoop, calls=%fused_computation.4 | loop fusion | flops 917504 | bytes 1179652 | tf_op jit(solution)/shard_map/convert_element_type | solution.py:241
  22.8 1.5 %collective-permute-start.4 = (bf16[4,64,256]{2,1,0:T(8,128)(2,1)S(1)}, bf16[4,64,256]{2,1,0:T(8,128)(2,1)S(1)}, u32[]{:S(2)}, u32[]{:S(2)}) collective-permute-start(bf16[4,64,256]{2,1,0:T(8,128)(2,1)S(1)} %get-tuple-element.27), channel_id=1, source_target_pairs={{0,1},{1,0},{2,3},{3,2},{4,5},{5,4},{6,7},{7,6},{8,9},{9,8},{10,11... | collective-permute-start | bytes 393224 | tf_op jit(solution)/shard_map/ppermute | solution.py:229
  24.2 0.0 collective-permute-done.6.x_ref
  24.2 3.9 %even.1 = (f32[4,128,512]{2,1,0:T(8,128)S(1)}, f32[4,128,512]{2,1,0:T(8,128)S(1)}) custom-call(bf16[4,128,512]{2,1,0:T(8,128)(2,1)S(1)} %collective-permute-done.6.x_ref, bf16[512,1536]{1,0:T(8,128)(2,1)S(1)} %copy-done.1, bf16[4,128,512]{2,1,0:T(8,128)(2,1)S(1)} %get-tuple-element.19.q_ref, f32[8]{0:T(128)S(1)} %copy-done.4, s32[4,8]{1,0:T(4,128)S(1)} %copy-done.3, ...), custom_call_target="tpu_custom_call" | custom-call | flops 1000000000 | bytes 1048576 | tf_op jit(solution)/shard_map/even/pallas_call | solution.py:214
  28.1 4.6 %odd.1.y_ref = f32[4,128,512]{2,1,0:T(8,128)S(1)} custom-call(bf16[4,128,512]{2,1,0:T(8,128)(2,1)S(1)} %collective-permute-done.5.x_ref, bf16[512,1536]{1,0:T(8,128)(2,1)S(1)} %copy-done.1, bf16[4,128,512]{2,1,0:T(8,128)(2,1)S(1)} %get-tuple-element.19.q_ref, f32[8]{0:T(128)S(1)} %copy-done.4, s32[4,8]{1,0:T(4,128)S(1)} %copy-done.3, s32[4]{0:T(128)S(1)} %copy-done.5, ...), custom_call_target="tpu_custom_call" | custom-call | flops 1000000000 | bytes 1048576 | tf_op jit(solution)/shard_map/odd/pallas_call | solution.py:214
  32.8 1.6 %closing.1 = bf16[4,128,512]{2,1,0:T(8,128)(2,1)} custom-call(bf16[4,128,512]{2,1,0:T(8,128)(2,1)S(1)} %get-tuple-element.19.q_ref, f32[4,128,512]{2,1,0:T(8,128)S(1)} %get-tuple-element.20.lin_ref, f32[4,64,256]{2,1,0:T(8,128)S(1)} %get-tuple-element.28.mine_ref, bf16[4,64,256]{2,1,0:T(8,128)(2,1)S(1)} %collective-permute-done.4.other_ref, ...), custom_call_target="tpu_custom_call" | custom-call | flops 1000000000 | bytes 1048576 | tf_op jit(solution)/shard_map/closing/pallas_call | solution.py:214
  (17 shorter events, 0.0 us)
Async XLA Ops:
  0.0 1.4 %copy-start = (bf16[512,1536]{1,0:T(8,128)(2,1)S(1)}, bf16[512,1536]{1,0:T(8,128)(2,1)}, u32[]{:S(2)}) copy-start(bf16[512,1536]{1,0:T(8,128)(2,1)} %w_ref.7) | copy-start | bytes 4718596
  1.4 13.4 %copy-start.1 = (bf16[512,1536]{1,0:T(8,128)(2,1)S(1)}, bf16[512,1536]{1,0:T(8,128)(2,1)}, u32[]{:S(2)}) copy-start(bf16[512,1536]{1,0:T(8,128)(2,1)} %w_ref.7) | copy-start | bytes 4718596
  1.4 13.4 %copy-start.3 = (s32[4,8]{1,0:T(4,128)S(1)}, s32[4,8]{1,0:T(4,128)}, u32[]{:S(2)}) copy-start(s32[4,8]{1,0:T(4,128)} %table_ref.5) | copy-start | bytes 388
  1.4 13.4 %copy-start.4 = (f32[8]{0:T(128)S(1)}, f32[8]{0:T(128)}, u32[]{:S(2)}) copy-start(f32[8]{0:T(128)} %sharp_ref.5) | copy-start | bytes 100
  1.4 13.4 %copy-start.5 = (s32[4]{0:T(128)S(1)}, s32[4]{0:T(128)}, u32[]{:S(2)}) copy-start(s32[4]{0:T(128)} %tally_ref.5) | copy-start | bytes 52
  4.7 0.8 %copy-start.6 = (bf16[4,128,512]{2,1,0:T(8,128)(2,1)}, bf16[4,128,512]{2,1,0:T(8,128)(2,1)S(1)}, u32[]{:S(2)}) copy-start(bf16[4,128,512]{2,1,0:T(8,128)(2,1)S(1)} %get-tuple-element.17.k_ref) | copy-start | bytes 1572868
  5.5 0.8 %copy-start.8 = (bf16[4,128,512]{2,1,0:T(8,128)(2,1)}, bf16[4,128,512]{2,1,0:T(8,128)(2,1)S(1)}, u32[]{:S(2)}) copy-start(bf16[4,128,512]{2,1,0:T(8,128)(2,1)S(1)} %get-tuple-element.18.v_ref) | copy-start | bytes 1572868
  6.3 5.2 %collective-permute-start = (bf16[4,64,256]{2,1,0:T(8,128)(2,1)S(1)}, bf16[4,64,256]{2,1,0:T(8,128)(2,1)S(1)}, u32[]{:S(2)}, u32[]{:S(2)}) collective-permute-start(bf16[4,64,256]{2,1,0:T(8,128)(2,1)S(1)} %get-tuple-element.22), channel_id=1, source_target_pairs={{0,1},{1,0},{2,3},{3,2},{4,5},{5,4},{6,7},{7,6},{8,9},{9,8},{10,11... | collective-permute-start | bytes 393224 | tf_op jit(solution)/shard_map/ppermute | solution.py:229
  7.0 17.3 %collective-permute-start.6 = (bf16[4,128,512]{2,1,0:T(8,128)(2,1)}, bf16[4,128,512]{2,1,0:T(8,128)(2,1)S(1)}, u32[]{:S(2)}, u32[]{:S(2)}) collective-permute-start(bf16[4,128,512]{2,1,0:T(8,128)(2,1)} %own_ref.1), channel_id=1, source_target_pairs={{0,8},{8,0},{16,24},{24,16},{1,9},{9,1},{17,25},{25,17},{2,10},{10... | collective-permute-start | bytes 1572872 | tf_op jit(solution)/shard_map/ppermute | solution.py:229
  7.0 21.1 %collective-permute-start.5 = (bf16[4,128,512]{2,1,0:T(8,128)(2,1)}, bf16[4,128,512]{2,1,0:T(8,128)(2,1)S(1)}, u32[]{:S(2)}, u32[]{:S(2)}) collective-permute-start(bf16[4,128,512]{2,1,0:T(8,128)(2,1)} %own_ref.1), channel_id=1, source_target_pairs={{8,16},{16,8},{9,17},{17,9},{10,18},{18,10},{11,19},{19,11},{12,20... | collective-permute-start | bytes 1572872 | tf_op jit(solution)/shard_map/ppermute | solution.py:229
  12.2 9.4 %collective-permute-start.1 = (bf16[4,64,256]{2,1,0:T(8,128)(2,1)}, bf16[4,64,256]{2,1,0:T(8,128)(2,1)}, u32[]{:S(2)}, u32[]{:S(2)}) collective-permute-start(bf16[4,64,256]{2,1,0:T(8,128)(2,1)} %fusion), channel_id=1, source_target_pairs={{0,2},{1,3},{2,0},{3,1},{4,6},{5,7},{6,4},{7,5},{8,10},{9,11},{10,... | collective-permute-start | bytes 393224 | tf_op jit(solution)/shard_map/ppermute | solution.py:229
  13.4 8.2 %collective-permute-start.2 = (bf16[4,64,256]{2,1,0:T(8,128)(2,1)}, bf16[4,64,256]{2,1,0:T(8,128)(2,1)}, u32[]{:S(2)}, u32[]{:S(2)}) collective-permute-start(bf16[4,64,256]{2,1,0:T(8,128)(2,1)} %fusion), channel_id=1, source_target_pairs={{0,4},{1,5},{2,6},{3,7},{4,0},{5,1},{6,2},{7,3},{8,12},{9,13},{10,... | collective-permute-start | bytes 393224 | tf_op jit(solution)/shard_map/ppermute | solution.py:229
  14.6 7.0 %collective-permute-start.3 = (bf16[4,64,256]{2,1,0:T(8,128)(2,1)}, bf16[4,64,256]{2,1,0:T(8,128)(2,1)}, u32[]{:S(2)}, u32[]{:S(2)}) collective-permute-start(bf16[4,64,256]{2,1,0:T(8,128)(2,1)} %fusion), channel_id=1, source_target_pairs={{0,6},{1,7},{2,4},{3,5},{4,2},{5,3},{6,0},{7,1},{8,14},{9,15},{10,... | collective-permute-start | bytes 393224 | tf_op jit(solution)/shard_map/ppermute | solution.py:229
  14.8 1.0 %copy-start.7 = (bf16[4,128,512]{2,1,0:T(8,128)(2,1)S(1)}, bf16[4,128,512]{2,1,0:T(8,128)(2,1)}, u32[]{:S(2)}) copy-start(bf16[4,128,512]{2,1,0:T(8,128)(2,1)} %copy-done.6) | copy-start | bytes 1572868
  15.9 1.0 %copy-start.9 = (bf16[4,128,512]{2,1,0:T(8,128)(2,1)S(1)}, bf16[4,128,512]{2,1,0:T(8,128)(2,1)}, u32[]{:S(2)}) copy-start(bf16[4,128,512]{2,1,0:T(8,128)(2,1)} %copy-done.8) | copy-start | bytes 1572868
  22.8 10.0 %collective-permute-start.4 = (bf16[4,64,256]{2,1,0:T(8,128)(2,1)S(1)}, bf16[4,64,256]{2,1,0:T(8,128)(2,1)S(1)}, u32[]{:S(2)}, u32[]{:S(2)}) collective-permute-start(bf16[4,64,256]{2,1,0:T(8,128)(2,1)S(1)} %get-tuple-element.27), channel_id=1, source_target_pairs={{0,1},{1,0},{2,3},{3,2},{4,5},{5,4},{6,7},{7,6},{8,9},{9,8},{10,11... | collective-permute-start | bytes 393224 | tf_op jit(solution)/shard_map/ppermute | solution.py:229
  24.2 3.9 %copy-start.2 = (bf16[1024,512]{1,0:T(8,128)(2,1)S(1)}, bf16[1024,512]{1,0:T(8,128)(2,1)}, u32[]{:S(2)}) copy-start(bf16[1024,512]{1,0:T(8,128)(2,1)} %close_ref.3) | copy-start | bytes 3145732

commit v2 on v1

v2 whole, which is shorter than its diff:
```python
import functools
import math

import jax
import jax.numpy as jnp
from jax import lax
from jax.experimental import pallas as pl
from jax.experimental.pallas import tpu as pltpu
from jax.sharding import PartitionSpec as P

NEAR = 4
HALF = 256
PAIR = 128
T = 32
F32 = jnp.float32
BF16 = jnp.bfloat16
VMEM = pltpu.VMEM
SMEM = pltpu.SMEM


def dot(a, b):
    return jnp.dot(a, b, preferred_element_type=F32)


def dot_nt(a, b):
    return lax.dot_general(a, b, (((1,), (1,)), ((), ())), preferred_element_type=F32)


def dot_tn(a, b):
    return lax.dot_general(a, b, (((0,), (0,)), ((), ())), preferred_element_type=F32)


def row_norm(x):
    xf = x.astype(F32)
    return (xf * lax.rsqrt(jnp.mean(xf * xf, axis=-1, keepdims=True) + 1e-06)).astype(BF16)


def head_ids(shape, axis, breadth):
    return lax.broadcasted_iota(jnp.int32, shape, axis) // breadth


def mean_matrix(breadth):
    same = head_ids((HALF, HALF), 0, breadth) == head_ids((HALF, HALF), 1, breadth)
    return jnp.where(same, 1.0 / breadth, 0.0).astype(BF16)


def head_norm(values, means, epsilon):
    square = (values * values).astype(BF16)
    return (values * lax.rsqrt(dot(square, means) + epsilon)).astype(BF16)


def own_head(values, j, breadth):
    ids = head_ids(values.shape, 1, breadth)
    return jnp.where(ids == j, values, jnp.zeros_like(values))


def multiplicity_mask(table_ref, tally_ref, base):
    groups, slots = table_ref.shape
    wide = groups * T
    ids = base + lax.broadcasted_iota(jnp.int32, (8, wide), 1) // T
    rows = []
    for g in range(groups):
        total = jnp.zeros((8, wide), F32)
        for j in range(slots):
            total += jnp.where((ids == table_ref[g, j]) & (j < tally_ref[g]), 1.0, 0.0)
        rows.append(jnp.broadcast_to(total[:1], (T, wide)))
    full = jnp.concatenate(rows, axis=0)
    t_row = lax.broadcasted_iota(jnp.int32, (wide, wide), 0) % T
    t_col = lax.broadcasted_iota(jnp.int32, (wide, wide), 1) % T
    return jnp.where(t_row == t_col, full, 0.0)


def pick(low, high, breadth):
    return jnp.where(head_ids(low.shape, 1, breadth) == 0, low, high)


def stack(values, breadth):
    return jnp.concatenate([own_head(values, j, breadth) for j in range(PAIR // breadth)], axis=0)


def cut(ref, c, u):
    groups = ref.shape[0]
    return ref[:, c * T : (c + 1) * T, u * PAIR : (u + 1) * PAIR].reshape(groups * T, PAIR)


def project(normed, w_ref, first, count):
    return [dot(normed, w_ref[:, first + h * HALF : first + (h + 1) * HALF]) for h in range(count)]


def keys_values(x_ref, w_ref, k_ref, v_ref, breadth):
    groups, patches, width = x_ref.shape
    halves = width // HALF
    means = mean_matrix(breadth)
    normed = row_norm(x_ref[...].reshape(groups * patches, width))
    keys = project(normed, w_ref, width, halves)
    values = project(normed, w_ref, 2 * width, halves)
    for h in range(halves):
        at = slice(h * HALF, (h + 1) * HALF)
        v_ref[:, :, at] = values[h].astype(BF16).reshape(groups, patches, HALF)
        k_ref[:, :, at] = head_norm(keys[h], means, 1e-06).reshape(groups, patches, HALF)
    return normed


def staggered(items, *stages):
    held = [{} for _ in stages]
    for i in range(len(items) + len(stages) - 1):
        for s, stage in enumerate(stages):
            if 0 <= i - s < len(items):
                before = (held[s - 1].pop(i - s),) if s else ()
                held[s][i - s] = stage(*before, *items[i - s])


def neighbours(breadth, q_ref, windows, sharp_ref, emit):
    groups, patches, width = q_ref.shape
    wide = groups * T
    heads = PAIR // breadth
    ones = stack(jnp.ones((wide, PAIR), BF16), breadth)
    scale = math.log2(math.e) / math.sqrt(breadth)
    lane = lax.broadcasted_iota(jnp.int32, (1, heads * wide), 1) // wide
    sharps = []
    for u in range(width // PAIR):
        row = jnp.full((1, heads * wide), sharp_ref[u * heads] * scale, F32)
        for j in range(1, heads):
            row = jnp.where(lane == j, sharp_ref[u * heads + j] * scale, row)
        sharps.append(row)
    masks = [jnp.concatenate([mask] * heads, axis=1) for _, _, mask in windows]
    sums = {}

    def score(u, c, n):
        return dot_nt(cut(q_ref, c, u), stack(cut(windows[n][0], c, u), breadth))

    def share(scores, u, c, n):
        return (jnp.exp2(scores * sharps[u]) * masks[n]).astype(BF16)

    def gather(shares, u, c, n):
        spread = jnp.concatenate([stack(cut(windows[n][1], c, u), breadth), ones], axis=1)
        part = dot(shares, spread)
        total = sums.pop((u, c)) + part if n else part
        if n + 1 < len(windows):
            sums[(u, c)] = total
        else:
            emit(c, u, total)

    items = [(u, c, n) for u in range(width // PAIR) for c in range(patches // T) for n in range(len(windows))]
    staggered(items, score, share, gather)


def states_kernel(breadth, x_ref, w_ref, n_ref, k_ref, v_ref, keep_ref, give_ref):
    groups, patches, width = x_ref.shape
    core = lax.axis_index("tm") % 2
    normed = keys_values(x_ref, w_ref, k_ref, v_ref, breadth)
    n_ref[...] = normed.reshape(n_ref.shape)
    for h in range(width // HALF):
        states = []
        for g in range(groups):
            pairs = []
            for u in range(h * HALF // PAIR, (h + 1) * HALF // PAIR):
                at = slice(u * PAIR, (u + 1) * PAIR)
                full = dot_tn(k_ref[g, :, at], v_ref[g, :, at])
                pairs.append(pick(full[:breadth], full[breadth:], breadth))
            states.append(jnp.concatenate(pairs, axis=1))

        @pl.when(core == h)
        def _():
            for g in range(groups):
                keep_ref[g] = states[g]

        @pl.when(core != h)
        def _():
            for g in range(groups):
                give_ref[g] = states[g].astype(BF16)


def own_kernel(breadth, n_ref, w_ref, k_ref, v_ref, q_ref, lin_ref):
    groups, patches, width = n_ref.shape
    halves = width // HALF
    means = mean_matrix(breadth)
    wide = (patches, patches * (PAIR // breadth))
    causal = lax.broadcasted_iota(jnp.int32, wide, 0) >= lax.broadcasted_iota(jnp.int32, wide, 1) % patches
    queries = project(n_ref[...].reshape(groups * patches, width), w_ref, 0, halves)
    for h in range(halves):
        q = head_norm(queries[h], means, 1e-06)
        q_ref[:, :, h * HALF : (h + 1) * HALF] = q.reshape(groups, patches, HALF)

    def score(h, g):
        scores = []
        for u in range(h * HALF // PAIR, (h + 1) * HALF // PAIR):
            at = slice(u * PAIR, (u + 1) * PAIR)
            scores.append(dot_nt(q_ref[g, :, at], stack(k_ref[g, :, at], breadth)))
        return scores

    def share(scores, h, g):
        return jnp.concatenate([jnp.where(causal, s, 0.0).astype(BF16) for s in scores], axis=1)

    def gather(shares, h, g):
        at = slice(h * HALF, (h + 1) * HALF)
        v = v_ref[g, :, at]
        spread = jnp.concatenate([own_head(v, j, breadth) for j in range(HALF // breadth)], axis=0)
        lin_ref[g, :, at] = dot(shares, spread)

    staggered([(h, g) for h in range(halves) for g in range(groups)], score, share, gather)


def even_kernel(breadth, x_ref, w_ref, k_ref, v_ref, q_ref, sharp_ref, table_ref, tally_ref, keep_ref, acc_ref, kept_ref, ke_ref, ve_ref):
    groups, patches, width = x_ref.shape
    station = lax.axis_index("stations")
    keys_values(x_ref, w_ref, ke_ref, ve_ref, breadth)
    windows = [
        (k_ref, v_ref, multiplicity_mask(table_ref, tally_ref, station * groups)),
        (ke_ref, ve_ref, multiplicity_mask(table_ref, tally_ref, (station ^ 1) * groups)),
    ]

    def emit(c, u, total):
        acc_ref[:, c * T : (c + 1) * T, u * 2 * PAIR : (u + 1) * 2 * PAIR] = total.reshape(groups, T, 2 * PAIR)

    neighbours(breadth, q_ref, windows, sharp_ref, emit)


def odd_kernel(breadth, x_ref, w_ref, q_ref, sharp_ref, table_ref, tally_ref, acc_ref, own_ref, close_ref, y_ref, k_ref, v_ref, gathered_ref):
    groups, patches, width = x_ref.shape
    station = lax.axis_index("stations")
    base = (station + 2 * (station % 2) - 1) * groups
    keys_values(x_ref, w_ref, k_ref, v_ref, breadth)
    windows = [(k_ref, v_ref, multiplicity_mask(table_ref, tally_ref, base))]

    def emit(c, u, total):
        span = slice(c * T, (c + 1) * T)
        total = total.reshape(groups, T, 2 * PAIR) + acc_ref[:, span, u * 2 * PAIR : (u + 1) * 2 * PAIR]
        gathered_ref[:, span, u * PAIR : (u + 1) * PAIR] = (total[:, :, :PAIR] / total[:, :, PAIR:]).astype(BF16)

    neighbours(breadth, q_ref, windows, sharp_ref, emit)
    mixed = dot(gathered_ref[...].reshape(groups * patches, width), close_ref[width:, :])
    y_ref[...] = own_ref[...].astype(F32) + mixed.reshape(groups, patches, width)


def closing_kernel(breadth, q_ref, lin_ref, mine_ref, other_ref, close_ref, y_ref, out_ref, normed_ref):
    groups, patches, width = q_ref.shape
    heads = HALF // breadth
    halves = width // HALF
    core = lax.axis_index("tm") % 2
    means = mean_matrix(breadth)
    same = head_ids((HALF, HALF), 0, breadth) == head_ids((HALF, HALF), 1, breadth)
    totals = []
    for h in range(halves):
        at = slice(h * HALF, (h + 1) * HALF)
        for g in range(groups):
            state = jnp.where(core == h, mine_ref[g], other_ref[g].astype(F32)).astype(BF16)
            block = jnp.where(same, jnp.concatenate([state] * heads, axis=0), jnp.zeros((), BF16))
            totals.append(lin_ref[g, :, at] + dot(q_ref[g, :, at], block))
    for h in range(halves):
        total = jnp.concatenate(totals[h * groups : (h + 1) * groups], axis=0)
        normed_ref[:, h * HALF : (h + 1) * HALF] = head_norm(total, means, 1e-05)
    mixed = dot(normed_ref[...], close_ref[:width, :])
    out_ref[...] = (y_ref[...] + mixed.reshape(groups, patches, width)).astype(BF16)


def call(kernel, breadth, outs, args, scratch=(), flops=10**9, name=None, through=None):
    def place(a):
        return pl.BlockSpec(memory_space=SMEM if a.size <= 64 else VMEM)

    in_specs, out_specs = [place(a) for a in args], [pl.BlockSpec(memory_space=VMEM) for _ in outs]
    aliases = {}
    if through is not None:
        in_specs[through[0]] = out_specs[through[1]] = pl.BlockSpec(memory_space=pl.ANY)
        aliases = {through[0]: through[1]}
    return pl.pallas_call(
        functools.partial(kernel, breadth),
        out_shape=[jax.ShapeDtypeStruct(s, d) for s, d in outs],
        in_specs=in_specs,
        out_specs=out_specs,
        scratch_shapes=[pltpu.VMEM(s, d) for s, d in scratch],
        input_output_aliases=aliases,
        compiler_params=pltpu.CompilerParams(vmem_limit_bytes=10 * 2**20),
        cost_estimate=pl.CostEstimate(flops=flops, bytes_accessed=2**20, transcendentals=0),
        name=name,
    )(*args)


def swap_with(value, axis, partner):
    size = lax.axis_size(axis)
    pairs = [(i, partner(i)) for i in range(size) if 0 <= partner(i) < size]
    return lax.ppermute(value, axis, pairs)


def per_device(x, w, close, sharp, table, tally):
    groups, patches, width = x.shape
    breadth = width // sharp.shape[0]
    core, chip = lax.axis_index("tm") % 2, lax.axis_index("tm") // 2
    chips = lax.axis_size("tm") // 2
    block = x.shape
    part = (groups, breadth, HALF)
    x_odd = swap_with(x, "stations", lambda i: i + 2 * (i % 2) - 1)
    x_even = swap_with(x, "stations", lambda i: i ^ 1)
    normed, k, v, keep, give = call(
        states_kernel, breadth, [(block, BF16)] * 3 + [(part, F32), (part, BF16)], (x, w), name="states"
    )
    got = swap_with(give, "tm", lambda i: i ^ 1)
    total = (keep + got.astype(F32)).astype(BF16)
    pieces = [swap_with(total, "tm", lambda i: i ^ (2 * m)) for m in range(1, chips)]
    q, lin = call(own_kernel, breadth, [(block, BF16), (block, F32)], (normed, w, k, v), name="own")
    acc, keep = call(
        even_kernel,
        breadth,
        [((groups, patches, 2 * width), F32), (part, F32)],
        (x_even, w, k, v, q, sharp, table, tally, keep),
        [(block, BF16)] * 2,
        name="even",
        through=(8, 1),
    )
    before = jnp.zeros_like(keep)
    for m, piece in enumerate(pieces, 1):
        before += jnp.where((chip ^ m) < chip, piece.astype(F32), 0.0)
    send = (before + jnp.where(core == 0, keep, 0.0)).astype(BF16)
    mine = before + jnp.where(core == 0, 0.0, got.astype(F32))
    other = swap_with(send, "tm", lambda i: i ^ 1)
    (y,) = call(
        odd_kernel,
        breadth,
        [(block, F32)],
        (x_odd, w, q, sharp, table, tally, acc, x, close),
        [(block, BF16)] * 3,
        name="odd",
    )
    (out,) = call(
        closing_kernel,
        breadth,
        [(block, BF16)],
        (q, lin, mine, other, close, y),
        [((groups * patches, width), BF16)],
        name="closing",
    )
    return out


def solution(mesh):
    return jax.shard_map(
        per_device,
        mesh=mesh,
        in_specs=(P("stations", "tm", None), P(), P(), P(), P("stations", None), P("stations")),
        out_specs=P("stations", "tm", None),
        check_vma=False,
    )
```

time: 34.7 us -> 27.5 us (0.79)
  Pallas kernels: 18.1 us -> 12.1 us
  local copies, waits for them, and re-layouts: 5.08 us -> 3.52 us
    pallas_call x5, Pallas kernels: 18.1 us -> 12.1 us  [call(): pl.pallas_call(functools.partial(kernel, breadth), out_shape=[jax.ShapeDt...]
    unnamed x20, local copies, waits for them, and re-layouts: 5.08 us -> 3.52 us
  transfers between devices with their start and end apart: 7 -> 7, of which waited for: 0 -> 0; matrix products, arithmetic and copies ran while one was open for 5% -> 7% of each run, Pallas kernels for 38% -> 39%
where the time goes in v2:
time: 27.5 us; the launch traced here: 27.1 us
  Pallas kernels  12.1 us (44%)
  starting transfers between devices  9.37 us (34%)
  local copies, waits for them, and re-layouts  3.52 us (13%)
  other arithmetic  1.86 us (7%)
    pallas_call x5, Pallas kernels, call(): pl.pallas_call(functools.partial(kernel, breadth), out_shape=[jax.ShapeDt...  12.1 us
    ppermute x7, starting transfers between devices, swap_with(): return lax.ppermute(value, axis, pairs)  9.37 us
    unnamed x20, local copies, waits for them, and re-layouts  3.52 us
    convert_element_type x1, other arithmetic, per_device(): send = (before + jnp.where(core == 0, keep, 0.0)).astype(BF16)  1.16 us
    convert_element_type x1, other arithmetic, per_device(): total = (keep + got.astype(F32)).astype(BF16)  0.7 us
  transfers between devices with their start and end apart: 7, of which 0 were waited for; matrix products, arithmetic and copies ran while one was open for 7% of the time, Pallas kernels for 39%

profile of v2, /device:TPU:9, one launch (start us, length us, event | category | flops | bytes accessed | tf_op | source)
XLA Modules:
  0.0 27.1 jit_solution(10314152180921021213)
XLA Ops:
  0.0 1.4 %copy-done = bf16[512,1536]{1,0:T(8,128)(2,1)S(1)} copy-done((bf16[512,1536]{1,0:T(8,128)(2,1)S(1)}, bf16[512,1536]{1,0:T(8,128)(2,1)}, u32[]{:S(2)}) %copy-start) | copy-done | bytes 1572888
  1.4 2.6 %states.1 = (bf16[4,128,512]{2,1,0:T(8,128)(2,1)S(1)}, bf16[4,128,512]{2,1,0:T(8,128)(2,1)S(1)}, bf16[4,128,512]{2,1,0:T(8,128)(2,1)S(1)}, f32[4,64,256]{2,1,0:T(8,128)S(1)}, bf16[4,64,256]{2,1,0:T(8,128)(2,1)S(1)}) custom-call(bf16[4,128,512]{2,1,0:T(8,128)(2,1)} %own_ref.1, bf16[512,1536]{1,0:T(8,128)(2,1)S(1)} %copy-done), custom_call_target="tpu_custom_call" | custom-call | flops 1000000000 | bytes 1048576 | tf_op jit(solution)/shard_map/states/pallas_call | solution.py:266
  4.0 0.0 copy-start.3
  4.0 0.7 %collective-permute-start = (bf16[4,64,256]{2,1,0:T(8,128)(2,1)S(1)}, bf16[4,64,256]{2,1,0:T(8,128)(2,1)S(1)}, u32[]{:S(2)}, u32[]{:S(2)}) collective-permute-start(bf16[4,64,256]{2,1,0:T(8,128)(2,1)S(1)} %get-tuple-element.20), channel_id=1, source_target_pairs={{0,1},{1,0},{2,3},{3,2},{4,5},{5,4},{6,7},{7,6},{8,9},{9,8},{10,11... | collective-permute-start | bytes 393224 | tf_op jit(solution)/shard_map/ppermute | solution.py:282
  4.8 4.8 %collective-permute-start.6 = (bf16[4,128,512]{2,1,0:T(8,128)(2,1)}, bf16[4,128,512]{2,1,0:T(8,128)(2,1)}, u32[]{:S(2)}, u32[]{:S(2)}) collective-permute-start(bf16[4,128,512]{2,1,0:T(8,128)(2,1)} %own_ref.1), channel_id=1, source_target_pairs={{8,16},{16,8},{9,17},{17,9},{10,18},{18,10},{11,19},{19,11},{12,20... | collective-permute-start | bytes 1572872 | tf_op jit(solution)/shard_map/ppermute | solution.py:282
  9.6 0.0 collective-permute-done
  9.6 0.0 copy-start.7
  9.6 0.0 copy-start.8
  9.6 0.0 copy-start.9
  9.6 0.7 %fusion = bf16[4,64,256]{2,1,0:T(8,128)(2,1)} fusion(f32[4,64,256]{2,1,0:T(8,128)S(1)} %get-tuple-element.19.keep_ref, bf16[4,64,256]{2,1,0:T(8,128)(2,1)S(1)} %collective-permute-done), kind=kLoop, calls=%fused_computation.2 | loop fusion | flops 196608 | bytes 524288 | tf_op jit(solution)/shard_map/convert_element_type | solution.py:298
  10.3 2.2 %collective-permute-start.3 = (bf16[4,64,256]{2,1,0:T(8,128)(2,1)}, bf16[4,64,256]{2,1,0:T(8,128)(2,1)}, u32[]{:S(2)}, u32[]{:S(2)}) collective-permute-start(bf16[4,64,256]{2,1,0:T(8,128)(2,1)} %fusion), channel_id=1, source_target_pairs={{0,6},{1,7},{2,4},{3,5},{4,2},{5,3},{6,0},{7,1},{8,14},{9,15},{10,... | collective-permute-start | bytes 393224 | tf_op jit(solution)/shard_map/ppermute | solution.py:282
  12.5 0.2 collective-permute-start.2
  12.7 0.3 collective-permute-start.1
  13.0 1.2 %own.1 = (bf16[4,128,512]{2,1,0:T(8,128)(2,1)S(1)}, f32[4,128,512]{2,1,0:T(8,128)S(1)}) custom-call(bf16[4,128,512]{2,1,0:T(8,128)(2,1)S(1)} %get-tuple-element.14.n_ref, bf16[512,1536]{1,0:T(8,128)(2,1)S(1)} %copy-done.1, bf16[4,128,512]{2,1,0:T(8,128)(2,1)S(1)} %get-tuple-element.15.k_ref, bf16[4,128,512]{2,1,0:T(8,128)(2,1)S(1)} %get-tuple-element.16.v_ref), custom_call_target="tpu_custom_call" | custom-call | flops 1000000000 | bytes 1048576 | tf_op jit(solution)/shard_map/own/pallas_call | solution.py:266
  14.3 0.0 copy-start.4
  14.3 1.0 %copy-done.4 = bf16[4,128,512]{2,1,0:T(8,128)(2,1)S(1)} copy-done((bf16[4,128,512]{2,1,0:T(8,128)(2,1)S(1)}, bf16[4,128,512]{2,1,0:T(8,128)(2,1)}, u32[]{:S(2)}) %copy-start.4) | copy-done | bytes 524312
  15.3 1.0 %copy-done.6 = bf16[4,128,512]{2,1,0:T(8,128)(2,1)S(1)} copy-done((bf16[4,128,512]{2,1,0:T(8,128)(2,1)S(1)}, bf16[4,128,512]{2,1,0:T(8,128)(2,1)}, u32[]{:S(2)}) %copy-start.6) | copy-done | bytes 524312
  16.4 3.4 %even.1 = (f32[4,128,1024]{2,1,0:T(8,128)S(1)}, f32[4,64,256]{2,1,0:T(8,128)S(1)}) custom-call(bf16[4,128,512]{2,1,0:T(8,128)(2,1)} %collective-permute-done.4.x_ref, bf16[512,1536]{1,0:T(8,128)(2,1)S(1)} %copy-done.1, bf16[4,128,512]{2,1,0:T(8,128)(2,1)S(1)} %copy-done.4, bf16[4,128,512]{2,1,0:T(8,128)(2,1)S(1)} %copy-done.6, ...), custom_call_target="tpu_custom_call", output_to_operand_aliasing={{1}: (8, {})} | custom-call | flops 1000000000 | bytes 1048576 | tf_op jit(solution)/shard_map/even/pallas_call | solution.py:266
  19.8 0.0 collective-permute-done.2
  19.8 0.0 collective-permute-done.1
  19.8 1.2 %add_convert_fusion = (bf16[4,64,256]{2,1,0:T(8,128)(2,1)S(1)}, f32[4,64,256]{2,1,0:T(8,128)S(1)}) fusion(f32[4,64,256]{2,1,0:T(8,128)S(1)} %get-tuple-element.21, pred[]{:T(512)S(6)} %eq.6, bf16[4,64,256]{2,1,0:T(8,128)(2,1)} %collective-permute-done.3, pred[]{:T(512)S(6)} %lt.17, bf16[4,64,256]{2,1,0:T(8,128)(2,1)} %collective-permute-done.2, pred[]{:T(512)S(6)} %lt.16, ...), kind=kLoop, calls=%fused_computation.4 | loop fusion | flops 917504 | bytes 1179652 | tf_op jit(solution)/shard_map/convert_element_type | solution.py:313
  21.0 1.2 %collective-permute-start.5 = (bf16[4,64,256]{2,1,0:T(8,128)(2,1)S(1)}, bf16[4,64,256]{2,1,0:T(8,128)(2,1)S(1)}, u32[]{:S(2)}, u32[]{:S(2)}) collective-permute-start(bf16[4,64,256]{2,1,0:T(8,128)(2,1)S(1)} %get-tuple-element.23), channel_id=1, source_target_pairs={{0,1},{1,0},{2,3},{3,2},{4,5},{5,4},{6,7},{7,6},{8,9},{9,8},{10,11... | collective-permute-start | bytes 393224 | tf_op jit(solution)/shard_map/ppermute | solution.py:282
  22.2 3.3 %odd.1.y_ref = f32[4,128,512]{2,1,0:T(8,128)S(1)} custom-call(bf16[4,128,512]{2,1,0:T(8,128)(2,1)} %collective-permute-done.6.x_ref, bf16[512,1536]{1,0:T(8,128)(2,1)S(1)} %copy-done.1, bf16[4,128,512]{2,1,0:T(8,128)(2,1)S(1)} %get-tuple-element.17.q_ref, f32[8]{0:T(128)S(1)} %copy-done.8, s32[4,8]{1,0:T(4,128)S(1)} %copy-done.7, s32[4]{0:T(128)S(1)} %copy-done.9, ...), custom_call_target="tpu_custom_call" | custom-call | flops 1000000000 | bytes 1048576 | tf_op jit(solution)/shard_map/odd/pallas_call | solution.py:266
  25.5 1.6 %closing.1 = bf16[4,128,512]{2,1,0:T(8,128)(2,1)} custom-call(bf16[4,128,512]{2,1,0:T(8,128)(2,1)S(1)} %get-tuple-element.17.q_ref, f32[4,128,512]{2,1,0:T(8,128)S(1)} %get-tuple-element.18.lin_ref, f32[4,64,256]{2,1,0:T(8,128)S(1)} %get-tuple-element.24.mine_ref, bf16[4,64,256]{2,1,0:T(8,128)(2,1)S(1)} %collective-permute-done.5.other_ref, ...), custom_call_target="tpu_custom_call" | custom-call | flops 1000000000 | bytes 1048576 | tf_op jit(solution)/shard_map/closing/pallas_call | solution.py:266
  (17 shorter events, 0.0 us)
Async XLA Ops:
  0.0 14.2 %collective-permute-start.4 = (bf16[4,128,512]{2,1,0:T(8,128)(2,1)}, bf16[4,128,512]{2,1,0:T(8,128)(2,1)}, u32[]{:S(2)}, u32[]{:S(2)}) collective-permute-start(bf16[4,128,512]{2,1,0:T(8,128)(2,1)} %own_ref.1), channel_id=1, source_target_pairs={{0,8},{8,0},{16,24},{24,16},{1,9},{9,1},{17,25},{25,17},{2,10},{10... | collective-permute-start | bytes 1572872 | tf_op jit(solution)/shard_map/ppermute | solution.py:282
  0.0 1.4 %copy-start = (bf16[512,1536]{1,0:T(8,128)(2,1)S(1)}, bf16[512,1536]{1,0:T(8,128)(2,1)}, u32[]{:S(2)}) copy-start(bf16[512,1536]{1,0:T(8,128)(2,1)} %w_ref.7) | copy-start | bytes 4718596
  1.4 11.5 %copy-start.1 = (bf16[512,1536]{1,0:T(8,128)(2,1)S(1)}, bf16[512,1536]{1,0:T(8,128)(2,1)}, u32[]{:S(2)}) copy-start(bf16[512,1536]{1,0:T(8,128)(2,1)} %w_ref.7) | copy-start | bytes 4718596
  4.0 10.2 %copy-start.3 = (bf16[4,128,512]{2,1,0:T(8,128)(2,1)}, bf16[4,128,512]{2,1,0:T(8,128)(2,1)S(1)}, u32[]{:S(2)}) copy-start(bf16[4,128,512]{2,1,0:T(8,128)(2,1)S(1)} %get-tuple-element.15.k_ref) | copy-start | bytes 1572868
  4.0 10.2 %copy-start.5 = (bf16[4,128,512]{2,1,0:T(8,128)(2,1)}, bf16[4,128,512]{2,1,0:T(8,128)(2,1)S(1)}, u32[]{:S(2)}) copy-start(bf16[4,128,512]{2,1,0:T(8,128)(2,1)S(1)} %get-tuple-element.16.v_ref) | copy-start | bytes 1572868
  4.0 5.5 %collective-permute-start = (bf16[4,64,256]{2,1,0:T(8,128)(2,1)S(1)}, bf16[4,64,256]{2,1,0:T(8,128)(2,1)S(1)}, u32[]{:S(2)}, u32[]{:S(2)}) collective-permute-start(bf16[4,64,256]{2,1,0:T(8,128)(2,1)S(1)} %get-tuple-element.20), channel_id=1, source_target_pairs={{0,1},{1,0},{2,3},{3,2},{4,5},{5,4},{6,7},{7,6},{8,9},{9,8},{10,11... | collective-permute-start | bytes 393224 | tf_op jit(solution)/shard_map/ppermute | solution.py:282
  4.8 17.4 %collective-permute-start.6 = (bf16[4,128,512]{2,1,0:T(8,128)(2,1)}, bf16[4,128,512]{2,1,0:T(8,128)(2,1)}, u32[]{:S(2)}, u32[]{:S(2)}) collective-permute-start(bf16[4,128,512]{2,1,0:T(8,128)(2,1)} %own_ref.1), channel_id=1, source_target_pairs={{8,16},{16,8},{9,17},{17,9},{10,18},{18,10},{11,19},{19,11},{12,20... | collective-permute-start | bytes 1572872 | tf_op jit(solution)/shard_map/ppermute | solution.py:282
  9.6 4.7 %copy-start.7 = (s32[4,8]{1,0:T(4,128)S(1)}, s32[4,8]{1,0:T(4,128)}, u32[]{:S(2)}) copy-start(s32[4,8]{1,0:T(4,128)} %table_ref.3) | copy-start | bytes 388
  9.6 4.7 %copy-start.8 = (f32[8]{0:T(128)S(1)}, f32[8]{0:T(128)}, u32[]{:S(2)}) copy-start(f32[8]{0:T(128)} %sharp_ref.3) | copy-start | bytes 100
  9.6 4.7 %copy-start.9 = (s32[4]{0:T(128)S(1)}, s32[4]{0:T(128)}, u32[]{:S(2)}) copy-start(s32[4]{0:T(128)} %tally_ref.3) | copy-start | bytes 52
  10.3 9.5 %collective-permute-start.3 = (bf16[4,64,256]{2,1,0:T(8,128)(2,1)}, bf16[4,64,256]{2,1,0:T(8,128)(2,1)}, u32[]{:S(2)}, u32[]{:S(2)}) collective-permute-start(bf16[4,64,256]{2,1,0:T(8,128)(2,1)} %fusion), channel_id=1, source_target_pairs={{0,6},{1,7},{2,4},{3,5},{4,2},{5,3},{6,0},{7,1},{8,14},{9,15},{10,... | collective-permute-start | bytes 393224 | tf_op jit(solution)/shard_map/ppermute | solution.py:282
  12.5 7.3 %collective-permute-start.2 = (bf16[4,64,256]{2,1,0:T(8,128)(2,1)}, bf16[4,64,256]{2,1,0:T(8,128)(2,1)}, u32[]{:S(2)}, u32[]{:S(2)}) collective-permute-start(bf16[4,64,256]{2,1,0:T(8,128)(2,1)} %fusion), channel_id=1, source_target_pairs={{0,4},{1,5},{2,6},{3,7},{4,0},{5,1},{6,2},{7,3},{8,12},{9,13},{10,... | collective-permute-start | bytes 393224 | tf_op jit(solution)/shard_map/ppermute | solution.py:282
  12.7 7.1 %collective-permute-start.1 = (bf16[4,64,256]{2,1,0:T(8,128)(2,1)}, bf16[4,64,256]{2,1,0:T(8,128)(2,1)}, u32[]{:S(2)}, u32[]{:S(2)}) collective-permute-start(bf16[4,64,256]{2,1,0:T(8,128)(2,1)} %fusion), channel_id=1, source_target_pairs={{0,2},{1,3},{2,0},{3,1},{4,6},{5,7},{6,4},{7,5},{8,10},{9,11},{10,... | collective-permute-start | bytes 393224 | tf_op jit(solution)/shard_map/ppermute | solution.py:282
  14.3 1.0 %copy-start.4 = (bf16[4,128,512]{2,1,0:T(8,128)(2,1)S(1)}, bf16[4,128,512]{2,1,0:T(8,128)(2,1)}, u32[]{:S(2)}) copy-start(bf16[4,128,512]{2,1,0:T(8,128)(2,1)} %copy-done.3) | copy-start | bytes 1572868
  15.3 1.0 %copy-start.6 = (bf16[4,128,512]{2,1,0:T(8,128)(2,1)S(1)}, bf16[4,128,512]{2,1,0:T(8,128)(2,1)}, u32[]{:S(2)}) copy-start(bf16[4,128,512]{2,1,0:T(8,128)(2,1)} %copy-done.5) | copy-start | bytes 1572868
  16.4 5.8 %copy-start.2 = (bf16[1024,512]{1,0:T(8,128)(2,1)S(1)}, bf16[1024,512]{1,0:T(8,128)(2,1)}, u32[]{:S(2)}) copy-start(bf16[1024,512]{1,0:T(8,128)(2,1)} %close_ref.3) | copy-start | bytes 3145732
  21.0 4.5 %collective-permute-start.5 = (bf16[4,64,256]{2,1,0:T(8,128)(2,1)S(1)}, bf16[4,64,256]{2,1,0:T(8,128)(2,1)S(1)}, u32[]{:S(2)}, u32[]{:S(2)}) collective-permute-start(bf16[4,64,256]{2,1,0:T(8,128)(2,1)S(1)} %get-tuple-element.23), channel_id=1, source_target_pairs={{0,1},{1,0},{2,3},{3,2},{4,5},{5,4},{6,7},{7,6},{8,9},{9,8},{10,11... | collective-permute-start | bytes 393224 | tf_op jit(solution)/shard_map/ppermute | solution.py:282

commit v3 on v2

--- a/solution.py
+++ b/solution.py
@@ -98,7 +98,6 @@
         at = slice(h * HALF, (h + 1) * HALF)
         v_ref[:, :, at] = values[h].astype(BF16).reshape(groups, patches, HALF)
         k_ref[:, :, at] = head_norm(keys[h], means, 1e-06).reshape(groups, patches, HALF)
-    return normed
 
 
 def staggered(items, *stages):
@@ -123,14 +122,13 @@
         for j in range(1, heads):
             row = jnp.where(lane == j, sharp_ref[u * heads + j] * scale, row)
         sharps.append(row)
-    masks = [jnp.concatenate([mask] * heads, axis=1) for _, _, mask in windows]
     sums = {}
 
     def score(u, c, n):
         return dot_nt(cut(q_ref, c, u), stack(cut(windows[n][0], c, u), breadth))
 
     def share(scores, u, c, n):
-        return (jnp.exp2(scores * sharps[u]) * masks[n]).astype(BF16)
+        return (jnp.exp2(scores * sharps[u]) * windows[n][2][...]).astype(BF16)
 
     def gather(shares, u, c, n):
         spread = jnp.concatenate([stack(cut(windows[n][1], c, u), breadth), ones], axis=1)
@@ -145,11 +143,19 @@
     staggered(items, score, share, gather)
 
 
-def states_kernel(breadth, x_ref, w_ref, n_ref, k_ref, v_ref, keep_ref, give_ref):
+def masks_kernel(breadth, table_ref, tally_ref, mask_ref):
+    groups = table_ref.shape[0]
+    station = lax.axis_index("stations")
+    around = (station, station ^ 1, station + 2 * (station % 2) - 1)
+    for n, place in enumerate(around):
+        mask = multiplicity_mask(table_ref, tally_ref, place * groups)
+        mask_ref[n] = jnp.concatenate([mask] * (PAIR // breadth), axis=1)
+
+
+def states_kernel(breadth, x_ref, w_ref, mask_ref, k_ref, v_ref, keep_ref, give_ref):
     groups, patches, width = x_ref.shape
     core = lax.axis_index("tm") % 2
-    normed = keys_values(x_ref, w_ref, k_ref, v_ref, breadth)
-    n_ref[...] = normed.reshape(n_ref.shape)
+    keys_values(x_ref, w_ref, k_ref, v_ref, breadth)
     for h in range(width // HALF):
         states = []
         for g in range(groups):
@@ -171,13 +177,13 @@
                 give_ref[g] = states[g].astype(BF16)
 
 
-def own_kernel(breadth, n_ref, w_ref, k_ref, v_ref, q_ref, lin_ref):
-    groups, patches, width = n_ref.shape
+def own_kernel(breadth, x_ref, w_ref, k_ref, v_ref, q_ref, lin_ref):
+    groups, patches, width = x_ref.shape
     halves = width // HALF
     means = mean_matrix(breadth)
     wide = (patches, patches * (PAIR // breadth))
     causal = lax.broadcasted_iota(jnp.int32, wide, 0) >= lax.broadcasted_iota(jnp.int32, wide, 1) % patches
-    queries = project(n_ref[...].reshape(groups * patches, width), w_ref, 0, halves)
+    queries = project(row_norm(x_ref[...].reshape(groups * patches, width)), w_ref, 0, halves)
     for h in range(halves):
         q = head_norm(queries[h], means, 1e-06)
         q_ref[:, :, h * HALF : (h + 1) * HALF] = q.reshape(groups, patches, HALF)
@@ -201,13 +207,12 @@
     staggered([(h, g) for h in range(halves) for g in range(groups)], score, share, gather)
 
 
-def even_kernel(breadth, x_ref, w_ref, k_ref, v_ref, q_ref, sharp_ref, table_ref, tally_ref, keep_ref, acc_ref, kept_ref, ke_ref, ve_ref):
-    groups, patches, width = x_ref.shape
-    station = lax.axis_index("stations")
+def even_kernel(breadth, x_ref, w_ref, k_ref, v_ref, q_ref, sharp_ref, mask_ref, keep_ref, acc_ref, kept_ref, ke_ref, ve_ref):
+    groups, patches, width = x_ref.shape
     keys_values(x_ref, w_ref, ke_ref, ve_ref, breadth)
     windows = [
-        (k_ref, v_ref, multiplicity_mask(table_ref, tally_ref, station * groups)),
-        (ke_ref, ve_ref, multiplicity_mask(table_ref, tally_ref, (station ^ 1) * groups)),
+        (k_ref, v_ref, mask_ref.at[0]),
+        (ke_ref, ve_ref, mask_ref.at[1]),
     ]
 
     def emit(c, u, total):
@@ -216,12 +221,10 @@
     neighbours(breadth, q_ref, windows, sharp_ref, emit)
 
 
-def odd_kernel(breadth, x_ref, w_ref, q_ref, sharp_ref, table_ref, tally_ref, acc_ref, own_ref, close_ref, y_ref, k_ref, v_ref, gathered_ref):
-    groups, patches, width = x_ref.shape
-    station = lax.axis_index("stations")
-    base = (station + 2 * (station % 2) - 1) * groups
+def odd_kernel(breadth, x_ref, w_ref, q_ref, sharp_ref, mask_ref, acc_ref, own_ref, close_ref, y_ref, k_ref, v_ref, gathered_ref):
+    groups, patches, width = x_ref.shape
     keys_values(x_ref, w_ref, k_ref, v_ref, breadth)
-    windows = [(k_ref, v_ref, multiplicity_mask(table_ref, tally_ref, base))]
+    windows = [(k_ref, v_ref, mask_ref.at[2])]
 
     def emit(c, u, total):
         span = slice(c * T, (c + 1) * T)
@@ -244,7 +247,7 @@
     for h in range(halves):
         at = slice(h * HALF, (h + 1) * HALF)
         for g in range(groups):
-            state = jnp.where(core == h, mine_ref[g], other_ref[g].astype(F32)).astype(BF16)
+            state = jnp.where(core == h, mine_ref[g], other_ref[g])
             block = jnp.where(same, jnp.concatenate([state] * heads, axis=0), jnp.zeros((), BF16))
             totals.append(lin_ref[g, :, at] + dot(q_ref[g, :, at], block))
     for h in range(halves):
@@ -254,22 +257,36 @@
     out_ref[...] = (y_ref[...] + mixed.reshape(groups, patches, width)).astype(BF16)
 
 
-def call(kernel, breadth, outs, args, scratch=(), flops=10**9, name=None, through=None):
+def combine_kernel(breadth, keep_ref, got_ref, total_ref):
+    total_ref[...] = (keep_ref[...] + got_ref[...].astype(F32)).astype(BF16)
+
+
+def carry_kernel(breadth, keep_ref, got_ref, *refs):
+    *pieces, send_ref, mine_ref = refs
+    core, chip = lax.axis_index("tm") % 2, lax.axis_index("tm") // 2
+    before = jnp.zeros(keep_ref.shape, F32)
+    for m, piece in enumerate(pieces, 1):
+        before += jnp.where((chip ^ m) < chip, piece[...].astype(F32), 0.0)
+    send_ref[...] = (before + jnp.where(core == 0, keep_ref[...], 0.0)).astype(BF16)
+    mine_ref[...] = (before + jnp.where(core == 0, 0.0, got_ref[...].astype(F32))).astype(BF16)
+
+
+def call(kernel, breadth, outs, args, scratch=(), flops=3 * 10**9, name=None, through=None):
     def place(a):
         return pl.BlockSpec(memory_space=SMEM if a.size <= 64 else VMEM)
 
     in_specs, out_specs = [place(a) for a in args], [pl.BlockSpec(memory_space=VMEM) for _ in outs]
-    aliases = {}
-    if through is not None:
-        in_specs[through[0]] = out_specs[through[1]] = pl.BlockSpec(memory_space=pl.ANY)
-        aliases = {through[0]: through[1]}
+    for i, o in (through or {}).items():
+        in_specs[i] = pl.BlockSpec(memory_space=pl.ANY)
+        if o is not None:
+            out_specs[o] = in_specs[i]
     return pl.pallas_call(
         functools.partial(kernel, breadth),
         out_shape=[jax.ShapeDtypeStruct(s, d) for s, d in outs],
         in_specs=in_specs,
         out_specs=out_specs,
         scratch_shapes=[pltpu.VMEM(s, d) for s, d in scratch],
-        input_output_aliases=aliases,
+        input_output_aliases={i: o for i, o in (through or {}).items() if o is not None},
         compiler_params=pltpu.CompilerParams(vmem_limit_bytes=10 * 2**20),
         cost_estimate=pl.CostEstimate(flops=flops, bytes_accessed=2**20, transcendentals=0),
         name=name,
@@ -285,39 +302,41 @@
 def per_device(x, w, close, sharp, table, tally):
     groups, patches, width = x.shape
     breadth = width // sharp.shape[0]
-    core, chip = lax.axis_index("tm") % 2, lax.axis_index("tm") // 2
     chips = lax.axis_size("tm") // 2
     block = x.shape
     part = (groups, breadth, HALF)
     x_odd = swap_with(x, "stations", lambda i: i + 2 * (i % 2) - 1)
     x_even = swap_with(x, "stations", lambda i: i ^ 1)
-    normed, k, v, keep, give = call(
-        states_kernel, breadth, [(block, BF16)] * 3 + [(part, F32), (part, BF16)], (x, w), name="states"
+    wide = groups * T
+    (masks,) = call(masks_kernel, breadth, [((3, wide, wide * PAIR // breadth), F32)], (table, tally), name="masks")
+    k, v, keep, give = call(
+        states_kernel,
+        breadth,
+        [(block, BF16)] * 2 + [(part, F32), (part, BF16)],
+        (x, w, masks),
+        name="states",
+        through={2: None},
     )
     got = swap_with(give, "tm", lambda i: i ^ 1)
-    total = (keep + got.astype(F32)).astype(BF16)
+    (total,) = call(combine_kernel, breadth, [(part, BF16)], (keep, got), name="combine")
     pieces = [swap_with(total, "tm", lambda i: i ^ (2 * m)) for m in range(1, chips)]
-    q, lin = call(own_kernel, breadth, [(block, BF16), (block, F32)], (normed, w, k, v), name="own")
+    q, lin = call(own_kernel, breadth, [(block, BF16), (block, F32)], (x, w, k, v), name="own")
     acc, keep = call(
         even_kernel,
         breadth,
         [((groups, patches, 2 * width), F32), (part, F32)],
-        (x_even, w, k, v, q, sharp, table, tally, keep),
+        (x_even, w, k, v, q, sharp, masks, keep),
         [(block, BF16)] * 2,
         name="even",
-        through=(8, 1),
-    )
-    before = jnp.zeros_like(keep)
-    for m, piece in enumerate(pieces, 1):
-        before += jnp.where((chip ^ m) < chip, piece.astype(F32), 0.0)
-    send = (before + jnp.where(core == 0, keep, 0.0)).astype(BF16)
-    mine = before + jnp.where(core == 0, 0.0, got.astype(F32))
+        through={7: 1},
+    )
+    send, mine = call(carry_kernel, breadth, [(part, BF16)] * 2, (keep, got, *pieces), name="carry")
     other = swap_with(send, "tm", lambda i: i ^ 1)
     (y,) = call(
         odd_kernel,
         breadth,
         [(block, F32)],
-        (x_odd, w, q, sharp, table, tally, acc, x, close),
+        (x_odd, w, q, sharp, masks, acc, x, close),
         [(block, BF16)] * 3,
         name="odd",
     )

time: 27.5 us -> 25.7 us (0.935)
  the two profiles are of different devices: /device:TPU:9 before, /device:TPU:12 now
where the time goes in v3:
time: 25.7 us; the launch traced here: 25.5 us
  Pallas kernels  10.8 us (42%)
  starting transfers between devices  8.74 us (34%)
  waiting for transfers between devices  3.55 us (14%)
  local copies, waits for them, and re-layouts  2.34 us (9%)
    pallas_call x8, Pallas kernels, call(): pl.pallas_call(functools.partial(kernel, breadth), out_shape=[jax.ShapeDt...  10.8 us
    ppermute x7, starting transfers between devices, swap_with(): return lax.ppermute(value, axis, pairs)  8.74 us
    ppermute x7, waiting for transfers between devices, swap_with(): return lax.ppermute(value, axis, pairs)  3.55 us
    unnamed x12, local copies, waits for them, and re-layouts  2.34 us
  transfers between devices with their start and end apart: 7, of which 2 were waited for; matrix products, arithmetic and copies ran while one was open for 0% of the time, Pallas kernels for 36%

profile of v3, /device:TPU:12, one launch (start us, length us, event | category | flops | bytes accessed | tf_op | source)
XLA Modules:
  0.0 25.5 jit_solution(14579968968423798464)
XLA Ops:
  0.0 0.4 %collective-permute-start = (bf16[4,128,512]{2,1,0:T(8,128)(2,1)}, bf16[4,128,512]{2,1,0:T(8,128)(2,1)S(1)}, u32[]{:S(2)}, u32[]{:S(2)}) collective-permute-start(bf16[4,128,512]{2,1,0:T(8,128)(2,1)} %own_ref.1), channel_id=1, source_target_pairs={{0,8},{8,0},{16,24},{24,16},{1,9},{9,1},{17,25},{25,17},{2,10},{10... | collective-permute-start | bytes 1572872 | tf_op jit(solution)/shard_map/ppermute | solution.py:299
  0.5 4.6 %collective-permute-start.6 = (bf16[4,128,512]{2,1,0:T(8,128)(2,1)}, bf16[4,128,512]{2,1,0:T(8,128)(2,1)S(1)}, u32[]{:S(2)}, u32[]{:S(2)}) collective-permute-start(bf16[4,128,512]{2,1,0:T(8,128)(2,1)} %own_ref.1), channel_id=1, source_target_pairs={{8,16},{16,8},{9,17},{17,9},{10,18},{18,10},{11,19},{19,11},{12,20... | collective-permute-start | bytes 1572872 | tf_op jit(solution)/shard_map/ppermute | solution.py:299
  5.1 0.7 %copy-done.3 = s32[4,8]{1,0:T(4,128)S(1)} copy-done((s32[4,8]{1,0:T(4,128)S(1)}, s32[4,8]{1,0:T(4,128)}, u32[]{:S(2)}) %copy-start.3) | copy-done | bytes 152
  5.7 0.7 %copy-done.4 = s32[4]{0:T(128)S(1)} copy-done((s32[4]{0:T(128)S(1)}, s32[4]{0:T(128)}, u32[]{:S(2)}) %copy-start.4) | copy-done | bytes 40
  6.4 0.7 %masks.1.mask_ref = f32[3,128,256]{2,1,0:T(8,128)S(1)} custom-call(s32[4,8]{1,0:T(4,128)S(1)} %copy-done.3, s32[4]{0:T(128)S(1)} %copy-done.4), custom_call_target="tpu_custom_call" | custom-call | flops 3000000000 | bytes 1048576 | tf_op jit(solution)/shard_map/masks/pallas_call | solution.py:283
  7.1 1.5 %states.1 = (bf16[4,128,512]{2,1,0:T(8,128)(2,1)S(1)}, bf16[4,128,512]{2,1,0:T(8,128)(2,1)S(1)}, f32[4,64,256]{2,1,0:T(8,128)S(1)}, bf16[4,64,256]{2,1,0:T(8,128)(2,1)S(1)}) custom-call(bf16[4,128,512]{2,1,0:T(8,128)(2,1)S(1)} %copy-done.2, bf16[512,1536]{1,0:T(8,128)(2,1)S(1)} %copy-done, f32[3,128,256]{2,1,0:T(8,128)S(1)} %masks.1.mask_ref), custom_call_target="tpu_custom_call" | custom-call | flops 3000000000 | bytes 1048576 | tf_op jit(solution)/shard_map/states/pallas_call | solution.py:283
  8.6 0.1 collective-permute-start.1
  8.6 1.3 %own.1 = (bf16[4,128,512]{2,1,0:T(8,128)(2,1)S(1)}, f32[4,128,512]{2,1,0:T(8,128)S(1)}) custom-call(bf16[4,128,512]{2,1,0:T(8,128)(2,1)S(1)} %copy-done.2, bf16[512,1536]{1,0:T(8,128)(2,1)S(1)} %copy-done, bf16[4,128,512]{2,1,0:T(8,128)(2,1)S(1)} %get-tuple-element.15.k_ref, bf16[4,128,512]{2,1,0:T(8,128)(2,1)S(1)} %get-tuple-element.16.v_ref), custom_call_target="tpu_custom_call" | custom-call | flops 3000000000 | bytes 1048576 | tf_op jit(solution)/shard_map/own/pallas_call | solution.py:283
  9.9 0.0 collective-permute-done.1.got_ref
  10.0 1.6 %collective-permute-start.2 = (bf16[4,64,256]{2,1,0:T(8,128)(2,1)S(1)}, bf16[4,64,256]{2,1,0:T(8,128)(2,1)S(1)}, u32[]{:S(2)}, u32[]{:S(2)}) collective-permute-start(bf16[4,64,256]{2,1,0:T(8,128)(2,1)S(1)} %combine.1), channel_id=1, source_target_pairs={{0,2},{1,3},{2,0},{3,1},{4,6},{5,7},{6,4},{7,5},{8,10},{9,11},{10,... | collective-permute-start | bytes 393224 | tf_op jit(solution)/shard_map/ppermute | solution.py:299
  11.6 0.5 %collective-permute-start.3 = (bf16[4,64,256]{2,1,0:T(8,128)(2,1)S(1)}, bf16[4,64,256]{2,1,0:T(8,128)(2,1)S(1)}, u32[]{:S(2)}, u32[]{:S(2)}) collective-permute-start(bf16[4,64,256]{2,1,0:T(8,128)(2,1)S(1)} %combine.1), channel_id=1, source_target_pairs={{0,4},{1,5},{2,6},{3,7},{4,0},{5,1},{6,2},{7,3},{8,12},{9,13},{10,... | collective-permute-start | bytes 393224 | tf_op jit(solution)/shard_map/ppermute | solution.py:299
  12.1 1.5 %collective-permute-start.4 = (bf16[4,64,256]{2,1,0:T(8,128)(2,1)S(1)}, bf16[4,64,256]{2,1,0:T(8,128)(2,1)S(1)}, u32[]{:S(2)}, u32[]{:S(2)}) collective-permute-start(bf16[4,64,256]{2,1,0:T(8,128)(2,1)S(1)} %combine.1), channel_id=1, source_target_pairs={{0,6},{1,7},{2,4},{3,5},{4,2},{5,3},{6,0},{7,1},{8,14},{9,15},{10,... | collective-permute-start | bytes 393224 | tf_op jit(solution)/shard_map/ppermute | solution.py:299
  13.6 0.3 %collective-permute-done.x_ref = bf16[4,128,512]{2,1,0:T(8,128)(2,1)S(1)} collective-permute-done((bf16[4,128,512]{2,1,0:T(8,128)(2,1)}, bf16[4,128,512]{2,1,0:T(8,128)(2,1)S(1)}, u32[]{:S(2)}, u32[]{:S(2)}) %collective-permute-start) | collective-permute-done | bytes 524320 | tf_op jit(solution)/shard_map/ppermute | solution.py:299
  13.9 2.9 %even.1 = (f32[4,128,1024]{2,1,0:T(8,128)S(1)}, f32[4,64,256]{2,1,0:T(8,128)S(1)}) custom-call(bf16[4,128,512]{2,1,0:T(8,128)(2,1)S(1)} %collective-permute-done.x_ref, bf16[512,1536]{1,0:T(8,128)(2,1)S(1)} %copy-done, bf16[4,128,512]{2,1,0:T(8,128)(2,1)S(1)} %get-tuple-element.15.k_ref, ...), custom_call_target="tpu_custom_call", output_to_operand_aliasing={{1}: (7, {})} | custom-call | flops 3000000000 | bytes 1048576 | tf_op jit(solution)/shard_map/even/pallas_call | solution.py:283
  16.8 0.0 collective-permute-done.2.refs_0_
  16.8 3.2 %collective-permute-done.3.refs_1_ = bf16[4,64,256]{2,1,0:T(8,128)(2,1)S(1)} collective-permute-done((bf16[4,64,256]{2,1,0:T(8,128)(2,1)S(1)}, bf16[4,64,256]{2,1,0:T(8,128)(2,1)S(1)}, u32[]{:S(2)}, u32[]{:S(2)}) %collective-permute-start.3) | collective-permute-done | bytes 131104 | tf_op jit(solution)/shard_map/ppermute | solution.py:299
  20.0 0.0 collective-permute-done.4.refs_2_
  20.0 0.1 carry.1
  20.1 0.1 collective-permute-start.5
  20.2 0.0 collective-permute-done.6.x_ref
  20.2 1.0 %copy-done.1 = bf16[1024,512]{1,0:T(8,128)(2,1)S(1)} copy-done((bf16[1024,512]{1,0:T(8,128)(2,1)S(1)}, bf16[1024,512]{1,0:T(8,128)(2,1)}, u32[]{:S(2)}) %copy-start.1) | copy-done | bytes 1048600
  21.2 2.7 %odd.1.y_ref = f32[4,128,512]{2,1,0:T(8,128)S(1)} custom-call(bf16[4,128,512]{2,1,0:T(8,128)(2,1)S(1)} %collective-permute-done.6.x_ref, bf16[512,1536]{1,0:T(8,128)(2,1)S(1)} %copy-done, bf16[4,128,512]{2,1,0:T(8,128)(2,1)S(1)} %get-tuple-element.17.q_ref, f32[8]{0:T(128)S(1)} %copy-done.5, f32[3,128,256]{2,1,0:T(8,128)S(1)} %masks.1.mask_ref, ...), custom_call_target="tpu_custom_call" | custom-call | flops 3000000000 | bytes 1048576 | tf_op jit(solution)/shard_map/odd/pallas_call | solution.py:283
  23.9 0.0 collective-permute-done.5.other_ref
  23.9 1.6 %closing.1 = bf16[4,128,512]{2,1,0:T(8,128)(2,1)} custom-call(bf16[4,128,512]{2,1,0:T(8,128)(2,1)S(1)} %get-tuple-element.17.q_ref, f32[4,128,512]{2,1,0:T(8,128)S(1)} %get-tuple-element.18.lin_ref, bf16[4,64,256]{2,1,0:T(8,128)(2,1)S(1)} %get-tuple-element.22.mine_ref, bf16[4,64,256]{2,1,0:T(8,128)(2,1)S(1)} %collective-permute-done.5.other_ref, ...), custom_call_target="tpu_custom_call" | custom-call | flops 3000000000 | bytes 1048576 | tf_op jit(solution)/shard_map/closing/pallas_call | solution.py:283
  (10 shorter events, 0.0 us)
Async XLA Ops:
  0.0 7.1 %copy-start.2 = (bf16[4,128,512]{2,1,0:T(8,128)(2,1)S(1)}, bf16[4,128,512]{2,1,0:T(8,128)(2,1)}, u32[]{:S(2)}) copy-start(bf16[4,128,512]{2,1,0:T(8,128)(2,1)} %own_ref.1) | copy-start | bytes 1572868
  0.0 7.1 %copy-start = (bf16[512,1536]{1,0:T(8,128)(2,1)S(1)}, bf16[512,1536]{1,0:T(8,128)(2,1)}, u32[]{:S(2)}) copy-start(bf16[512,1536]{1,0:T(8,128)(2,1)} %w_ref.7) | copy-start | bytes 4718596
  0.0 13.9 %collective-permute-start = (bf16[4,128,512]{2,1,0:T(8,128)(2,1)}, bf16[4,128,512]{2,1,0:T(8,128)(2,1)S(1)}, u32[]{:S(2)}, u32[]{:S(2)}) collective-permute-start(bf16[4,128,512]{2,1,0:T(8,128)(2,1)} %own_ref.1), channel_id=1, source_target_pairs={{0,8},{8,0},{16,24},{24,16},{1,9},{9,1},{17,25},{25,17},{2,10},{10... | collective-permute-start | bytes 1572872 | tf_op jit(solution)/shard_map/ppermute | solution.py:299
  0.5 19.7 %collective-permute-start.6 = (bf16[4,128,512]{2,1,0:T(8,128)(2,1)}, bf16[4,128,512]{2,1,0:T(8,128)(2,1)S(1)}, u32[]{:S(2)}, u32[]{:S(2)}) collective-permute-start(bf16[4,128,512]{2,1,0:T(8,128)(2,1)} %own_ref.1), channel_id=1, source_target_pairs={{8,16},{16,8},{9,17},{17,9},{10,18},{18,10},{11,19},{19,11},{12,20... | collective-permute-start | bytes 1572872 | tf_op jit(solution)/shard_map/ppermute | solution.py:299
  5.1 0.7 %copy-start.3 = (s32[4,8]{1,0:T(4,128)S(1)}, s32[4,8]{1,0:T(4,128)}, u32[]{:S(2)}) copy-start(s32[4,8]{1,0:T(4,128)} %table_ref.1) | copy-start | bytes 388
  5.7 0.7 %copy-start.4 = (s32[4]{0:T(128)S(1)}, s32[4]{0:T(128)}, u32[]{:S(2)}) copy-start(s32[4]{0:T(128)} %tally_ref.1) | copy-start | bytes 52
  8.6 1.4 %collective-permute-start.1 = (bf16[4,64,256]{2,1,0:T(8,128)(2,1)S(1)}, bf16[4,64,256]{2,1,0:T(8,128)(2,1)S(1)}, u32[]{:S(2)}, u32[]{:S(2)}) collective-permute-start(bf16[4,64,256]{2,1,0:T(8,128)(2,1)S(1)} %get-tuple-element.21), channel_id=1, source_target_pairs={{0,1},{1,0},{2,3},{3,2},{4,5},{5,4},{6,7},{7,6},{8,9},{9,8},{10,11... | collective-permute-start | bytes 393224 | tf_op jit(solution)/shard_map/ppermute | solution.py:299
  10.0 3.9 %copy-start.5 = (f32[8]{0:T(128)S(1)}, f32[8]{0:T(128)}, u32[]{:S(2)}) copy-start(f32[8]{0:T(128)} %sharp_ref.3) | copy-start | bytes 100
  10.0 6.8 %collective-permute-start.2 = (bf16[4,64,256]{2,1,0:T(8,128)(2,1)S(1)}, bf16[4,64,256]{2,1,0:T(8,128)(2,1)S(1)}, u32[]{:S(2)}, u32[]{:S(2)}) collective-permute-start(bf16[4,64,256]{2,1,0:T(8,128)(2,1)S(1)} %combine.1), channel_id=1, source_target_pairs={{0,2},{1,3},{2,0},{3,1},{4,6},{5,7},{6,4},{7,5},{8,10},{9,11},{10,... | collective-permute-start | bytes 393224 | tf_op jit(solution)/shard_map/ppermute | solution.py:299
  11.6 8.4 %collective-permute-start.3 = (bf16[4,64,256]{2,1,0:T(8,128)(2,1)S(1)}, bf16[4,64,256]{2,1,0:T(8,128)(2,1)S(1)}, u32[]{:S(2)}, u32[]{:S(2)}) collective-permute-start(bf16[4,64,256]{2,1,0:T(8,128)(2,1)S(1)} %combine.1), channel_id=1, source_target_pairs={{0,4},{1,5},{2,6},{3,7},{4,0},{5,1},{6,2},{7,3},{8,12},{9,13},{10,... | collective-permute-start | bytes 393224 | tf_op jit(solution)/shard_map/ppermute | solution.py:299
  12.1 7.9 %collective-permute-start.4 = (bf16[4,64,256]{2,1,0:T(8,128)(2,1)S(1)}, bf16[4,64,256]{2,1,0:T(8,128)(2,1)S(1)}, u32[]{:S(2)}, u32[]{:S(2)}) collective-permute-start(bf16[4,64,256]{2,1,0:T(8,128)(2,1)S(1)} %combine.1), channel_id=1, source_target_pairs={{0,6},{1,7},{2,4},{3,5},{4,2},{5,3},{6,0},{7,1},{8,14},{9,15},{10,... | collective-permute-start | bytes 393224 | tf_op jit(solution)/shard_map/ppermute | solution.py:299
  20.0 1.2 %copy-start.1 = (bf16[1024,512]{1,0:T(8,128)(2,1)S(1)}, bf16[1024,512]{1,0:T(8,128)(2,1)}, u32[]{:S(2)}) copy-start(bf16[1024,512]{1,0:T(8,128)(2,1)} %close_ref.3) | copy-start | bytes 3145732
  20.1 3.8 %collective-permute-start.5 = (bf16[4,64,256]{2,1,0:T(8,128)(2,1)S(1)}, bf16[4,64,256]{2,1,0:T(8,128)(2,1)S(1)}, u32[]{:S(2)}, u32[]{:S(2)}) collective-permute-start(bf16[4,64,256]{2,1,0:T(8,128)(2,1)S(1)} %get-tuple-element.23), channel_id=1, source_target_pairs={{0,1},{1,0},{2,3},{3,2},{4,5},{5,4},{6,7},{7,6},{8,9},{9,8},{10,11... | collective-permute-start | bytes 393224 | tf_op jit(solution)/shard_map/ppermute | solution.py:299

commit v4 on v3

--- a/solution.py
+++ b/solution.py
@@ -39,9 +39,9 @@
     return lax.broadcasted_iota(jnp.int32, shape, axis) // breadth
 
 
-def mean_matrix(breadth):
+def means_kernel(breadth, means_ref):
     same = head_ids((HALF, HALF), 0, breadth) == head_ids((HALF, HALF), 1, breadth)
-    return jnp.where(same, 1.0 / breadth, 0.0).astype(BF16)
+    means_ref[...] = jnp.where(same, 1.0 / breadth, 0.0).astype(BF16)
 
 
 def head_norm(values, means, epsilon):
@@ -87,10 +87,10 @@
     return [dot(normed, w_ref[:, first + h * HALF : first + (h + 1) * HALF]) for h in range(count)]
 
 
-def keys_values(x_ref, w_ref, k_ref, v_ref, breadth):
+def keys_values(x_ref, w_ref, means_ref, k_ref, v_ref, breadth):
     groups, patches, width = x_ref.shape
     halves = width // HALF
-    means = mean_matrix(breadth)
+    means = means_ref[...]
     normed = row_norm(x_ref[...].reshape(groups * patches, width))
     keys = project(normed, w_ref, width, halves)
     values = project(normed, w_ref, 2 * width, halves)
@@ -143,7 +143,7 @@
     staggered(items, score, share, gather)
 
 
-def masks_kernel(breadth, table_ref, tally_ref, mask_ref):
+def masks_kernel(breadth, table_ref, tally_ref, total_ref, mask_ref):
     groups = table_ref.shape[0]
     station = lax.axis_index("stations")
     around = (station, station ^ 1, station + 2 * (station % 2) - 1)
@@ -152,10 +152,10 @@
         mask_ref[n] = jnp.concatenate([mask] * (PAIR // breadth), axis=1)
 
 
-def states_kernel(breadth, x_ref, w_ref, mask_ref, k_ref, v_ref, keep_ref, give_ref):
+def states_kernel(breadth, x_ref, w_ref, means_ref, k_ref, v_ref, keep_ref, give_ref):
     groups, patches, width = x_ref.shape
     core = lax.axis_index("tm") % 2
-    keys_values(x_ref, w_ref, k_ref, v_ref, breadth)
+    keys_values(x_ref, w_ref, means_ref, k_ref, v_ref, breadth)
     for h in range(width // HALF):
         states = []
         for g in range(groups):
@@ -177,10 +177,10 @@
                 give_ref[g] = states[g].astype(BF16)
 
 
-def own_kernel(breadth, x_ref, w_ref, k_ref, v_ref, q_ref, lin_ref):
+def own_kernel(breadth, x_ref, w_ref, means_ref, k_ref, v_ref, total_ref, q_ref, lin_ref):
     groups, patches, width = x_ref.shape
     halves = width // HALF
-    means = mean_matrix(breadth)
+    means = means_ref[...]
     wide = (patches, patches * (PAIR // breadth))
     causal = lax.broadcasted_iota(jnp.int32, wide, 0) >= lax.broadcasted_iota(jnp.int32, wide, 1) % patches
     queries = project(row_norm(x_ref[...].reshape(groups * patches, width)), w_ref, 0, halves)
@@ -207,53 +207,75 @@
     staggered([(h, g) for h in range(halves) for g in range(groups)], score, share, gather)
 
 
-def even_kernel(breadth, x_ref, w_ref, k_ref, v_ref, q_ref, sharp_ref, mask_ref, keep_ref, acc_ref, kept_ref, ke_ref, ve_ref):
-    groups, patches, width = x_ref.shape
-    keys_values(x_ref, w_ref, ke_ref, ve_ref, breadth)
-    windows = [
-        (k_ref, v_ref, mask_ref.at[0]),
-        (ke_ref, ve_ref, mask_ref.at[1]),
-    ]
+def near_kernel(breadth, k_ref, v_ref, q_ref, sharp_ref, mask_ref, acc_ref):
+    groups = q_ref.shape[0]
 
     def emit(c, u, total):
         acc_ref[:, c * T : (c + 1) * T, u * 2 * PAIR : (u + 1) * 2 * PAIR] = total.reshape(groups, T, 2 * PAIR)
 
-    neighbours(breadth, q_ref, windows, sharp_ref, emit)
-
-
-def odd_kernel(breadth, x_ref, w_ref, q_ref, sharp_ref, mask_ref, acc_ref, own_ref, close_ref, y_ref, k_ref, v_ref, gathered_ref):
-    groups, patches, width = x_ref.shape
-    keys_values(x_ref, w_ref, k_ref, v_ref, breadth)
-    windows = [(k_ref, v_ref, mask_ref.at[2])]
+    neighbours(breadth, q_ref, [(k_ref, v_ref, mask_ref.at[0])], sharp_ref, emit)
+
+
+def even_kernel(breadth, x_ref, w_ref, means_ref, q_ref, sharp_ref, mask_ref, acc_ref, keep_ref, sum_ref, kept_ref, k_ref, v_ref):
+    groups = x_ref.shape[0]
+    keys_values(x_ref, w_ref, means_ref, k_ref, v_ref, breadth)
 
     def emit(c, u, total):
-        span = slice(c * T, (c + 1) * T)
-        total = total.reshape(groups, T, 2 * PAIR) + acc_ref[:, span, u * 2 * PAIR : (u + 1) * 2 * PAIR]
-        gathered_ref[:, span, u * PAIR : (u + 1) * PAIR] = (total[:, :, :PAIR] / total[:, :, PAIR:]).astype(BF16)
-
-    neighbours(breadth, q_ref, windows, sharp_ref, emit)
-    mixed = dot(gathered_ref[...].reshape(groups * patches, width), close_ref[width:, :])
-    y_ref[...] = own_ref[...].astype(F32) + mixed.reshape(groups, patches, width)
-
-
-def closing_kernel(breadth, q_ref, lin_ref, mine_ref, other_ref, close_ref, y_ref, out_ref, normed_ref):
+        at = (slice(None), slice(c * T, (c + 1) * T), slice(u * 2 * PAIR, (u + 1) * 2 * PAIR))
+        sum_ref[at] = acc_ref[at] + total.reshape(groups, T, 2 * PAIR)
+
+    neighbours(breadth, q_ref, [(k_ref, v_ref, mask_ref.at[1])], sharp_ref, emit)
+
+
+def closing_kernel(breadth, q_ref, lin_ref, mine_ref, other_ref, means_ref, close_ref, x_ref, y_ref, normed_ref):
     groups, patches, width = q_ref.shape
     heads = HALF // breadth
     halves = width // HALF
     core = lax.axis_index("tm") % 2
-    means = mean_matrix(breadth)
-    same = head_ids((HALF, HALF), 0, breadth) == head_ids((HALF, HALF), 1, breadth)
+    means = means_ref[...]
     totals = []
     for h in range(halves):
         at = slice(h * HALF, (h + 1) * HALF)
         for g in range(groups):
             state = jnp.where(core == h, mine_ref[g], other_ref[g])
-            block = jnp.where(same, jnp.concatenate([state] * heads, axis=0), jnp.zeros((), BF16))
+            block = jnp.where(means > 0, jnp.concatenate([state] * heads, axis=0), jnp.zeros((), BF16))
             totals.append(lin_ref[g, :, at] + dot(q_ref[g, :, at], block))
     for h in range(halves):
         total = jnp.concatenate(totals[h * groups : (h + 1) * groups], axis=0)
         normed_ref[:, h * HALF : (h + 1) * HALF] = head_norm(total, means, 1e-05)
     mixed = dot(normed_ref[...], close_ref[:width, :])
+    y_ref[...] = x_ref[...].astype(F32) + mixed.reshape(groups, patches, width)
+
+
+def odd_kernel(breadth, x_ref, w_ref, means_ref, q_ref, sharp_ref, mask_ref, acc_ref, close_ref, y_ref, out_ref, k_ref, v_ref, gathered_ref):
+    groups, patches, width = x_ref.shape
+    station = lax.axis_index("stations")
+    partner = station + 2 * (station % 2) - 1
+    there = (partner >= 0) & (partner < lax.axis_size("stations"))
+
+    def part(c, u):
+        return (slice(None), slice(c * T, (c + 1) * T), slice(u * 2 * PAIR, (u + 1) * 2 * PAIR))
+
+    def finish(c, u, total):
+        share = total[:, :, :PAIR] / total[:, :, PAIR:]
+        gathered_ref[:, c * T : (c + 1) * T, u * PAIR : (u + 1) * PAIR] = share.astype(BF16)
+
+    @pl.when(there)
+    def _():
+        keys_values(x_ref, w_ref, means_ref, k_ref, v_ref, breadth)
+
+        def emit(c, u, total):
+            finish(c, u, acc_ref[part(c, u)] + total.reshape(groups, T, 2 * PAIR))
+
+        neighbours(breadth, q_ref, [(k_ref, v_ref, mask_ref.at[2])], sharp_ref, emit)
+
+    @pl.when(jnp.logical_not(there))
+    def _():
+        for u in range(width // PAIR):
+            for c in range(patches // T):
+                finish(c, u, acc_ref[part(c, u)])
+
+    mixed = dot(gathered_ref[...].reshape(groups * patches, width), close_ref[width:, :])
     out_ref[...] = (y_ref[...] + mixed.reshape(groups, patches, width)).astype(BF16)
 
 
@@ -271,7 +293,7 @@
     mine_ref[...] = (before + jnp.where(core == 0, 0.0, got_ref[...].astype(F32))).astype(BF16)
 
 
-def call(kernel, breadth, outs, args, scratch=(), flops=3 * 10**9, name=None, through=None):
+def call(kernel, breadth, outs, args, scratch=(), flops=10**9, name=None, through=None):
     def place(a):
         return pl.BlockSpec(memory_space=SMEM if a.size <= 64 else VMEM)
 
@@ -308,24 +330,36 @@
     x_odd = swap_with(x, "stations", lambda i: i + 2 * (i % 2) - 1)
     x_even = swap_with(x, "stations", lambda i: i ^ 1)
     wide = groups * T
-    (masks,) = call(masks_kernel, breadth, [((3, wide, wide * PAIR // breadth), F32)], (table, tally), name="masks")
+    sums = (groups, patches, 2 * width)
+    (means,) = call(means_kernel, breadth, [((HALF, HALF), BF16)], (), name="means")
     k, v, keep, give = call(
-        states_kernel,
-        breadth,
-        [(block, BF16)] * 2 + [(part, F32), (part, BF16)],
-        (x, w, masks),
-        name="states",
-        through={2: None},
+        states_kernel, breadth, [(block, BF16)] * 2 + [(part, F32), (part, BF16)], (x, w, means), name="states"
     )
     got = swap_with(give, "tm", lambda i: i ^ 1)
     (total,) = call(combine_kernel, breadth, [(part, BF16)], (keep, got), name="combine")
     pieces = [swap_with(total, "tm", lambda i: i ^ (2 * m)) for m in range(1, chips)]
-    q, lin = call(own_kernel, breadth, [(block, BF16), (block, F32)], (x, w, k, v), name="own")
+    q, lin = call(
+        own_kernel,
+        breadth,
+        [(block, BF16), (block, F32)],
+        (x, w, means, k, v, total),
+        name="own",
+        through={5: None},
+    )
+    (masks,) = call(
+        masks_kernel,
+        breadth,
+        [((3, wide, wide * PAIR // breadth), F32)],
+        (table, tally, total),
+        name="masks",
+        through={2: None},
+    )
+    (acc,) = call(near_kernel, breadth, [(sums, F32)], (k, v, q, sharp, masks), name="near")
     acc, keep = call(
         even_kernel,
         breadth,
-        [((groups, patches, 2 * width), F32), (part, F32)],
-        (x_even, w, k, v, q, sharp, masks, keep),
+        [(sums, F32), (part, F32)],
+        (x_even, w, means, q, sharp, masks, acc, keep),
         [(block, BF16)] * 2,
         name="even",
         through={7: 1},
@@ -333,20 +367,20 @@
     send, mine = call(carry_kernel, breadth, [(part, BF16)] * 2, (keep, got, *pieces), name="carry")
     other = swap_with(send, "tm", lambda i: i ^ 1)
     (y,) = call(
+        closing_kernel,
+        breadth,
+        [(block, F32)],
+        (q, lin, mine, other, means, close, x),
+        [((groups * patches, width), BF16)],
+        name="closing",
+    )
+    (out,) = call(
         odd_kernel,
         breadth,
-        [(block, F32)],
-        (x_odd, w, q, sharp, masks, acc, x, close),
+        [(block, BF16)],
+        (x_odd, w, means, q, sharp, masks, acc, close, y),
         [(block, BF16)] * 3,
         name="odd",
-    )
-    (out,) = call(
-        closing_kernel,
-        breadth,
-        [(block, BF16)],
-        (q, lin, mine, other, close, y),
-        [((groups * patches, width), BF16)],
-        name="closing",
     )
     return out
 

time: 25.7 us -> 23.2 us (0.903)
  the two profiles are of different devices: /device:TPU:12 before, /device:TPU:9 now
where the time goes in v4:
time: 23.2 us; the launch traced here: 22.9 us
  Pallas kernels  11.8 us (51%)
  starting transfers between devices  8.23 us (35%)
  local copies, waits for them, and re-layouts  1.55 us (7%)
  waiting for transfers between devices  1.07 us (5%)
    pallas_call x10, Pallas kernels, call(): pl.pallas_call(functools.partial(kernel, breadth), out_shape=[jax.ShapeDt...  11.8 us
    ppermute x7, starting transfers between devices, swap_with(): return lax.ppermute(value, axis, pairs)  8.23 us
    unnamed x12, local copies, waits for them, and re-layouts  1.55 us
    ppermute x7, waiting for transfers between devices, swap_with(): return lax.ppermute(value, axis, pairs)  1.07 us
  transfers between devices with their start and end apart: 7, of which 2 were waited for; matrix products, arithmetic and copies ran while one was open for 0% of the time, Pallas kernels for 36%

profile of v4, /device:TPU:9, one launch (start us, length us, event | category | flops | bytes accessed | tf_op | source)
XLA Modules:
  0.0 22.9 jit_solution(4260454873866485226)
XLA Ops:
  0.1 1.0 %copy-done.2 = bf16[4,128,512]{2,1,0:T(8,128)(2,1)S(1)} copy-done((bf16[4,128,512]{2,1,0:T(8,128)(2,1)S(1)}, bf16[4,128,512]{2,1,0:T(8,128)(2,1)}, u32[]{:S(2)}) %copy-start.2) | copy-done | bytes 524312
  1.0 0.5 %copy-done = bf16[512,1536]{1,0:T(8,128)(2,1)S(1)} copy-done((bf16[512,1536]{1,0:T(8,128)(2,1)S(1)}, bf16[512,1536]{1,0:T(8,128)(2,1)}, u32[]{:S(2)}) %copy-start) | copy-done | bytes 1572888
  1.6 1.5 %states.1 = (bf16[4,128,512]{2,1,0:T(8,128)(2,1)S(1)}, bf16[4,128,512]{2,1,0:T(8,128)(2,1)S(1)}, f32[4,64,256]{2,1,0:T(8,128)S(1)}, bf16[4,64,256]{2,1,0:T(8,128)(2,1)S(1)}) custom-call(bf16[4,128,512]{2,1,0:T(8,128)(2,1)S(1)} %copy-done.2, bf16[512,1536]{1,0:T(8,128)(2,1)S(1)} %copy-done, bf16[256,256]{1,0:T(8,128)(2,1)S(1)} %means.1.means_ref), custom_call_target="tpu_custom_call" | custom-call | flops 1000000000 | bytes 1048576 | tf_op jit(solution)/shard_map/states/pallas_call | solution.py:305
  3.0 0.7 %collective-permute-start.1 = (bf16[4,64,256]{2,1,0:T(8,128)(2,1)S(1)}, bf16[4,64,256]{2,1,0:T(8,128)(2,1)S(1)}, u32[]{:S(2)}, u32[]{:S(2)}) collective-permute-start(bf16[4,64,256]{2,1,0:T(8,128)(2,1)S(1)} %get-tuple-element.18), channel_id=1, source_target_pairs={{0,1},{1,0},{2,3},{3,2},{4,5},{5,4},{6,7},{7,6},{8,9},{9,8},{10,11... | collective-permute-start | bytes 393224 | tf_op jit(solution)/shard_map/ppermute | solution.py:321
  3.8 3.3 %collective-permute-start = (bf16[4,128,512]{2,1,0:T(8,128)(2,1)S(1)}, bf16[4,128,512]{2,1,0:T(8,128)(2,1)S(1)}, u32[]{:S(2)}, u32[]{:S(2)}) collective-permute-start(bf16[4,128,512]{2,1,0:T(8,128)(2,1)S(1)} %copy-done.2), channel_id=1, source_target_pairs={{8,16},{16,8},{9,17},{17,9},{10,18},{18,10},{11,19},{19,11},{12,20... | collective-permute-start | bytes 1572872 | tf_op jit(solution)/shard_map/ppermute | solution.py:321
  7.0 0.0 collective-permute-done.1.got_ref
  7.1 0.0 copy-start.4
  7.1 0.0 copy-start.5
  7.1 1.3 %collective-permute-start.3 = (bf16[4,64,256]{2,1,0:T(8,128)(2,1)S(1)}, bf16[4,64,256]{2,1,0:T(8,128)(2,1)S(1)}, u32[]{:S(2)}, u32[]{:S(2)}) collective-permute-start(bf16[4,64,256]{2,1,0:T(8,128)(2,1)S(1)} %combine.1.total_ref), channel_id=1, source_target_pairs={{0,2},{1,3},{2,0},{3,1},{4,6},{5,7},{6,4},{7,5},{8,10},{9,11},{10,... | collective-permute-start | bytes 393224 | tf_op jit(solution)/shard_map/ppermute | solution.py:321
  8.4 1.2 %collective-permute-start.4 = (bf16[4,64,256]{2,1,0:T(8,128)(2,1)S(1)}, bf16[4,64,256]{2,1,0:T(8,128)(2,1)S(1)}, u32[]{:S(2)}, u32[]{:S(2)}) collective-permute-start(bf16[4,64,256]{2,1,0:T(8,128)(2,1)S(1)} %combine.1.total_ref), channel_id=1, source_target_pairs={{0,4},{1,5},{2,6},{3,7},{4,0},{5,1},{6,2},{7,3},{8,12},{9,13},{10,... | collective-permute-start | bytes 393224 | tf_op jit(solution)/shard_map/ppermute | solution.py:321
  9.6 0.2 collective-permute-start.5
  9.8 1.3 %own.1 = (bf16[4,128,512]{2,1,0:T(8,128)(2,1)S(1)}, f32[4,128,512]{2,1,0:T(8,128)S(1)}) custom-call(bf16[4,128,512]{2,1,0:T(8,128)(2,1)S(1)} %copy-done.2, bf16[512,1536]{1,0:T(8,128)(2,1)S(1)} %copy-done, bf16[256,256]{1,0:T(8,128)(2,1)S(1)} %means.1.means_ref, bf16[4,128,512]{2,1,0:T(8,128)(2,1)S(1)} %get-tuple-element.15.k_ref, ...), custom_call_target="tpu_custom_call" | custom-call | flops 1000000000 | bytes 1048576 | tf_op jit(solution)/shard_map/own/pallas_call | solution.py:305
  11.2 0.0 copy-start.3
  11.2 0.7 %masks.1.mask_ref = f32[3,128,256]{2,1,0:T(8,128)S(1)} custom-call(s32[4,8]{1,0:T(4,128)S(1)} %copy-done.4, s32[4]{0:T(128)S(1)} %copy-done.5, bf16[4,64,256]{2,1,0:T(8,128)(2,1)S(1)} %combine.1.total_ref), custom_call_target="tpu_custom_call" | custom-call | flops 1000000000 | bytes 1048576 | tf_op jit(solution)/shard_map/masks/pallas_call | solution.py:305
  11.9 1.4 %near.1.acc_ref = f32[4,128,1024]{2,1,0:T(8,128)S(1)} custom-call(bf16[4,128,512]{2,1,0:T(8,128)(2,1)S(1)} %get-tuple-element.15.k_ref, bf16[4,128,512]{2,1,0:T(8,128)(2,1)S(1)} %get-tuple-element.16.v_ref, bf16[4,128,512]{2,1,0:T(8,128)(2,1)S(1)} %get-tuple-element.19.q_ref, f32[8]{0:T(128)S(1)} %copy-done.3, f32[3,128,256]{2,1,0:T(8,128)S(1)} %masks.1.mask_ref), custom_call_target="tpu_custom_call" | custom-call | flops 1000000000 | bytes 1048576 | tf_op jit(solution)/shard_map/near/pallas_call | solution.py:305
  13.3 0.0 collective-permute-done.2.x_ref
  13.3 2.3 %even.1 = (f32[4,128,1024]{2,1,0:T(8,128)S(1)}, f32[4,64,256]{2,1,0:T(8,128)S(1)}) custom-call(bf16[4,128,512]{2,1,0:T(8,128)(2,1)S(1)} %collective-permute-done.2.x_ref, bf16[512,1536]{1,0:T(8,128)(2,1)S(1)} %copy-done, bf16[256,256]{1,0:T(8,128)(2,1)S(1)} %means.1.means_ref, ...), custom_call_target="tpu_custom_call", output_to_operand_aliasing={{1}: (7, {})} | custom-call | flops 1000000000 | bytes 1048576 | tf_op jit(solution)/shard_map/even/pallas_call | solution.py:305
  15.6 0.0 copy-start.1
  15.7 0.1 carry.1
  15.8 1.5 %collective-permute-start.6 = (bf16[4,64,256]{2,1,0:T(8,128)(2,1)S(1)}, bf16[4,64,256]{2,1,0:T(8,128)(2,1)S(1)}, u32[]{:S(2)}, u32[]{:S(2)}) collective-permute-start(bf16[4,64,256]{2,1,0:T(8,128)(2,1)S(1)} %get-tuple-element.24), channel_id=1, source_target_pairs={{0,1},{1,0},{2,3},{3,2},{4,5},{5,4},{6,7},{7,6},{8,9},{9,8},{10,11... | collective-permute-start | bytes 393224 | tf_op jit(solution)/shard_map/ppermute | solution.py:321
  17.3 1.0 %collective-permute-done.6.other_ref = bf16[4,64,256]{2,1,0:T(8,128)(2,1)S(1)} collective-permute-done((bf16[4,64,256]{2,1,0:T(8,128)(2,1)S(1)}, bf16[4,64,256]{2,1,0:T(8,128)(2,1)S(1)}, u32[]{:S(2)}, u32[]{:S(2)}) %collective-permute-start.6) | collective-permute-done | bytes 131104 | tf_op jit(solution)/shard_map/ppermute | solution.py:321
  18.3 0.8 %closing.1.y_ref = f32[4,128,512]{2,1,0:T(8,128)S(1)} custom-call(bf16[4,128,512]{2,1,0:T(8,128)(2,1)S(1)} %get-tuple-element.19.q_ref, f32[4,128,512]{2,1,0:T(8,128)S(1)} %get-tuple-element.21.lin_ref, bf16[4,64,256]{2,1,0:T(8,128)(2,1)S(1)} %get-tuple-element.23.mine_ref, bf16[4,64,256]{2,1,0:T(8,128)(2,1)S(1)} %collective-permute-done.6.other_ref, ...), custom_call_target="tpu_custom_call" | custom-call | flops 1000000000 | bytes 1048576 | tf_op jit(solution)/shard_map/closing/pallas_call | solution.py:305
  19.1 0.1 collective-permute-done.x_ref
  19.2 3.7 %odd.1 = bf16[4,128,512]{2,1,0:T(8,128)(2,1)} custom-call(bf16[4,128,512]{2,1,0:T(8,128)(2,1)S(1)} %collective-permute-done.x_ref, bf16[512,1536]{1,0:T(8,128)(2,1)S(1)} %copy-done, bf16[256,256]{1,0:T(8,128)(2,1)S(1)} %means.1.means_ref, bf16[4,128,512]{2,1,0:T(8,128)(2,1)S(1)} %get-tuple-element.19.q_ref, f32[8]{0:T(128)S(1)} %copy-done.3, ...), custom_call_target="tpu_custom_call" | custom-call | flops 1000000000 | bytes 1048576 | tf_op jit(solution)/shard_map/odd/pallas_call | solution.py:305
  (12 shorter events, 0.1 us)
Async XLA Ops:
  0.0 1.0 %copy-start.2 = (bf16[4,128,512]{2,1,0:T(8,128)(2,1)S(1)}, bf16[4,128,512]{2,1,0:T(8,128)(2,1)}, u32[]{:S(2)}) copy-start(bf16[4,128,512]{2,1,0:T(8,128)(2,1)} %x_ref.5) | copy-start | bytes 1572868
  0.0 1.6 %copy-start = (bf16[512,1536]{1,0:T(8,128)(2,1)S(1)}, bf16[512,1536]{1,0:T(8,128)(2,1)}, u32[]{:S(2)}) copy-start(bf16[512,1536]{1,0:T(8,128)(2,1)} %w_ref.7) | copy-start | bytes 4718596
  0.0 13.3 %collective-permute-start.2 = (bf16[4,128,512]{2,1,0:T(8,128)(2,1)}, bf16[4,128,512]{2,1,0:T(8,128)(2,1)S(1)}, u32[]{:S(2)}, u32[]{:S(2)}) collective-permute-start(bf16[4,128,512]{2,1,0:T(8,128)(2,1)} %x_ref.5), channel_id=1, source_target_pairs={{0,8},{8,0},{16,24},{24,16},{1,9},{9,1},{17,25},{25,17},{2,10},{10... | collective-permute-start | bytes 1572872 | tf_op jit(solution)/shard_map/ppermute | solution.py:321
  3.0 4.0 %collective-permute-start.1 = (bf16[4,64,256]{2,1,0:T(8,128)(2,1)S(1)}, bf16[4,64,256]{2,1,0:T(8,128)(2,1)S(1)}, u32[]{:S(2)}, u32[]{:S(2)}) collective-permute-start(bf16[4,64,256]{2,1,0:T(8,128)(2,1)S(1)} %get-tuple-element.18), channel_id=1, source_target_pairs={{0,1},{1,0},{2,3},{3,2},{4,5},{5,4},{6,7},{7,6},{8,9},{9,8},{10,11... | collective-permute-start | bytes 393224 | tf_op jit(solution)/shard_map/ppermute | solution.py:321
  3.8 15.4 %collective-permute-start = (bf16[4,128,512]{2,1,0:T(8,128)(2,1)S(1)}, bf16[4,128,512]{2,1,0:T(8,128)(2,1)S(1)}, u32[]{:S(2)}, u32[]{:S(2)}) collective-permute-start(bf16[4,128,512]{2,1,0:T(8,128)(2,1)S(1)} %copy-done.2), channel_id=1, source_target_pairs={{8,16},{16,8},{9,17},{17,9},{10,18},{18,10},{11,19},{19,11},{12,20... | collective-permute-start | bytes 1572872 | tf_op jit(solution)/shard_map/ppermute | solution.py:321
  7.1 4.1 %copy-start.4 = (s32[4,8]{1,0:T(4,128)S(1)}, s32[4,8]{1,0:T(4,128)}, u32[]{:S(2)}) copy-start(s32[4,8]{1,0:T(4,128)} %table_ref.1) | copy-start | bytes 388
  7.1 4.1 %copy-start.5 = (s32[4]{0:T(128)S(1)}, s32[4]{0:T(128)}, u32[]{:S(2)}) copy-start(s32[4]{0:T(128)} %tally_ref.1) | copy-start | bytes 52
  7.1 8.5 %collective-permute-start.3 = (bf16[4,64,256]{2,1,0:T(8,128)(2,1)S(1)}, bf16[4,64,256]{2,1,0:T(8,128)(2,1)S(1)}, u32[]{:S(2)}, u32[]{:S(2)}) collective-permute-start(bf16[4,64,256]{2,1,0:T(8,128)(2,1)S(1)} %combine.1.total_ref), channel_id=1, source_target_pairs={{0,2},{1,3},{2,0},{3,1},{4,6},{5,7},{6,4},{7,5},{8,10},{9,11},{10,... | collective-permute-start | bytes 393224 | tf_op jit(solution)/shard_map/ppermute | solution.py:321
  8.4 7.2 %collective-permute-start.4 = (bf16[4,64,256]{2,1,0:T(8,128)(2,1)S(1)}, bf16[4,64,256]{2,1,0:T(8,128)(2,1)S(1)}, u32[]{:S(2)}, u32[]{:S(2)}) collective-permute-start(bf16[4,64,256]{2,1,0:T(8,128)(2,1)S(1)} %combine.1.total_ref), channel_id=1, source_target_pairs={{0,4},{1,5},{2,6},{3,7},{4,0},{5,1},{6,2},{7,3},{8,12},{9,13},{10,... | collective-permute-start | bytes 393224 | tf_op jit(solution)/shard_map/ppermute | solution.py:321
  9.6 6.0 %collective-permute-start.5 = (bf16[4,64,256]{2,1,0:T(8,128)(2,1)S(1)}, bf16[4,64,256]{2,1,0:T(8,128)(2,1)S(1)}, u32[]{:S(2)}, u32[]{:S(2)}) collective-permute-start(bf16[4,64,256]{2,1,0:T(8,128)(2,1)S(1)} %combine.1.total_ref), channel_id=1, source_target_pairs={{0,6},{1,7},{2,4},{3,5},{4,2},{5,3},{6,0},{7,1},{8,14},{9,15},{10,... | collective-permute-start | bytes 393224 | tf_op jit(solution)/shard_map/ppermute | solution.py:321
  11.2 0.7 %copy-start.3 = (f32[8]{0:T(128)S(1)}, f32[8]{0:T(128)}, u32[]{:S(2)}) copy-start(f32[8]{0:T(128)} %sharp_ref.5) | copy-start | bytes 100
  15.6 2.7 %copy-start.1 = (bf16[1024,512]{1,0:T(8,128)(2,1)S(1)}, bf16[1024,512]{1,0:T(8,128)(2,1)}, u32[]{:S(2)}) copy-start(bf16[1024,512]{1,0:T(8,128)(2,1)} %close_ref.3) | copy-start | bytes 3145732
  15.8 2.5 %collective-permute-start.6 = (bf16[4,64,256]{2,1,0:T(8,128)(2,1)S(1)}, bf16[4,64,256]{2,1,0:T(8,128)(2,1)S(1)}, u32[]{:S(2)}, u32[]{:S(2)}) collective-permute-start(bf16[4,64,256]{2,1,0:T(8,128)(2,1)S(1)} %get-tuple-element.24), channel_id=1, source_target_pairs={{0,1},{1,0},{2,3},{3,2},{4,5},{5,4},{6,7},{7,6},{8,9},{9,8},{10,11... | collective-permute-start | bytes 393224 | tf_op jit(solution)/shard_map/ppermute | solution.py:321

commit v5 on v4

--- a/solution.py
+++ b/solution.py
@@ -52,22 +52,6 @@
 def own_head(values, j, breadth):
     ids = head_ids(values.shape, 1, breadth)
     return jnp.where(ids == j, values, jnp.zeros_like(values))
-
-
-def multiplicity_mask(table_ref, tally_ref, base):
-    groups, slots = table_ref.shape
-    wide = groups * T
-    ids = base + lax.broadcasted_iota(jnp.int32, (8, wide), 1) // T
-    rows = []
-    for g in range(groups):
-        total = jnp.zeros((8, wide), F32)
-        for j in range(slots):
-            total += jnp.where((ids == table_ref[g, j]) & (j < tally_ref[g]), 1.0, 0.0)
-        rows.append(jnp.broadcast_to(total[:1], (T, wide)))
-    full = jnp.concatenate(rows, axis=0)
-    t_row = lax.broadcasted_iota(jnp.int32, (wide, wide), 0) % T
-    t_col = lax.broadcasted_iota(jnp.int32, (wide, wide), 1) % T
-    return jnp.where(t_row == t_col, full, 0.0)
 
 
 def pick(low, high, breadth):
@@ -144,12 +128,26 @@
 
 
 def masks_kernel(breadth, table_ref, tally_ref, total_ref, mask_ref):
-    groups = table_ref.shape[0]
+    groups, slots = table_ref.shape
+    wide = groups * T
     station = lax.axis_index("stations")
     around = (station, station ^ 1, station + 2 * (station % 2) - 1)
-    for n, place in enumerate(around):
-        mask = multiplicity_mask(table_ref, tally_ref, place * groups)
-        mask_ref[n] = jnp.concatenate([mask] * (PAIR // breadth), axis=1)
+    position = lax.broadcasted_iota(jnp.int32, (8, wide), 1) // T
+    ids = jnp.concatenate([place * groups + position for place in around], axis=1)
+    rows = []
+    for g in range(groups):
+        counts = jnp.zeros(ids.shape, F32)
+        for j in range(slots):
+            slot = jnp.where(j < tally_ref[g], table_ref[g, j], -(1 << 20))
+            counts += jnp.where(ids == slot, 1.0, 0.0)
+        rows.append(counts[:1])
+    t_row = lax.broadcasted_iota(jnp.int32, (T, wide), 0)
+    t_col = lax.broadcasted_iota(jnp.int32, (T, wide), 1) % T
+    for n in range(len(around)):
+        for g in range(groups):
+            block = jnp.where(t_row == t_col, jnp.broadcast_to(rows[g][:, n * wide : (n + 1) * wide], (T, wide)), 0.0)
+            for j in range(PAIR // breadth):
+                mask_ref[n, g * T : (g + 1) * T, j * wide : (j + 1) * wide] = block
 
 
 def states_kernel(breadth, x_ref, w_ref, means_ref, k_ref, v_ref, keep_ref, give_ref):
@@ -227,12 +225,45 @@
     neighbours(breadth, q_ref, [(k_ref, v_ref, mask_ref.at[1])], sharp_ref, emit)
 
 
-def closing_kernel(breadth, q_ref, lin_ref, mine_ref, other_ref, means_ref, close_ref, x_ref, y_ref, normed_ref):
+def odd_kernel(breadth, x_ref, w_ref, means_ref, q_ref, sharp_ref, mask_ref, acc_ref, gathered_ref, k_ref, v_ref):
+    groups, patches, width = x_ref.shape
+    station = lax.axis_index("stations")
+    partner = station + 2 * (station % 2) - 1
+    there = (partner >= 0) & (partner < lax.axis_size("stations"))
+
+    def part(c, u):
+        return (slice(None), slice(c * T, (c + 1) * T), slice(u * 2 * PAIR, (u + 1) * 2 * PAIR))
+
+    def finish(c, u, total):
+        share, weight = total[:, :, :PAIR], total[:, :, PAIR:]
+        near = pl.reciprocal(weight, approx=True)
+        share = share * (near * (2.0 - weight * near))
+        gathered_ref[:, c * T : (c + 1) * T, u * PAIR : (u + 1) * PAIR] = share.astype(BF16)
+
+    @pl.when(there)
+    def _():
+        keys_values(x_ref, w_ref, means_ref, k_ref, v_ref, breadth)
+
+        def emit(c, u, total):
+            finish(c, u, acc_ref[part(c, u)] + total.reshape(groups, T, 2 * PAIR))
+
+        neighbours(breadth, q_ref, [(k_ref, v_ref, mask_ref.at[2])], sharp_ref, emit)
+
+    @pl.when(jnp.logical_not(there))
+    def _():
+        for u in range(width // PAIR):
+            for c in range(patches // T):
+                finish(c, u, acc_ref[part(c, u)])
+
+
+def closing_kernel(breadth, q_ref, lin_ref, mine_ref, other_ref, means_ref, close_ref, x_ref, gathered_ref, out_ref):
     groups, patches, width = q_ref.shape
+    rows = groups * patches
     heads = HALF // breadth
     halves = width // HALF
     core = lax.axis_index("tm") % 2
     means = means_ref[...]
+    mixed = dot(gathered_ref[...].reshape(rows, width), close_ref[width:, :])
     totals = []
     for h in range(halves):
         at = slice(h * HALF, (h + 1) * HALF)
@@ -242,41 +273,8 @@
             totals.append(lin_ref[g, :, at] + dot(q_ref[g, :, at], block))
     for h in range(halves):
         total = jnp.concatenate(totals[h * groups : (h + 1) * groups], axis=0)
-        normed_ref[:, h * HALF : (h + 1) * HALF] = head_norm(total, means, 1e-05)
-    mixed = dot(normed_ref[...], close_ref[:width, :])
-    y_ref[...] = x_ref[...].astype(F32) + mixed.reshape(groups, patches, width)
-
-
-def odd_kernel(breadth, x_ref, w_ref, means_ref, q_ref, sharp_ref, mask_ref, acc_ref, close_ref, y_ref, out_ref, k_ref, v_ref, gathered_ref):
-    groups, patches, width = x_ref.shape
-    station = lax.axis_index("stations")
-    partner = station + 2 * (station % 2) - 1
-    there = (partner >= 0) & (partner < lax.axis_size("stations"))
-
-    def part(c, u):
-        return (slice(None), slice(c * T, (c + 1) * T), slice(u * 2 * PAIR, (u + 1) * 2 * PAIR))
-
-    def finish(c, u, total):
-        share = total[:, :, :PAIR] / total[:, :, PAIR:]
-        gathered_ref[:, c * T : (c + 1) * T, u * PAIR : (u + 1) * PAIR] = share.astype(BF16)
-
-    @pl.when(there)
-    def _():
-        keys_values(x_ref, w_ref, means_ref, k_ref, v_ref, breadth)
-
-        def emit(c, u, total):
-            finish(c, u, acc_ref[part(c, u)] + total.reshape(groups, T, 2 * PAIR))
-
-        neighbours(breadth, q_ref, [(k_ref, v_ref, mask_ref.at[2])], sharp_ref, emit)
-
-    @pl.when(jnp.logical_not(there))
-    def _():
-        for u in range(width // PAIR):
-            for c in range(patches // T):
-                finish(c, u, acc_ref[part(c, u)])
-
-    mixed = dot(gathered_ref[...].reshape(groups * patches, width), close_ref[width:, :])
-    out_ref[...] = (y_ref[...] + mixed.reshape(groups, patches, width)).astype(BF16)
+        mixed += dot(head_norm(total, means, 1e-05), close_ref[h * HALF : (h + 1) * HALF, :])
+    out_ref[...] = (x_ref[...].astype(F32) + mixed.reshape(groups, patches, width)).astype(BF16)
 
 
 def combine_kernel(breadth, keep_ref, got_ref, total_ref):
@@ -293,7 +291,7 @@
     mine_ref[...] = (before + jnp.where(core == 0, 0.0, got_ref[...].astype(F32))).astype(BF16)
 
 
-def call(kernel, breadth, outs, args, scratch=(), flops=10**9, name=None, through=None):
+def call(kernel, breadth, outs, args, scratch=(), flops=10**6, name=None, through=None):
     def place(a):
         return pl.BlockSpec(memory_space=SMEM if a.size <= 64 else VMEM)
 
@@ -331,7 +329,7 @@
     x_even = swap_with(x, "stations", lambda i: i ^ 1)
     wide = groups * T
     sums = (groups, patches, 2 * width)
-    (means,) = call(means_kernel, breadth, [((HALF, HALF), BF16)], (), name="means")
+    (means,) = call(means_kernel, breadth, [((HALF, HALF), BF16)], (), name="means", flops=10**10)
     k, v, keep, give = call(
         states_kernel, breadth, [(block, BF16)] * 2 + [(part, F32), (part, BF16)], (x, w, means), name="states"
     )
@@ -366,21 +364,16 @@
     )
     send, mine = call(carry_kernel, breadth, [(part, BF16)] * 2, (keep, got, *pieces), name="carry")
     other = swap_with(send, "tm", lambda i: i ^ 1)
-    (y,) = call(
-        closing_kernel,
-        breadth,
-        [(block, F32)],
-        (q, lin, mine, other, means, close, x),
-        [((groups * patches, width), BF16)],
-        name="closing",
-    )
-    (out,) = call(
+    (gathered,) = call(
         odd_kernel,
         breadth,
         [(block, BF16)],
-        (x_odd, w, means, q, sharp, masks, acc, close, y),
-        [(block, BF16)] * 3,
+        (x_odd, w, means, q, sharp, masks, acc),
+        [(block, BF16)] * 2,
         name="odd",
+    )
+    (out,) = call(
+        closing_kernel, breadth, [(block, BF16)], (q, lin, mine, other, means, close, x, gathered), name="closing"
     )
     return out
 

time: 23.2 us -> 23.2 us (level)
  starting transfers between devices: 8.23 us -> 10.1 us
  local copies, waits for them, and re-layouts: 1.55 us -> 0.03 us
    ppermute x7, starting transfers between devices: 8.23 us -> 10.1 us  [swap_with(): return lax.ppermute(value, axis, pairs)]
    unnamed x12, local copies, waits for them, and re-layouts: 1.55 us -> 0.03 us
  transfers between devices with their start and end apart: 7 -> 7, of which waited for: 2 -> 1; matrix products, arithmetic and copies ran while one was open for 0% -> 0% of each run, Pallas kernels for 36% -> 43%
where the time goes in v5:
time: 23.2 us; the launch traced here: 23 us
  Pallas kernels  11.8 us (51%)
  starting transfers between devices  10.1 us (44%)
  waiting for transfers between devices  1 us (4%)
    pallas_call x10, Pallas kernels, call(): pl.pallas_call(functools.partial(kernel, breadth), out_shape=[jax.ShapeDt...  11.8 us
    ppermute x7, starting transfers between devices, swap_with(): return lax.ppermute(value, axis, pairs)  10.1 us
    ppermute x7, waiting for transfers between devices, swap_with(): return lax.ppermute(value, axis, pairs)  1 us
  transfers between devices with their start and end apart: 7, of which 1 were waited for; matrix products, arithmetic and copies ran while one was open for 0% of the time, Pallas kernels for 43%

profile of v5, /device:TPU:9, one launch (start us, length us, event | category | flops | bytes accessed | tf_op | source)
XLA Modules:
  0.0 23.0 jit_solution(15105954491592333723)
XLA Ops:
  0.0 0.0 collective-permute-start.1
  0.0 4.5 %collective-permute-start.6 = (bf16[4,128,512]{2,1,0:T(8,128)(2,1)}, bf16[4,128,512]{2,1,0:T(8,128)(2,1)S(1)}, u32[]{:S(2)}, u32[]{:S(2)}) collective-permute-start(bf16[4,128,512]{2,1,0:T(8,128)(2,1)} %x_ref.5), channel_id=1, source_target_pairs={{8,16},{16,8},{9,17},{17,9},{10,18},{18,10},{11,19},{19,11},{12,20... | collective-permute-start | bytes 1572872 | tf_op jit(solution)/shard_map/ppermute | solution.py:319
  4.6 1.5 %states.1 = (bf16[4,128,512]{2,1,0:T(8,128)(2,1)S(1)}, bf16[4,128,512]{2,1,0:T(8,128)(2,1)S(1)}, f32[4,64,256]{2,1,0:T(8,128)S(1)}, bf16[4,64,256]{2,1,0:T(8,128)(2,1)S(1)}) custom-call(bf16[4,128,512]{2,1,0:T(8,128)(2,1)S(1)} %copy-done.1, bf16[512,1536]{1,0:T(8,128)(2,1)S(1)} %copy-done, bf16[256,256]{1,0:T(8,128)(2,1)S(1)} %means.1.means_ref), custom_call_target="tpu_custom_call" | custom-call | flops 1000000 | bytes 1048576 | tf_op jit(solution)/shard_map/states/pallas_call | solution.py:303
  6.0 0.0 copy-start.4
  6.0 0.0 copy-start.5
  6.0 1.3 %collective-permute-start = (bf16[4,64,256]{2,1,0:T(8,128)(2,1)S(1)}, bf16[4,64,256]{2,1,0:T(8,128)(2,1)S(1)}, u32[]{:S(2)}, u32[]{:S(2)}) collective-permute-start(bf16[4,64,256]{2,1,0:T(8,128)(2,1)S(1)} %get-tuple-element.18), channel_id=1, source_target_pairs={{0,1},{1,0},{2,3},{3,2},{4,5},{5,4},{6,7},{7,6},{8,9},{9,8},{10,11... | collective-permute-start | bytes 393224 | tf_op jit(solution)/shard_map/ppermute | solution.py:319
  7.3 1.0 %collective-permute-done.got_ref = bf16[4,64,256]{2,1,0:T(8,128)(2,1)S(1)} collective-permute-done((bf16[4,64,256]{2,1,0:T(8,128)(2,1)S(1)}, bf16[4,64,256]{2,1,0:T(8,128)(2,1)S(1)}, u32[]{:S(2)}, u32[]{:S(2)}) %collective-permute-start) | collective-permute-done | bytes 131104 | tf_op jit(solution)/shard_map/ppermute | solution.py:319
  8.4 0.0 copy-start.3
  8.4 1.3 %collective-permute-start.2 = (bf16[4,64,256]{2,1,0:T(8,128)(2,1)S(1)}, bf16[4,64,256]{2,1,0:T(8,128)(2,1)S(1)}, u32[]{:S(2)}, u32[]{:S(2)}) collective-permute-start(bf16[4,64,256]{2,1,0:T(8,128)(2,1)S(1)} %combine.1.total_ref), channel_id=1, source_target_pairs={{0,2},{1,3},{2,0},{3,1},{4,6},{5,7},{6,4},{7,5},{8,10},{9,11},{10,... | collective-permute-start | bytes 393224 | tf_op jit(solution)/shard_map/ppermute | solution.py:319
  9.7 1.2 %collective-permute-start.3 = (bf16[4,64,256]{2,1,0:T(8,128)(2,1)S(1)}, bf16[4,64,256]{2,1,0:T(8,128)(2,1)S(1)}, u32[]{:S(2)}, u32[]{:S(2)}) collective-permute-start(bf16[4,64,256]{2,1,0:T(8,128)(2,1)S(1)} %combine.1.total_ref), channel_id=1, source_target_pairs={{0,4},{1,5},{2,6},{3,7},{4,0},{5,1},{6,2},{7,3},{8,12},{9,13},{10,... | collective-permute-start | bytes 393224 | tf_op jit(solution)/shard_map/ppermute | solution.py:319
  10.9 0.2 collective-permute-start.4
  11.1 1.3 %own.1 = (bf16[4,128,512]{2,1,0:T(8,128)(2,1)S(1)}, f32[4,128,512]{2,1,0:T(8,128)S(1)}) custom-call(bf16[4,128,512]{2,1,0:T(8,128)(2,1)S(1)} %copy-done.1, bf16[512,1536]{1,0:T(8,128)(2,1)S(1)} %copy-done, bf16[256,256]{1,0:T(8,128)(2,1)S(1)} %means.1.means_ref, bf16[4,128,512]{2,1,0:T(8,128)(2,1)S(1)} %get-tuple-element.15.k_ref, ...), custom_call_target="tpu_custom_call" | custom-call | flops 1000000 | bytes 1048576 | tf_op jit(solution)/shard_map/own/pallas_call | solution.py:303
  12.4 0.6 %masks.1.mask_ref = f32[3,128,256]{2,1,0:T(8,128)S(1)} custom-call(s32[4,8]{1,0:T(4,128)S(1)} %copy-done.4, s32[4]{0:T(128)S(1)} %copy-done.5, bf16[4,64,256]{2,1,0:T(8,128)(2,1)S(1)} %combine.1.total_ref), custom_call_target="tpu_custom_call" | custom-call | flops 1000000 | bytes 1048576 | tf_op jit(solution)/shard_map/masks/pallas_call | solution.py:303
  13.1 1.4 %near.1.acc_ref = f32[4,128,1024]{2,1,0:T(8,128)S(1)} custom-call(bf16[4,128,512]{2,1,0:T(8,128)(2,1)S(1)} %get-tuple-element.15.k_ref, bf16[4,128,512]{2,1,0:T(8,128)(2,1)S(1)} %get-tuple-element.16.v_ref, bf16[4,128,512]{2,1,0:T(8,128)(2,1)S(1)} %get-tuple-element.19.q_ref, f32[8]{0:T(128)S(1)} %copy-done.3, f32[3,128,256]{2,1,0:T(8,128)S(1)} %masks.1.mask_ref), custom_call_target="tpu_custom_call" | custom-call | flops 1000000 | bytes 1048576 | tf_op jit(solution)/shard_map/near/pallas_call | solution.py:303
  14.5 0.0 collective-permute-done.1.x_ref
  14.5 2.3 %even.1 = (f32[4,128,1024]{2,1,0:T(8,128)S(1)}, f32[4,64,256]{2,1,0:T(8,128)S(1)}) custom-call(bf16[4,128,512]{2,1,0:T(8,128)(2,1)S(1)} %collective-permute-done.1.x_ref, bf16[512,1536]{1,0:T(8,128)(2,1)S(1)} %copy-done, bf16[256,256]{1,0:T(8,128)(2,1)S(1)} %means.1.means_ref, ...), custom_call_target="tpu_custom_call", output_to_operand_aliasing={{1}: (7, {})} | custom-call | flops 1000000 | bytes 1048576 | tf_op jit(solution)/shard_map/even/pallas_call | solution.py:303
  16.8 0.0 collective-permute-done.2.refs_0_
  16.8 0.0 collective-permute-done.3.refs_1_
  16.9 0.0 collective-permute-done.4.refs_2_
  16.9 0.1 carry.1
  17.0 1.6 %collective-permute-start.5 = (bf16[4,64,256]{2,1,0:T(8,128)(2,1)S(1)}, bf16[4,64,256]{2,1,0:T(8,128)(2,1)S(1)}, u32[]{:S(2)}, u32[]{:S(2)}) collective-permute-start(bf16[4,64,256]{2,1,0:T(8,128)(2,1)S(1)} %get-tuple-element.23), channel_id=1, source_target_pairs={{0,1},{1,0},{2,3},{3,2},{4,5},{5,4},{6,7},{7,6},{8,9},{9,8},{10,11... | collective-permute-start | bytes 393224 | tf_op jit(solution)/shard_map/ppermute | solution.py:319
  18.6 0.0 collective-permute-done.6.x_ref
  18.6 2.5 %odd.1.gathered_ref = bf16[4,128,512]{2,1,0:T(8,128)(2,1)S(1)} custom-call(bf16[4,128,512]{2,1,0:T(8,128)(2,1)S(1)} %collective-permute-done.6.x_ref, bf16[512,1536]{1,0:T(8,128)(2,1)S(1)} %copy-done, bf16[256,256]{1,0:T(8,128)(2,1)S(1)} %means.1.means_ref, bf16[4,128,512]{2,1,0:T(8,128)(2,1)S(1)} %get-tuple-element.19.q_ref, f32[8]{0:T(128)S(1)} %copy-done.3, ...), custom_call_target="tpu_custom_call" | custom-call | flops 1000000 | bytes 1048576 | tf_op jit(solution)/shard_map/odd/pallas_call | solution.py:303
  21.1 1.9 %closing.1 = bf16[4,128,512]{2,1,0:T(8,128)(2,1)} custom-call(bf16[4,128,512]{2,1,0:T(8,128)(2,1)S(1)} %get-tuple-element.19.q_ref, f32[4,128,512]{2,1,0:T(8,128)S(1)} %get-tuple-element.20.lin_ref, bf16[4,64,256]{2,1,0:T(8,128)(2,1)S(1)} %get-tuple-element.22.mine_ref, bf16[4,64,256]{2,1,0:T(8,128)(2,1)S(1)} %collective-permute-done.5.other_ref, ...), custom_call_target="tpu_custom_call" | custom-call | flops 1000000 | bytes 1048576 | tf_op jit(solution)/shard_map/closing/pallas_call | solution.py:303
  (12 shorter events, 0.1 us)
Async XLA Ops:
  0.0 4.5 %copy-start.1 = (bf16[4,128,512]{2,1,0:T(8,128)(2,1)S(1)}, bf16[4,128,512]{2,1,0:T(8,128)(2,1)}, u32[]{:S(2)}) copy-start(bf16[4,128,512]{2,1,0:T(8,128)(2,1)} %x_ref.5) | copy-start | bytes 1572868
  0.0 4.6 %copy-start = (bf16[512,1536]{1,0:T(8,128)(2,1)S(1)}, bf16[512,1536]{1,0:T(8,128)(2,1)}, u32[]{:S(2)}) copy-start(bf16[512,1536]{1,0:T(8,128)(2,1)} %w_ref.7) | copy-start | bytes 4718596
  0.0 14.5 %collective-permute-start.1 = (bf16[4,128,512]{2,1,0:T(8,128)(2,1)}, bf16[4,128,512]{2,1,0:T(8,128)(2,1)S(1)}, u32[]{:S(2)}, u32[]{:S(2)}) collective-permute-start(bf16[4,128,512]{2,1,0:T(8,128)(2,1)} %x_ref.5), channel_id=1, source_target_pairs={{0,8},{8,0},{16,24},{24,16},{1,9},{9,1},{17,25},{25,17},{2,10},{10... | collective-permute-start | bytes 1572872 | tf_op jit(solution)/shard_map/ppermute | solution.py:319
  0.0 18.6 %collective-permute-start.6 = (bf16[4,128,512]{2,1,0:T(8,128)(2,1)}, bf16[4,128,512]{2,1,0:T(8,128)(2,1)S(1)}, u32[]{:S(2)}, u32[]{:S(2)}) collective-permute-start(bf16[4,128,512]{2,1,0:T(8,128)(2,1)} %x_ref.5), channel_id=1, source_target_pairs={{8,16},{16,8},{9,17},{17,9},{10,18},{18,10},{11,19},{19,11},{12,20... | collective-permute-start | bytes 1572872 | tf_op jit(solution)/shard_map/ppermute | solution.py:319
  6.0 6.4 %copy-start.4 = (s32[4,8]{1,0:T(4,128)S(1)}, s32[4,8]{1,0:T(4,128)}, u32[]{:S(2)}) copy-start(s32[4,8]{1,0:T(4,128)} %table_ref.1) | copy-start | bytes 388
  6.0 6.4 %copy-start.5 = (s32[4]{0:T(128)S(1)}, s32[4]{0:T(128)}, u32[]{:S(2)}) copy-start(s32[4]{0:T(128)} %tally_ref.1) | copy-start | bytes 52
  6.0 2.3 %collective-permute-start = (bf16[4,64,256]{2,1,0:T(8,128)(2,1)S(1)}, bf16[4,64,256]{2,1,0:T(8,128)(2,1)S(1)}, u32[]{:S(2)}, u32[]{:S(2)}) collective-permute-start(bf16[4,64,256]{2,1,0:T(8,128)(2,1)S(1)} %get-tuple-element.18), channel_id=1, source_target_pairs={{0,1},{1,0},{2,3},{3,2},{4,5},{5,4},{6,7},{7,6},{8,9},{9,8},{10,11... | collective-permute-start | bytes 393224 | tf_op jit(solution)/shard_map/ppermute | solution.py:319
  8.4 4.7 %copy-start.3 = (f32[8]{0:T(128)S(1)}, f32[8]{0:T(128)}, u32[]{:S(2)}) copy-start(f32[8]{0:T(128)} %sharp_ref.5) | copy-start | bytes 100
  8.4 8.5 %collective-permute-start.2 = (bf16[4,64,256]{2,1,0:T(8,128)(2,1)S(1)}, bf16[4,64,256]{2,1,0:T(8,128)(2,1)S(1)}, u32[]{:S(2)}, u32[]{:S(2)}) collective-permute-start(bf16[4,64,256]{2,1,0:T(8,128)(2,1)S(1)} %combine.1.total_ref), channel_id=1, source_target_pairs={{0,2},{1,3},{2,0},{3,1},{4,6},{5,7},{6,4},{7,5},{8,10},{9,11},{10,... | collective-permute-start | bytes 393224 | tf_op jit(solution)/shard_map/ppermute | solution.py:319
  9.7 7.2 %collective-permute-start.3 = (bf16[4,64,256]{2,1,0:T(8,128)(2,1)S(1)}, bf16[4,64,256]{2,1,0:T(8,128)(2,1)S(1)}, u32[]{:S(2)}, u32[]{:S(2)}) collective-permute-start(bf16[4,64,256]{2,1,0:T(8,128)(2,1)S(1)} %combine.1.total_ref), channel_id=1, source_target_pairs={{0,4},{1,5},{2,6},{3,7},{4,0},{5,1},{6,2},{7,3},{8,12},{9,13},{10,... | collective-permute-start | bytes 393224 | tf_op jit(solution)/shard_map/ppermute | solution.py:319
  10.9 6.0 %collective-permute-start.4 = (bf16[4,64,256]{2,1,0:T(8,128)(2,1)S(1)}, bf16[4,64,256]{2,1,0:T(8,128)(2,1)S(1)}, u32[]{:S(2)}, u32[]{:S(2)}) collective-permute-start(bf16[4,64,256]{2,1,0:T(8,128)(2,1)S(1)} %combine.1.total_ref), channel_id=1, source_target_pairs={{0,6},{1,7},{2,4},{3,5},{4,2},{5,3},{6,0},{7,1},{8,14},{9,15},{10,... | collective-permute-start | bytes 393224 | tf_op jit(solution)/shard_map/ppermute | solution.py:319
  17.0 4.1 %collective-permute-start.5 = (bf16[4,64,256]{2,1,0:T(8,128)(2,1)S(1)}, bf16[4,64,256]{2,1,0:T(8,128)(2,1)S(1)}, u32[]{:S(2)}, u32[]{:S(2)}) collective-permute-start(bf16[4,64,256]{2,1,0:T(8,128)(2,1)S(1)} %get-tuple-element.23), channel_id=1, source_target_pairs={{0,1},{1,0},{2,3},{3,2},{4,5},{5,4},{6,7},{7,6},{8,9},{9,8},{10,11... | collective-permute-start | bytes 393224 | tf_op jit(solution)/shard_map/ppermute | solution.py:319
  18.6 2.5 %copy-start.2 = (bf16[1024,512]{1,0:T(8,128)(2,1)S(1)}, bf16[1024,512]{1,0:T(8,128)(2,1)}, u32[]{:S(2)}) copy-start(bf16[1024,512]{1,0:T(8,128)(2,1)} %close_ref.1) | copy-start | bytes 3145732

commit v6 on v5

--- a/solution.py
+++ b/solution.py
@@ -15,7 +15,6 @@
 F32 = jnp.float32
 BF16 = jnp.bfloat16
 VMEM = pltpu.VMEM
-SMEM = pltpu.SMEM
 
 
 def dot(a, b):
@@ -93,26 +92,17 @@
                 held[s][i - s] = stage(*before, *items[i - s])
 
 
-def neighbours(breadth, q_ref, windows, sharp_ref, emit):
+def neighbours(breadth, q_ref, windows, row_ref, emit):
     groups, patches, width = q_ref.shape
     wide = groups * T
-    heads = PAIR // breadth
     ones = stack(jnp.ones((wide, PAIR), BF16), breadth)
-    scale = math.log2(math.e) / math.sqrt(breadth)
-    lane = lax.broadcasted_iota(jnp.int32, (1, heads * wide), 1) // wide
-    sharps = []
-    for u in range(width // PAIR):
-        row = jnp.full((1, heads * wide), sharp_ref[u * heads] * scale, F32)
-        for j in range(1, heads):
-            row = jnp.where(lane == j, sharp_ref[u * heads + j] * scale, row)
-        sharps.append(row)
     sums = {}
 
     def score(u, c, n):
         return dot_nt(cut(q_ref, c, u), stack(cut(windows[n][0], c, u), breadth))
 
     def share(scores, u, c, n):
-        return (jnp.exp2(scores * sharps[u]) * windows[n][2][...]).astype(BF16)
+        return (jnp.exp2(scores * row_ref[u : u + 1, :]) * windows[n][2][...]).astype(BF16)
 
     def gather(shares, u, c, n):
         spread = jnp.concatenate([stack(cut(windows[n][1], c, u), breadth), ones], axis=1)
@@ -127,26 +117,34 @@
     staggered(items, score, share, gather)
 
 
-def masks_kernel(breadth, table_ref, tally_ref, total_ref, mask_ref):
+def masks_kernel(breadth, table_ref, tally_ref, sharp_ref, total_ref, mask_ref, row_ref):
     groups, slots = table_ref.shape
     wide = groups * T
+    heads = PAIR // breadth
+    scale = math.log2(math.e) / math.sqrt(breadth)
+    lane = lax.broadcasted_iota(jnp.int32, (1, heads * wide), 1) // wide
+    for u in range(row_ref.shape[0]):
+        row = jnp.zeros(lane.shape, F32)
+        for j in range(heads):
+            row = jnp.where(lane == j, sharp_ref[:, u * heads + j : u * heads + j + 1], row)
+        row_ref[u : u + 1, :] = row * scale
     station = lax.axis_index("stations")
     around = (station, station ^ 1, station + 2 * (station % 2) - 1)
-    position = lax.broadcasted_iota(jnp.int32, (8, wide), 1) // T
+    position = lax.broadcasted_iota(jnp.int32, (1, wide), 1) // T
     ids = jnp.concatenate([place * groups + position for place in around], axis=1)
     rows = []
     for g in range(groups):
         counts = jnp.zeros(ids.shape, F32)
         for j in range(slots):
-            slot = jnp.where(j < tally_ref[g], table_ref[g, j], -(1 << 20))
+            slot = jnp.where(tally_ref[:, g : g + 1] > j, table_ref[g : g + 1, j : j + 1], -(1 << 20))
             counts += jnp.where(ids == slot, 1.0, 0.0)
-        rows.append(counts[:1])
+        rows.append(counts)
     t_row = lax.broadcasted_iota(jnp.int32, (T, wide), 0)
     t_col = lax.broadcasted_iota(jnp.int32, (T, wide), 1) % T
     for n in range(len(around)):
         for g in range(groups):
             block = jnp.where(t_row == t_col, jnp.broadcast_to(rows[g][:, n * wide : (n + 1) * wide], (T, wide)), 0.0)
-            for j in range(PAIR // breadth):
+            for j in range(heads):
                 mask_ref[n, g * T : (g + 1) * T, j * wide : (j + 1) * wide] = block
 
 
@@ -175,7 +173,7 @@
                 give_ref[g] = states[g].astype(BF16)
 
 
-def own_kernel(breadth, x_ref, w_ref, means_ref, k_ref, v_ref, total_ref, q_ref, lin_ref):
+def own_kernel(breadth, x_ref, w_ref, means_ref, k_ref, v_ref, q_ref, lin_ref):
     groups, patches, width = x_ref.shape
     halves = width // HALF
     means = means_ref[...]
@@ -205,16 +203,16 @@
     staggered([(h, g) for h in range(halves) for g in range(groups)], score, share, gather)
 
 
-def near_kernel(breadth, k_ref, v_ref, q_ref, sharp_ref, mask_ref, acc_ref):
+def near_kernel(breadth, k_ref, v_ref, q_ref, row_ref, mask_ref, acc_ref):
     groups = q_ref.shape[0]
 
     def emit(c, u, total):
         acc_ref[:, c * T : (c + 1) * T, u * 2 * PAIR : (u + 1) * 2 * PAIR] = total.reshape(groups, T, 2 * PAIR)
 
-    neighbours(breadth, q_ref, [(k_ref, v_ref, mask_ref.at[0])], sharp_ref, emit)
-
-
-def even_kernel(breadth, x_ref, w_ref, means_ref, q_ref, sharp_ref, mask_ref, acc_ref, keep_ref, sum_ref, kept_ref, k_ref, v_ref):
+    neighbours(breadth, q_ref, [(k_ref, v_ref, mask_ref.at[0])], row_ref, emit)
+
+
+def even_kernel(breadth, x_ref, w_ref, means_ref, q_ref, row_ref, mask_ref, acc_ref, keep_ref, sum_ref, kept_ref, k_ref, v_ref):
     groups = x_ref.shape[0]
     keys_values(x_ref, w_ref, means_ref, k_ref, v_ref, breadth)
 
@@ -222,10 +220,10 @@
         at = (slice(None), slice(c * T, (c + 1) * T), slice(u * 2 * PAIR, (u + 1) * 2 * PAIR))
         sum_ref[at] = acc_ref[at] + total.reshape(groups, T, 2 * PAIR)
 
-    neighbours(breadth, q_ref, [(k_ref, v_ref, mask_ref.at[1])], sharp_ref, emit)
-
-
-def odd_kernel(breadth, x_ref, w_ref, means_ref, q_ref, sharp_ref, mask_ref, acc_ref, gathered_ref, k_ref, v_ref):
+    neighbours(breadth, q_ref, [(k_ref, v_ref, mask_ref.at[1])], row_ref, emit)
+
+
+def odd_kernel(breadth, x_ref, w_ref, means_ref, q_ref, row_ref, mask_ref, acc_ref, gathered_ref, k_ref, v_ref):
     groups, patches, width = x_ref.shape
     station = lax.axis_index("stations")
     partner = station + 2 * (station % 2) - 1
@@ -247,7 +245,7 @@
         def emit(c, u, total):
             finish(c, u, acc_ref[part(c, u)] + total.reshape(groups, T, 2 * PAIR))
 
-        neighbours(breadth, q_ref, [(k_ref, v_ref, mask_ref.at[2])], sharp_ref, emit)
+        neighbours(breadth, q_ref, [(k_ref, v_ref, mask_ref.at[2])], row_ref, emit)
 
     @pl.when(jnp.logical_not(there))
     def _():
@@ -256,28 +254,39 @@
                 finish(c, u, acc_ref[part(c, u)])
 
 
-def closing_kernel(breadth, q_ref, lin_ref, mine_ref, other_ref, means_ref, close_ref, x_ref, gathered_ref, out_ref):
+def closing_kernel(breadth, q_ref, lin_ref, mine_ref, other_ref, means_ref, close_ref, x_ref, gathered_ref, out_hbm, out_ref, sem):
     groups, patches, width = q_ref.shape
-    rows = groups * patches
     heads = HALF // breadth
-    halves = width // HALF
     core = lax.axis_index("tm") % 2
     means = means_ref[...]
-    mixed = dot(gathered_ref[...].reshape(rows, width), close_ref[width:, :])
-    totals = []
-    for h in range(halves):
-        at = slice(h * HALF, (h + 1) * HALF)
-        for g in range(groups):
+    copies = [pltpu.make_async_copy(out_ref.at[g], out_hbm.at[g], sem.at[g]) for g in range(groups)]
+
+    def totals(g):
+        both = []
+        for h in range(width // HALF):
+            at = slice(h * HALF, (h + 1) * HALF)
             state = jnp.where(core == h, mine_ref[g], other_ref[g])
             block = jnp.where(means > 0, jnp.concatenate([state] * heads, axis=0), jnp.zeros((), BF16))
-            totals.append(lin_ref[g, :, at] + dot(q_ref[g, :, at], block))
-    for h in range(halves):
-        total = jnp.concatenate(totals[h * groups : (h + 1) * groups], axis=0)
-        mixed += dot(head_norm(total, means, 1e-05), close_ref[h * HALF : (h + 1) * HALF, :])
-    out_ref[...] = (x_ref[...].astype(F32) + mixed.reshape(groups, patches, width)).astype(BF16)
-
-
-def combine_kernel(breadth, keep_ref, got_ref, total_ref):
+            both.append(lin_ref[g, :, at] + dot(q_ref[g, :, at], block))
+        return both
+
+    def squares(both, g):
+        return both, [dot((t * t).astype(BF16), means) for t in both]
+
+    def normalize(pair, g):
+        return [(t * lax.rsqrt(m + 1e-05)).astype(BF16) for t, m in zip(*pair)]
+
+    def output(parts, g):
+        mixed = dot(jnp.concatenate(parts + [gathered_ref[g]], axis=1), close_ref[...])
+        out_ref[g] = (x_ref[g].astype(F32) + mixed).astype(BF16)
+        copies[g].start()
+
+    staggered([(g,) for g in range(groups)], totals, squares, normalize, output)
+    for copy in copies:
+        copy.wait()
+
+
+def combine_kernel(breadth, keep_ref, got_ref, q_ref, total_ref):
     total_ref[...] = (keep_ref[...] + got_ref[...].astype(F32)).astype(BF16)
 
 
@@ -291,11 +300,9 @@
     mine_ref[...] = (before + jnp.where(core == 0, 0.0, got_ref[...].astype(F32))).astype(BF16)
 
 
-def call(kernel, breadth, outs, args, scratch=(), flops=10**6, name=None, through=None):
-    def place(a):
-        return pl.BlockSpec(memory_space=SMEM if a.size <= 64 else VMEM)
-
-    in_specs, out_specs = [place(a) for a in args], [pl.BlockSpec(memory_space=VMEM) for _ in outs]
+def call(kernel, breadth, outs, args, scratch=(), flops=10**6, name=None, through=None, space=VMEM):
+    in_specs = [pl.BlockSpec(memory_space=VMEM) for _ in args]
+    out_specs = [pl.BlockSpec(memory_space=space) for _ in outs]
     for i, o in (through or {}).items():
         in_specs[i] = pl.BlockSpec(memory_space=pl.ANY)
         if o is not None:
@@ -305,7 +312,7 @@
         out_shape=[jax.ShapeDtypeStruct(s, d) for s, d in outs],
         in_specs=in_specs,
         out_specs=out_specs,
-        scratch_shapes=[pltpu.VMEM(s, d) for s, d in scratch],
+        scratch_shapes=[pltpu.VMEM(*s) if isinstance(s, tuple) else s for s in scratch],
         input_output_aliases={i: o for i, o in (through or {}).items() if o is not None},
         compiler_params=pltpu.CompilerParams(vmem_limit_bytes=10 * 2**20),
         cost_estimate=pl.CostEstimate(flops=flops, bytes_accessed=2**20, transcendentals=0),
@@ -334,30 +341,29 @@
         states_kernel, breadth, [(block, BF16)] * 2 + [(part, F32), (part, BF16)], (x, w, means), name="states"
     )
     got = swap_with(give, "tm", lambda i: i ^ 1)
-    (total,) = call(combine_kernel, breadth, [(part, BF16)], (keep, got), name="combine")
-    pieces = [swap_with(total, "tm", lambda i: i ^ (2 * m)) for m in range(1, chips)]
     q, lin = call(
         own_kernel,
         breadth,
         [(block, BF16), (block, F32)],
-        (x, w, means, k, v, total),
+        (x, w, means, k, v),
         name="own",
-        through={5: None},
-    )
-    (masks,) = call(
+    )
+    (total,) = call(combine_kernel, breadth, [(part, BF16)], (keep, got, q), name="combine", through={2: None})
+    pieces = [swap_with(total, "tm", lambda i: i ^ (2 * m)) for m in range(1, chips)]
+    masks, rows = call(
         masks_kernel,
         breadth,
-        [((3, wide, wide * PAIR // breadth), F32)],
-        (table, tally, total),
+        [((3, wide, wide * PAIR // breadth), F32), ((width // PAIR, wide * PAIR // breadth), F32)],
+        (table, tally.reshape(1, -1), sharp.reshape(1, -1), total),
         name="masks",
-        through={2: None},
-    )
-    (acc,) = call(near_kernel, breadth, [(sums, F32)], (k, v, q, sharp, masks), name="near")
+        through={3: None},
+    )
+    (acc,) = call(near_kernel, breadth, [(sums, F32)], (k, v, q, rows, masks), name="near")
     acc, keep = call(
         even_kernel,
         breadth,
         [(sums, F32), (part, F32)],
-        (x_even, w, means, q, sharp, masks, acc, keep),
+        (x_even, w, means, q, rows, masks, acc, keep),
         [(block, BF16)] * 2,
         name="even",
         through={7: 1},
@@ -368,12 +374,18 @@
         odd_kernel,
         breadth,
         [(block, BF16)],
-        (x_odd, w, means, q, sharp, masks, acc),
+        (x_odd, w, means, q, rows, masks, acc),
         [(block, BF16)] * 2,
         name="odd",
     )
     (out,) = call(
-        closing_kernel, breadth, [(block, BF16)], (q, lin, mine, other, means, close, x, gathered), name="closing"
+        closing_kernel,
+        breadth,
+        [(block, BF16)],
+        (q, lin, mine, other, means, close, x, gathered),
+        [(block, BF16), pltpu.SemaphoreType.DMA((groups,))],
+        name="closing",
+        space=pl.ANY,
     )
     return out
 

time: 23.2 us -> 22.9 us (0.987)
  Pallas kernels: 11.8 us -> 9.66 us
  waiting for transfers between devices: 1 us -> 3.13 us
  starting transfers between devices: 10.1 us -> 9.83 us
    ppermute x7, waiting for transfers between devices: 1 us -> 3.13 us  [swap_with(): return lax.ppermute(value, axis, pairs)]
    pallas_call x10, Pallas kernels: 11.8 us -> 9.66 us  [call(): pl.pallas_call(functools.partial(kernel, breadth), out_shape=[jax.ShapeDt...]
    ppermute x7, starting transfers between devices: 10.1 us -> 9.83 us  [swap_with(): return lax.ppermute(value, axis, pairs)]
  transfers between devices with their start and end apart: 7 -> 7, of which waited for: 1 -> 3; matrix products, arithmetic and copies ran while one was open for 0% -> 0% of each run, Pallas kernels for 43% -> 34%
where the time goes in v6:
time: 22.9 us; the launch traced here: 22.8 us
  starting transfers between devices  9.83 us (43%)
  Pallas kernels  9.66 us (42%)
  waiting for transfers between devices  3.13 us (14%)
    ppermute x7, starting transfers between devices, swap_with(): return lax.ppermute(value, axis, pairs)  9.83 us
    pallas_call x10, Pallas kernels, call(): pl.pallas_call(functools.partial(kernel, breadth), out_shape=[jax.ShapeDt...  9.66 us
    ppermute x7, waiting for transfers between devices, swap_with(): return lax.ppermute(value, axis, pairs)  3.13 us
  transfers between devices with their start and end apart: 7, of which 3 were waited for; matrix products, arithmetic and copies ran while one was open for 0% of the time, Pallas kernels for 34%

profile of v6, /device:TPU:9, one launch (start us, length us, event | category | flops | bytes accessed | tf_op | source)
XLA Modules:
  0.0 22.8 jit_solution(15461623596131507091)
XLA Ops:
  0.0 0.0 collective-permute-start
  0.0 4.5 %collective-permute-start.6 = (bf16[4,128,512]{2,1,0:T(8,128)(2,1)}, bf16[4,128,512]{2,1,0:T(8,128)(2,1)S(1)}, u32[]{:S(2)}, u32[]{:S(2)}) collective-permute-start(bf16[4,128,512]{2,1,0:T(8,128)(2,1)} %x_ref.5), channel_id=1, source_target_pairs={{8,16},{16,8},{9,17},{17,9},{10,18},{18,10},{11,19},{19,11},{12,20... | collective-permute-start | bytes 1572872 | tf_op jit(solution)/shard_map/ppermute | solution.py:326
  4.5 0.0 copy-done.1
  4.6 1.5 %states.1 = (bf16[4,128,512]{2,1,0:T(8,128)(2,1)S(1)}, bf16[4,128,512]{2,1,0:T(8,128)(2,1)S(1)}, f32[4,64,256]{2,1,0:T(8,128)S(1)}, bf16[4,64,256]{2,1,0:T(8,128)(2,1)S(1)}) custom-call(bf16[4,128,512]{2,1,0:T(8,128)(2,1)S(1)} %copy-done.1, bf16[512,1536]{1,0:T(8,128)(2,1)S(1)} %copy-done, bf16[256,256]{1,0:T(8,128)(2,1)S(1)} %means.1.means_ref), custom_call_target="tpu_custom_call" | custom-call | flops 1000000 | bytes 1048576 | tf_op jit(solution)/shard_map/states/pallas_call | solution.py:310
  6.0 1.3 %collective-permute-start.1 = (bf16[4,64,256]{2,1,0:T(8,128)(2,1)S(1)}, bf16[4,64,256]{2,1,0:T(8,128)(2,1)S(1)}, u32[]{:S(2)}, u32[]{:S(2)}) collective-permute-start(bf16[4,64,256]{2,1,0:T(8,128)(2,1)S(1)} %get-tuple-element.22), channel_id=1, source_target_pairs={{0,1},{1,0},{2,3},{3,2},{4,5},{5,4},{6,7},{7,6},{8,9},{9,8},{10,11... | collective-permute-start | bytes 393224 | tf_op jit(solution)/shard_map/ppermute | solution.py:326
  7.3 1.3 %own.1 = (bf16[4,128,512]{2,1,0:T(8,128)(2,1)S(1)}, f32[4,128,512]{2,1,0:T(8,128)S(1)}) custom-call(bf16[4,128,512]{2,1,0:T(8,128)(2,1)S(1)} %copy-done.1, bf16[512,1536]{1,0:T(8,128)(2,1)S(1)} %copy-done, bf16[256,256]{1,0:T(8,128)(2,1)S(1)} %means.1.means_ref, bf16[4,128,512]{2,1,0:T(8,128)(2,1)S(1)} %get-tuple-element.17.k_ref, ...), custom_call_target="tpu_custom_call" | custom-call | flops 1000000 | bytes 1048576 | tf_op jit(solution)/shard_map/own/pallas_call | solution.py:310
  8.7 0.0 collective-permute-done.1.got_ref
  8.7 1.3 %collective-permute-start.2 = (bf16[4,64,256]{2,1,0:T(8,128)(2,1)S(1)}, bf16[4,64,256]{2,1,0:T(8,128)(2,1)S(1)}, u32[]{:S(2)}, u32[]{:S(2)}) collective-permute-start(bf16[4,64,256]{2,1,0:T(8,128)(2,1)S(1)} %combine.1.total_ref), channel_id=1, source_target_pairs={{0,2},{1,3},{2,0},{3,1},{4,6},{5,7},{6,4},{7,5},{8,10},{9,11},{10,... | collective-permute-start | bytes 393224 | tf_op jit(solution)/shard_map/ppermute | solution.py:326
  10.0 1.2 %collective-permute-start.3 = (bf16[4,64,256]{2,1,0:T(8,128)(2,1)S(1)}, bf16[4,64,256]{2,1,0:T(8,128)(2,1)S(1)}, u32[]{:S(2)}, u32[]{:S(2)}) collective-permute-start(bf16[4,64,256]{2,1,0:T(8,128)(2,1)S(1)} %combine.1.total_ref), channel_id=1, source_target_pairs={{0,4},{1,5},{2,6},{3,7},{4,0},{5,1},{6,2},{7,3},{8,12},{9,13},{10,... | collective-permute-start | bytes 393224 | tf_op jit(solution)/shard_map/ppermute | solution.py:326
  11.2 0.2 collective-permute-start.4
  11.4 0.0 copy-done.4
  11.4 0.2 masks.1
  11.7 0.9 %near.1.acc_ref = f32[4,128,1024]{2,1,0:T(8,128)S(1)} custom-call(bf16[4,128,512]{2,1,0:T(8,128)(2,1)S(1)} %get-tuple-element.17.k_ref, bf16[4,128,512]{2,1,0:T(8,128)(2,1)S(1)} %get-tuple-element.18.v_ref, bf16[4,128,512]{2,1,0:T(8,128)(2,1)S(1)} %get-tuple-element.19.q_ref, f32[4,256]{1,0:T(4,128)S(1)} %get-tuple-element.23.row_ref, ...), custom_call_target="tpu_custom_call" | custom-call | flops 1000000 | bytes 1048576 | tf_op jit(solution)/shard_map/near/pallas_call | solution.py:310
  12.5 0.5 %collective-permute-done.x_ref = bf16[4,128,512]{2,1,0:T(8,128)(2,1)S(1)} collective-permute-done((bf16[4,128,512]{2,1,0:T(8,128)(2,1)}, bf16[4,128,512]{2,1,0:T(8,128)(2,1)S(1)}, u32[]{:S(2)}, u32[]{:S(2)}) %collective-permute-start) | collective-permute-done | bytes 524320 | tf_op jit(solution)/shard_map/ppermute | solution.py:326
  13.0 1.8 %even.1 = (f32[4,128,1024]{2,1,0:T(8,128)S(1)}, f32[4,64,256]{2,1,0:T(8,128)S(1)}) custom-call(bf16[4,128,512]{2,1,0:T(8,128)(2,1)S(1)} %collective-permute-done.x_ref, bf16[512,1536]{1,0:T(8,128)(2,1)S(1)} %copy-done, bf16[256,256]{1,0:T(8,128)(2,1)S(1)} %means.1.means_ref, ...), custom_call_target="tpu_custom_call", output_to_operand_aliasing={{1}: (7, {})} | custom-call | flops 1000000 | bytes 1048576 | tf_op jit(solution)/shard_map/even/pallas_call | solution.py:310
  14.8 0.0 collective-permute-done.2.refs_0_
  14.8 1.6 %collective-permute-done.3.refs_1_ = bf16[4,64,256]{2,1,0:T(8,128)(2,1)S(1)} collective-permute-done((bf16[4,64,256]{2,1,0:T(8,128)(2,1)S(1)}, bf16[4,64,256]{2,1,0:T(8,128)(2,1)S(1)}, u32[]{:S(2)}, u32[]{:S(2)}) %collective-permute-start.3) | collective-permute-done | bytes 131104 | tf_op jit(solution)/shard_map/ppermute | solution.py:326
  16.4 1.0 %collective-permute-done.4.refs_2_ = bf16[4,64,256]{2,1,0:T(8,128)(2,1)S(1)} collective-permute-done((bf16[4,64,256]{2,1,0:T(8,128)(2,1)S(1)}, bf16[4,64,256]{2,1,0:T(8,128)(2,1)S(1)}, u32[]{:S(2)}, u32[]{:S(2)}) %collective-permute-start.4) | collective-permute-done | bytes 131104 | tf_op jit(solution)/shard_map/ppermute | solution.py:326
  17.4 0.1 carry.1
  17.6 1.3 %collective-permute-start.5 = (bf16[4,64,256]{2,1,0:T(8,128)(2,1)S(1)}, bf16[4,64,256]{2,1,0:T(8,128)(2,1)S(1)}, u32[]{:S(2)}, u32[]{:S(2)}) collective-permute-start(bf16[4,64,256]{2,1,0:T(8,128)(2,1)S(1)} %get-tuple-element.27), channel_id=1, source_target_pairs={{0,1},{1,0},{2,3},{3,2},{4,5},{5,4},{6,7},{7,6},{8,9},{9,8},{10,11... | collective-permute-start | bytes 393224 | tf_op jit(solution)/shard_map/ppermute | solution.py:326
  18.9 0.0 collective-permute-done.6.x_ref
  18.9 1.9 %odd.1.gathered_ref = bf16[4,128,512]{2,1,0:T(8,128)(2,1)S(1)} custom-call(bf16[4,128,512]{2,1,0:T(8,128)(2,1)S(1)} %collective-permute-done.6.x_ref, bf16[512,1536]{1,0:T(8,128)(2,1)S(1)} %copy-done, bf16[256,256]{1,0:T(8,128)(2,1)S(1)} %means.1.means_ref, bf16[4,128,512]{2,1,0:T(8,128)(2,1)S(1)} %get-tuple-element.19.q_ref, ...), custom_call_target="tpu_custom_call" | custom-call | flops 1000000 | bytes 1048576 | tf_op jit(solution)/shard_map/odd/pallas_call | solution.py:310
  20.9 0.0 collective-permute-done.5.other_ref
  20.9 1.9 %closing.1 = bf16[4,128,512]{2,1,0:T(8,128)(2,1)} custom-call(bf16[4,128,512]{2,1,0:T(8,128)(2,1)S(1)} %get-tuple-element.19.q_ref, f32[4,128,512]{2,1,0:T(8,128)S(1)} %get-tuple-element.20.lin_ref, bf16[4,64,256]{2,1,0:T(8,128)(2,1)S(1)} %get-tuple-element.26.mine_ref, bf16[4,64,256]{2,1,0:T(8,128)(2,1)S(1)} %collective-permute-done.5.other_ref, ...), custom_call_target="tpu_custom_call" | custom-call | flops 1000000 | bytes 1048576 | tf_op jit(solution)/shard_map/closing/pallas_call | solution.py:310
  (12 shorter events, 0.1 us)
Async XLA Ops:
  0.0 4.5 %copy-start.1 = (bf16[4,128,512]{2,1,0:T(8,128)(2,1)S(1)}, bf16[4,128,512]{2,1,0:T(8,128)(2,1)}, u32[]{:S(2)}) copy-start(bf16[4,128,512]{2,1,0:T(8,128)(2,1)} %x_ref.5) | copy-start | bytes 1572868
  0.0 4.6 %copy-start = (bf16[512,1536]{1,0:T(8,128)(2,1)S(1)}, bf16[512,1536]{1,0:T(8,128)(2,1)}, u32[]{:S(2)}) copy-start(bf16[512,1536]{1,0:T(8,128)(2,1)} %w_ref.7) | copy-start | bytes 4718596
  0.0 13.0 %collective-permute-start = (bf16[4,128,512]{2,1,0:T(8,128)(2,1)}, bf16[4,128,512]{2,1,0:T(8,128)(2,1)S(1)}, u32[]{:S(2)}, u32[]{:S(2)}) collective-permute-start(bf16[4,128,512]{2,1,0:T(8,128)(2,1)} %x_ref.5), channel_id=1, source_target_pairs={{0,8},{8,0},{16,24},{24,16},{1,9},{9,1},{17,25},{25,17},{2,10},{10... | collective-permute-start | bytes 1572872 | tf_op jit(solution)/shard_map/ppermute | solution.py:326
  0.0 18.9 %collective-permute-start.6 = (bf16[4,128,512]{2,1,0:T(8,128)(2,1)}, bf16[4,128,512]{2,1,0:T(8,128)(2,1)S(1)}, u32[]{:S(2)}, u32[]{:S(2)}) collective-permute-start(bf16[4,128,512]{2,1,0:T(8,128)(2,1)} %x_ref.5), channel_id=1, source_target_pairs={{8,16},{16,8},{9,17},{17,9},{10,18},{18,10},{11,19},{19,11},{12,20... | collective-permute-start | bytes 1572872 | tf_op jit(solution)/shard_map/ppermute | solution.py:326
  6.0 2.6 %collective-permute-start.1 = (bf16[4,64,256]{2,1,0:T(8,128)(2,1)S(1)}, bf16[4,64,256]{2,1,0:T(8,128)(2,1)S(1)}, u32[]{:S(2)}, u32[]{:S(2)}) collective-permute-start(bf16[4,64,256]{2,1,0:T(8,128)(2,1)S(1)} %get-tuple-element.22), channel_id=1, source_target_pairs={{0,1},{1,0},{2,3},{3,2},{4,5},{5,4},{6,7},{7,6},{8,9},{9,8},{10,11... | collective-permute-start | bytes 393224 | tf_op jit(solution)/shard_map/ppermute | solution.py:326
  7.3 4.1 %copy-start.3 = (s32[4,8]{1,0:T(4,128)S(1)}, s32[4,8]{1,0:T(4,128)}, u32[]{:S(2)}) copy-start(s32[4,8]{1,0:T(4,128)} %table_ref.1) | copy-start | bytes 388
  7.3 4.1 %copy-start.4 = (s32[4]{0:T(128)S(1)}, s32[4]{0:T(128)}, u32[]{:S(2)}) copy-start(s32[4]{0:T(128)} %param.11) | copy-start | bytes 52
  7.3 4.1 %copy-start.5 = (f32[8]{0:T(128)S(1)}, f32[8]{0:T(128)}, u32[]{:S(2)}) copy-start(f32[8]{0:T(128)} %param.9) | copy-start | bytes 100
  8.7 6.1 %collective-permute-start.2 = (bf16[4,64,256]{2,1,0:T(8,128)(2,1)S(1)}, bf16[4,64,256]{2,1,0:T(8,128)(2,1)S(1)}, u32[]{:S(2)}, u32[]{:S(2)}) collective-permute-start(bf16[4,64,256]{2,1,0:T(8,128)(2,1)S(1)} %combine.1.total_ref), channel_id=1, source_target_pairs={{0,2},{1,3},{2,0},{3,1},{4,6},{5,7},{6,4},{7,5},{8,10},{9,11},{10,... | collective-permute-start | bytes 393224 | tf_op jit(solution)/shard_map/ppermute | solution.py:326
  10.0 6.5 %collective-permute-start.3 = (bf16[4,64,256]{2,1,0:T(8,128)(2,1)S(1)}, bf16[4,64,256]{2,1,0:T(8,128)(2,1)S(1)}, u32[]{:S(2)}, u32[]{:S(2)}) collective-permute-start(bf16[4,64,256]{2,1,0:T(8,128)(2,1)S(1)} %combine.1.total_ref), channel_id=1, source_target_pairs={{0,4},{1,5},{2,6},{3,7},{4,0},{5,1},{6,2},{7,3},{8,12},{9,13},{10,... | collective-permute-start | bytes 393224 | tf_op jit(solution)/shard_map/ppermute | solution.py:326
  11.2 6.2 %collective-permute-start.4 = (bf16[4,64,256]{2,1,0:T(8,128)(2,1)S(1)}, bf16[4,64,256]{2,1,0:T(8,128)(2,1)S(1)}, u32[]{:S(2)}, u32[]{:S(2)}) collective-permute-start(bf16[4,64,256]{2,1,0:T(8,128)(2,1)S(1)} %combine.1.total_ref), channel_id=1, source_target_pairs={{0,6},{1,7},{2,4},{3,5},{4,2},{5,3},{6,0},{7,1},{8,14},{9,15},{10,... | collective-permute-start | bytes 393224 | tf_op jit(solution)/shard_map/ppermute | solution.py:326
  17.6 3.3 %collective-permute-start.5 = (bf16[4,64,256]{2,1,0:T(8,128)(2,1)S(1)}, bf16[4,64,256]{2,1,0:T(8,128)(2,1)S(1)}, u32[]{:S(2)}, u32[]{:S(2)}) collective-permute-start(bf16[4,64,256]{2,1,0:T(8,128)(2,1)S(1)} %get-tuple-element.27), channel_id=1, source_target_pairs={{0,1},{1,0},{2,3},{3,2},{4,5},{5,4},{6,7},{7,6},{8,9},{9,8},{10,11... | collective-permute-start | bytes 393224 | tf_op jit(solution)/shard_map/ppermute | solution.py:326
  18.9 2.0 %copy-start.2 = (bf16[1024,512]{1,0:T(8,128)(2,1)S(1)}, bf16[1024,512]{1,0:T(8,128)(2,1)}, u32[]{:S(2)}) copy-start(bf16[1024,512]{1,0:T(8,128)(2,1)} %close_ref.1) | copy-start | bytes 3145732

commit v7 on v6

--- a/solution.py
+++ b/solution.py
@@ -173,7 +173,7 @@
                 give_ref[g] = states[g].astype(BF16)
 
 
-def own_kernel(breadth, x_ref, w_ref, means_ref, k_ref, v_ref, q_ref, lin_ref):
+def own_kernel(breadth, x_ref, w_ref, means_ref, k_ref, v_ref, total_ref, q_ref, lin_ref):
     groups, patches, width = x_ref.shape
     halves = width // HALF
     means = means_ref[...]
@@ -223,11 +223,21 @@
     neighbours(breadth, q_ref, [(k_ref, v_ref, mask_ref.at[1])], row_ref, emit)
 
 
-def odd_kernel(breadth, x_ref, w_ref, means_ref, q_ref, row_ref, mask_ref, acc_ref, gathered_ref, k_ref, v_ref):
-    groups, patches, width = x_ref.shape
+def odd_partner():
     station = lax.axis_index("stations")
     partner = station + 2 * (station % 2) - 1
-    there = (partner >= 0) & (partner < lax.axis_size("stations"))
+    return (partner >= 0) & (partner < lax.axis_size("stations"))
+
+
+def odd_keys_kernel(breadth, x_ref, w_ref, means_ref, keep_ref, k_ref, v_ref, kept_ref):
+    @pl.when(odd_partner())
+    def _():
+        keys_values(x_ref, w_ref, means_ref, k_ref, v_ref, breadth)
+
+
+def odd_kernel(breadth, k_ref, v_ref, q_ref, row_ref, mask_ref, acc_ref, gathered_ref):
+    groups, patches, width = q_ref.shape
+    there = odd_partner()
 
     def part(c, u):
         return (slice(None), slice(c * T, (c + 1) * T), slice(u * 2 * PAIR, (u + 1) * 2 * PAIR))
@@ -240,8 +250,6 @@
 
     @pl.when(there)
     def _():
-        keys_values(x_ref, w_ref, means_ref, k_ref, v_ref, breadth)
-
         def emit(c, u, total):
             finish(c, u, acc_ref[part(c, u)] + total.reshape(groups, T, 2 * PAIR))
 
@@ -286,7 +294,7 @@
         copy.wait()
 
 
-def combine_kernel(breadth, keep_ref, got_ref, q_ref, total_ref):
+def combine_kernel(breadth, keep_ref, got_ref, total_ref):
     total_ref[...] = (keep_ref[...] + got_ref[...].astype(F32)).astype(BF16)
 
 
@@ -315,7 +323,7 @@
         scratch_shapes=[pltpu.VMEM(*s) if isinstance(s, tuple) else s for s in scratch],
         input_output_aliases={i: o for i, o in (through or {}).items() if o is not None},
         compiler_params=pltpu.CompilerParams(vmem_limit_bytes=10 * 2**20),
-        cost_estimate=pl.CostEstimate(flops=flops, bytes_accessed=2**20, transcendentals=0),
+        cost_estimate=pl.CostEstimate(flops=flops, bytes_accessed=2**12, transcendentals=0),
         name=name,
     )(*args)
 
@@ -341,15 +349,16 @@
         states_kernel, breadth, [(block, BF16)] * 2 + [(part, F32), (part, BF16)], (x, w, means), name="states"
     )
     got = swap_with(give, "tm", lambda i: i ^ 1)
+    (total,) = call(combine_kernel, breadth, [(part, BF16)], (keep, got), name="combine")
+    pieces = [swap_with(total, "tm", lambda i: i ^ (2 * m)) for m in range(1, chips)]
     q, lin = call(
         own_kernel,
         breadth,
         [(block, BF16), (block, F32)],
-        (x, w, means, k, v),
+        (x, w, means, k, v, total),
         name="own",
-    )
-    (total,) = call(combine_kernel, breadth, [(part, BF16)], (keep, got, q), name="combine", through={2: None})
-    pieces = [swap_with(total, "tm", lambda i: i ^ (2 * m)) for m in range(1, chips)]
+        through={5: None},
+    )
     masks, rows = call(
         masks_kernel,
         breadth,
@@ -368,16 +377,17 @@
         name="even",
         through={7: 1},
     )
+    k_odd, v_odd, keep = call(
+        odd_keys_kernel,
+        breadth,
+        [(block, BF16)] * 2 + [(part, F32)],
+        (x_odd, w, means, keep),
+        name="keys",
+        through={3: 2},
+    )
     send, mine = call(carry_kernel, breadth, [(part, BF16)] * 2, (keep, got, *pieces), name="carry")
     other = swap_with(send, "tm", lambda i: i ^ 1)
-    (gathered,) = call(
-        odd_kernel,
-        breadth,
-        [(block, BF16)],
-        (x_odd, w, means, q, rows, masks, acc),
-        [(block, BF16)] * 2,
-        name="odd",
-    )
+    (gathered,) = call(odd_kernel, breadth, [(block, BF16)], (k_odd, v_odd, q, rows, masks, acc), name="odd")
     (out,) = call(
         closing_kernel,
         breadth,

time: 22.9 us -> 22.1 us (0.965)
  waiting for transfers between devices: 3.13 us -> 1.72 us
  starting transfers between devices: 9.83 us -> 10.1 us
    ppermute x7, waiting for transfers between devices: 3.13 us -> 1.72 us  [swap_with(): return lax.ppermute(value, axis, pairs)]
    ppermute x7, starting transfers between devices: 9.83 us -> 10.1 us  [swap_with(): return lax.ppermute(value, axis, pairs)]
    pallas_call x10 -> x11, Pallas kernels: 9.66 us -> 9.62 us  [call(): pl.pallas_call(functools.partial(kernel, breadth), out_shape=[jax.ShapeDt...]
  transfers between devices with their start and end apart: 7 -> 7, of which waited for: 3 -> 2; matrix products, arithmetic and copies ran while one was open for 0% -> 0% of each run, Pallas kernels for 34% -> 35%
where the time goes in v7:
time: 22.1 us; the launch traced here: 21.8 us
  starting transfers between devices  10.1 us (46%)
  Pallas kernels  9.62 us (44%)
  waiting for transfers between devices  1.72 us (8%)
    ppermute x7, starting transfers between devices, swap_with(): return lax.ppermute(value, axis, pairs)  10.1 us
    pallas_call x11, Pallas kernels, call(): pl.pallas_call(functools.partial(kernel, breadth), out_shape=[jax.ShapeDt...  9.62 us
    ppermute x7, waiting for transfers between devices, swap_with(): return lax.ppermute(value, axis, pairs)  1.72 us
  transfers between devices with their start and end apart: 7, of which 2 were waited for; matrix products, arithmetic and copies ran while one was open for 0% of the time, Pallas kernels for 35%

profile of v7, /device:TPU:9, one launch (start us, length us, event | category | flops | bytes accessed | tf_op | source)
XLA Modules:
  0.0 21.8 jit_solution(5484759583137759444)
XLA Ops:
  0.0 0.0 collective-permute-start.2
  0.0 4.5 %collective-permute-start.1 = (bf16[4,128,512]{2,1,0:T(8,128)(2,1)}, bf16[4,128,512]{2,1,0:T(8,128)(2,1)S(1)}, u32[]{:S(2)}, u32[]{:S(2)}) collective-permute-start(bf16[4,128,512]{2,1,0:T(8,128)(2,1)} %x_ref.5), channel_id=1, source_target_pairs={{8,16},{16,8},{9,17},{17,9},{10,18},{18,10},{11,19},{19,11},{12,20... | collective-permute-start | bytes 1572872 | tf_op jit(solution)/shard_map/ppermute | solution.py:334
  4.6 1.4 %states.1 = (bf16[4,128,512]{2,1,0:T(8,128)(2,1)S(1)}, bf16[4,128,512]{2,1,0:T(8,128)(2,1)S(1)}, f32[4,64,256]{2,1,0:T(8,128)S(1)}, bf16[4,64,256]{2,1,0:T(8,128)(2,1)S(1)}) custom-call(bf16[4,128,512]{2,1,0:T(8,128)(2,1)S(1)} %copy-done.1, bf16[512,1536]{1,0:T(8,128)(2,1)S(1)} %copy-done, bf16[256,256]{1,0:T(8,128)(2,1)S(1)} %means.1.means_ref), custom_call_target="tpu_custom_call" | custom-call | flops 1000000 | bytes 4096 | tf_op jit(solution)/shard_map/states/pallas_call | solution.py:318
  6.0 0.0 copy-start.3
  6.0 0.0 copy-start.4
  6.0 0.0 copy-start.5
  6.1 1.3 %collective-permute-start = (bf16[4,64,256]{2,1,0:T(8,128)(2,1)S(1)}, bf16[4,64,256]{2,1,0:T(8,128)(2,1)S(1)}, u32[]{:S(2)}, u32[]{:S(2)}) collective-permute-start(bf16[4,64,256]{2,1,0:T(8,128)(2,1)S(1)} %get-tuple-element.23), channel_id=1, source_target_pairs={{0,1},{1,0},{2,3},{3,2},{4,5},{5,4},{6,7},{7,6},{8,9},{9,8},{10,11... | collective-permute-start | bytes 393224 | tf_op jit(solution)/shard_map/ppermute | solution.py:334
  7.4 1.0 %collective-permute-done.got_ref = bf16[4,64,256]{2,1,0:T(8,128)(2,1)S(1)} collective-permute-done((bf16[4,64,256]{2,1,0:T(8,128)(2,1)S(1)}, bf16[4,64,256]{2,1,0:T(8,128)(2,1)S(1)}, u32[]{:S(2)}, u32[]{:S(2)}) %collective-permute-start) | collective-permute-done | bytes 131104 | tf_op jit(solution)/shard_map/ppermute | solution.py:334
  8.4 1.3 %collective-permute-start.3 = (bf16[4,64,256]{2,1,0:T(8,128)(2,1)S(1)}, bf16[4,64,256]{2,1,0:T(8,128)(2,1)S(1)}, u32[]{:S(2)}, u32[]{:S(2)}) collective-permute-start(bf16[4,64,256]{2,1,0:T(8,128)(2,1)S(1)} %combine.1.total_ref), channel_id=1, source_target_pairs={{0,2},{1,3},{2,0},{3,1},{4,6},{5,7},{6,4},{7,5},{8,10},{9,11},{10,... | collective-permute-start | bytes 393224 | tf_op jit(solution)/shard_map/ppermute | solution.py:334
  9.6 1.2 %collective-permute-start.4 = (bf16[4,64,256]{2,1,0:T(8,128)(2,1)S(1)}, bf16[4,64,256]{2,1,0:T(8,128)(2,1)S(1)}, u32[]{:S(2)}, u32[]{:S(2)}) collective-permute-start(bf16[4,64,256]{2,1,0:T(8,128)(2,1)S(1)} %combine.1.total_ref), channel_id=1, source_target_pairs={{0,4},{1,5},{2,6},{3,7},{4,0},{5,1},{6,2},{7,3},{8,12},{9,13},{10,... | collective-permute-start | bytes 393224 | tf_op jit(solution)/shard_map/ppermute | solution.py:334
  10.9 0.2 collective-permute-start.5
  11.1 1.3 %own.1 = (bf16[4,128,512]{2,1,0:T(8,128)(2,1)S(1)}, f32[4,128,512]{2,1,0:T(8,128)S(1)}) custom-call(bf16[4,128,512]{2,1,0:T(8,128)(2,1)S(1)} %copy-done.1, bf16[512,1536]{1,0:T(8,128)(2,1)S(1)} %copy-done, bf16[256,256]{1,0:T(8,128)(2,1)S(1)} %means.1.means_ref, bf16[4,128,512]{2,1,0:T(8,128)(2,1)S(1)} %get-tuple-element.20.k_ref, ...), custom_call_target="tpu_custom_call" | custom-call | flops 1000000 | bytes 4096 | tf_op jit(solution)/shard_map/own/pallas_call | solution.py:318
  12.4 0.2 %masks.1 = (f32[3,128,256]{2,1,0:T(8,128)S(1)}, f32[4,256]{1,0:T(4,128)S(1)}) custom-call(s32[4,8]{1,0:T(4,128)S(1)} %copy-done.3, s32[1,4]{1,0:T(1,128)S(1)} %bitcast.2, f32[1,8]{1,0:T(1,128)S(1)} %bitcast.3, bf16[4,64,256]{2,1,0:T(8,128)(2,1)S(1)} %combine.1.total_ref), custom_call_target="tpu_custom_call" | custom-call | flops 1000000 | bytes 4096 | tf_op jit(solution)/shard_map/masks/pallas_call | solution.py:318
  12.7 0.8 %near.1.acc_ref = f32[4,128,1024]{2,1,0:T(8,128)S(1)} custom-call(bf16[4,128,512]{2,1,0:T(8,128)(2,1)S(1)} %get-tuple-element.20.k_ref, bf16[4,128,512]{2,1,0:T(8,128)(2,1)S(1)} %get-tuple-element.21.v_ref, bf16[4,128,512]{2,1,0:T(8,128)(2,1)S(1)} %get-tuple-element.24.q_ref, f32[4,256]{1,0:T(4,128)S(1)} %get-tuple-element.26.row_ref, ...), custom_call_target="tpu_custom_call" | custom-call | flops 1000000 | bytes 4096 | tf_op jit(solution)/shard_map/near/pallas_call | solution.py:318
  13.5 0.0 collective-permute-done.2.x_ref
  13.5 1.8 %even.1 = (f32[4,128,1024]{2,1,0:T(8,128)S(1)}, f32[4,64,256]{2,1,0:T(8,128)S(1)}) custom-call(bf16[4,128,512]{2,1,0:T(8,128)(2,1)S(1)} %collective-permute-done.2.x_ref, bf16[512,1536]{1,0:T(8,128)(2,1)S(1)} %copy-done, bf16[256,256]{1,0:T(8,128)(2,1)S(1)} %means.1.means_ref, ...), custom_call_target="tpu_custom_call", output_to_operand_aliasing={{1}: (7, {})} | custom-call | flops 1000000 | bytes 4096 | tf_op jit(solution)/shard_map/even/pallas_call | solution.py:318
  15.3 0.7 %collective-permute-done.1.x_ref = bf16[4,128,512]{2,1,0:T(8,128)(2,1)S(1)} collective-permute-done((bf16[4,128,512]{2,1,0:T(8,128)(2,1)}, bf16[4,128,512]{2,1,0:T(8,128)(2,1)S(1)}, u32[]{:S(2)}, u32[]{:S(2)}) %collective-permute-start.1) | collective-permute-done | bytes 524320 | tf_op jit(solution)/shard_map/ppermute | solution.py:334
  16.0 0.9 %keys.1 = (bf16[4,128,512]{2,1,0:T(8,128)(2,1)S(1)}, bf16[4,128,512]{2,1,0:T(8,128)(2,1)S(1)}, f32[4,64,256]{2,1,0:T(8,128)S(1)}) custom-call(bf16[4,128,512]{2,1,0:T(8,128)(2,1)S(1)} %collective-permute-done.1.x_ref, bf16[512,1536]{1,0:T(8,128)(2,1)S(1)} %copy-done, bf16[256,256]{1,0:T(8,128)(2,1)S(1)} %means.1.means_ref, ...), custom_call_target="tpu_custom_call", output_to_operand_aliasing={{2}: (3, {})} | custom-call | flops 1000000 | bytes 4096 | tf_op jit(solution)/shard_map/keys/pallas_call | solution.py:318
  17.0 0.0 collective-permute-done.4.refs_1_
  17.0 0.1 carry.1
  17.1 1.6 %collective-permute-start.6 = (bf16[4,64,256]{2,1,0:T(8,128)(2,1)S(1)}, bf16[4,64,256]{2,1,0:T(8,128)(2,1)S(1)}, u32[]{:S(2)}, u32[]{:S(2)}) collective-permute-start(bf16[4,64,256]{2,1,0:T(8,128)(2,1)S(1)} %get-tuple-element.31), channel_id=1, source_target_pairs={{0,1},{1,0},{2,3},{3,2},{4,5},{5,4},{6,7},{7,6},{8,9},{9,8},{10,11... | collective-permute-start | bytes 393224 | tf_op jit(solution)/shard_map/ppermute | solution.py:334
  18.7 1.0 %odd.1.gathered_ref = bf16[4,128,512]{2,1,0:T(8,128)(2,1)S(1)} custom-call(bf16[4,128,512]{2,1,0:T(8,128)(2,1)S(1)} %get-tuple-element.32.k_ref, bf16[4,128,512]{2,1,0:T(8,128)(2,1)S(1)} %get-tuple-element.33.v_ref, bf16[4,128,512]{2,1,0:T(8,128)(2,1)S(1)} %get-tuple-element.24.q_ref, f32[4,256]{1,0:T(4,128)S(1)} %get-tuple-element.26.row_ref, ...), custom_call_target="tpu_custom_call" | custom-call | flops 1000000 | bytes 4096 | tf_op jit(solution)/shard_map/odd/pallas_call | solution.py:318
  19.8 0.2 copy-done.2
  20.0 1.9 %closing.1 = bf16[4,128,512]{2,1,0:T(8,128)(2,1)} custom-call(bf16[4,128,512]{2,1,0:T(8,128)(2,1)S(1)} %get-tuple-element.24.q_ref, f32[4,128,512]{2,1,0:T(8,128)S(1)} %get-tuple-element.25.lin_ref, bf16[4,64,256]{2,1,0:T(8,128)(2,1)S(1)} %get-tuple-element.30.mine_ref, bf16[4,64,256]{2,1,0:T(8,128)(2,1)S(1)} %collective-permute-done.6.other_ref, ...), custom_call_target="tpu_custom_call" | custom-call | flops 1000000 | bytes 4096 | tf_op jit(solution)/shard_map/closing/pallas_call | solution.py:318
  (13 shorter events, 0.1 us)
Async XLA Ops:
  0.0 4.5 %copy-start.1 = (bf16[4,128,512]{2,1,0:T(8,128)(2,1)S(1)}, bf16[4,128,512]{2,1,0:T(8,128)(2,1)}, u32[]{:S(2)}) copy-start(bf16[4,128,512]{2,1,0:T(8,128)(2,1)} %x_ref.5) | copy-start | bytes 1572868
  0.0 4.6 %copy-start = (bf16[512,1536]{1,0:T(8,128)(2,1)S(1)}, bf16[512,1536]{1,0:T(8,128)(2,1)}, u32[]{:S(2)}) copy-start(bf16[512,1536]{1,0:T(8,128)(2,1)} %w_ref.7) | copy-start | bytes 4718596
  0.0 13.5 %collective-permute-start.2 = (bf16[4,128,512]{2,1,0:T(8,128)(2,1)}, bf16[4,128,512]{2,1,0:T(8,128)(2,1)S(1)}, u32[]{:S(2)}, u32[]{:S(2)}) collective-permute-start(bf16[4,128,512]{2,1,0:T(8,128)(2,1)} %x_ref.5), channel_id=1, source_target_pairs={{0,8},{8,0},{16,24},{24,16},{1,9},{9,1},{17,25},{25,17},{2,10},{10... | collective-permute-start | bytes 1572872 | tf_op jit(solution)/shard_map/ppermute | solution.py:334
  0.0 16.0 %collective-permute-start.1 = (bf16[4,128,512]{2,1,0:T(8,128)(2,1)}, bf16[4,128,512]{2,1,0:T(8,128)(2,1)S(1)}, u32[]{:S(2)}, u32[]{:S(2)}) collective-permute-start(bf16[4,128,512]{2,1,0:T(8,128)(2,1)} %x_ref.5), channel_id=1, source_target_pairs={{8,16},{16,8},{9,17},{17,9},{10,18},{18,10},{11,19},{19,11},{12,20... | collective-permute-start | bytes 1572872 | tf_op jit(solution)/shard_map/ppermute | solution.py:334
  6.0 6.4 %copy-start.3 = (s32[4,8]{1,0:T(4,128)S(1)}, s32[4,8]{1,0:T(4,128)}, u32[]{:S(2)}) copy-start(s32[4,8]{1,0:T(4,128)} %table_ref.1) | copy-start | bytes 388
  6.0 6.4 %copy-start.4 = (s32[4]{0:T(128)S(1)}, s32[4]{0:T(128)}, u32[]{:S(2)}) copy-start(s32[4]{0:T(128)} %param.11) | copy-start | bytes 52
  6.0 6.4 %copy-start.5 = (f32[8]{0:T(128)S(1)}, f32[8]{0:T(128)}, u32[]{:S(2)}) copy-start(f32[8]{0:T(128)} %param.9) | copy-start | bytes 100
  6.1 2.3 %collective-permute-start = (bf16[4,64,256]{2,1,0:T(8,128)(2,1)S(1)}, bf16[4,64,256]{2,1,0:T(8,128)(2,1)S(1)}, u32[]{:S(2)}, u32[]{:S(2)}) collective-permute-start(bf16[4,64,256]{2,1,0:T(8,128)(2,1)S(1)} %get-tuple-element.23), channel_id=1, source_target_pairs={{0,1},{1,0},{2,3},{3,2},{4,5},{5,4},{6,7},{7,6},{8,9},{9,8},{10,11... | collective-permute-start | bytes 393224 | tf_op jit(solution)/shard_map/ppermute | solution.py:334
  8.4 8.6 %collective-permute-start.3 = (bf16[4,64,256]{2,1,0:T(8,128)(2,1)S(1)}, bf16[4,64,256]{2,1,0:T(8,128)(2,1)S(1)}, u32[]{:S(2)}, u32[]{:S(2)}) collective-permute-start(bf16[4,64,256]{2,1,0:T(8,128)(2,1)S(1)} %combine.1.total_ref), channel_id=1, source_target_pairs={{0,2},{1,3},{2,0},{3,1},{4,6},{5,7},{6,4},{7,5},{8,10},{9,11},{10,... | collective-permute-start | bytes 393224 | tf_op jit(solution)/shard_map/ppermute | solution.py:334
  9.6 7.3 %collective-permute-start.4 = (bf16[4,64,256]{2,1,0:T(8,128)(2,1)S(1)}, bf16[4,64,256]{2,1,0:T(8,128)(2,1)S(1)}, u32[]{:S(2)}, u32[]{:S(2)}) collective-permute-start(bf16[4,64,256]{2,1,0:T(8,128)(2,1)S(1)} %combine.1.total_ref), channel_id=1, source_target_pairs={{0,4},{1,5},{2,6},{3,7},{4,0},{5,1},{6,2},{7,3},{8,12},{9,13},{10,... | collective-permute-start | bytes 393224 | tf_op jit(solution)/shard_map/ppermute | solution.py:334
  10.9 6.1 %collective-permute-start.5 = (bf16[4,64,256]{2,1,0:T(8,128)(2,1)S(1)}, bf16[4,64,256]{2,1,0:T(8,128)(2,1)S(1)}, u32[]{:S(2)}, u32[]{:S(2)}) collective-permute-start(bf16[4,64,256]{2,1,0:T(8,128)(2,1)S(1)} %combine.1.total_ref), channel_id=1, source_target_pairs={{0,6},{1,7},{2,4},{3,5},{4,2},{5,3},{6,0},{7,1},{8,14},{9,15},{10,... | collective-permute-start | bytes 393224 | tf_op jit(solution)/shard_map/ppermute | solution.py:334
  17.1 2.7 %collective-permute-start.6 = (bf16[4,64,256]{2,1,0:T(8,128)(2,1)S(1)}, bf16[4,64,256]{2,1,0:T(8,128)(2,1)S(1)}, u32[]{:S(2)}, u32[]{:S(2)}) collective-permute-start(bf16[4,64,256]{2,1,0:T(8,128)(2,1)S(1)} %get-tuple-element.31), channel_id=1, source_target_pairs={{0,1},{1,0},{2,3},{3,2},{4,5},{5,4},{6,7},{7,6},{8,9},{9,8},{10,11... | collective-permute-start | bytes 393224 | tf_op jit(solution)/shard_map/ppermute | solution.py:334
  18.7 1.2 %copy-start.2 = (bf16[1024,512]{1,0:T(8,128)(2,1)S(1)}, bf16[1024,512]{1,0:T(8,128)(2,1)}, u32[]{:S(2)}) copy-start(bf16[1024,512]{1,0:T(8,128)(2,1)} %close_ref.1) | copy-start | bytes 3145732

commit v8 on v7

--- a/solution.py
+++ b/solution.py
@@ -29,9 +29,9 @@
     return lax.dot_general(a, b, (((0,), (0,)), ((), ())), preferred_element_type=F32)
 
 
-def row_norm(x):
+def row_scale(x):
     xf = x.astype(F32)
-    return (xf * lax.rsqrt(jnp.mean(xf * xf, axis=-1, keepdims=True) + 1e-06)).astype(BF16)
+    return lax.rsqrt(jnp.mean(xf * xf, axis=-1, keepdims=True) + 1e-06)
 
 
 def head_ids(shape, axis, breadth):
@@ -66,21 +66,22 @@
     return ref[:, c * T : (c + 1) * T, u * PAIR : (u + 1) * PAIR].reshape(groups * T, PAIR)
 
 
-def project(normed, w_ref, first, count):
-    return [dot(normed, w_ref[:, first + h * HALF : first + (h + 1) * HALF]) for h in range(count)]
+def project(rows, w_ref, first, count):
+    return [dot(rows, w_ref[:, first + h * HALF : first + (h + 1) * HALF]) for h in range(count)]
 
 
 def keys_values(x_ref, w_ref, means_ref, k_ref, v_ref, breadth):
     groups, patches, width = x_ref.shape
     halves = width // HALF
     means = means_ref[...]
-    normed = row_norm(x_ref[...].reshape(groups * patches, width))
-    keys = project(normed, w_ref, width, halves)
-    values = project(normed, w_ref, 2 * width, halves)
+    rows = x_ref[...].reshape(groups * patches, width)
+    keys = project(rows, w_ref, width, halves)
+    values = project(rows, w_ref, 2 * width, halves)
+    scale = row_scale(rows)
     for h in range(halves):
         at = slice(h * HALF, (h + 1) * HALF)
-        v_ref[:, :, at] = values[h].astype(BF16).reshape(groups, patches, HALF)
-        k_ref[:, :, at] = head_norm(keys[h], means, 1e-06).reshape(groups, patches, HALF)
+        v_ref[:, :, at] = (values[h] * scale).astype(BF16).reshape(groups, patches, HALF)
+        k_ref[:, :, at] = head_norm(keys[h] * scale, means, 1e-06).reshape(groups, patches, HALF)
 
 
 def staggered(items, *stages):
@@ -179,9 +180,11 @@
     means = means_ref[...]
     wide = (patches, patches * (PAIR // breadth))
     causal = lax.broadcasted_iota(jnp.int32, wide, 0) >= lax.broadcasted_iota(jnp.int32, wide, 1) % patches
-    queries = project(row_norm(x_ref[...].reshape(groups * patches, width)), w_ref, 0, halves)
+    rows = x_ref[...].reshape(groups * patches, width)
+    queries = project(rows, w_ref, 0, halves)
+    scale = row_scale(rows)
     for h in range(halves):
-        q = head_norm(queries[h], means, 1e-06)
+        q = head_norm(queries[h] * scale, means, 1e-06)
         q_ref[:, :, h * HALF : (h + 1) * HALF] = q.reshape(groups, patches, HALF)
 
     def score(h, g):
@@ -229,7 +232,7 @@
     return (partner >= 0) & (partner < lax.axis_size("stations"))
 
 
-def odd_keys_kernel(breadth, x_ref, w_ref, means_ref, keep_ref, k_ref, v_ref, kept_ref):
+def odd_keys_kernel(breadth, x_ref, w_ref, means_ref, keep_ref, close_ref, k_ref, v_ref, kept_ref):
     @pl.when(odd_partner())
     def _():
         keys_values(x_ref, w_ref, means_ref, k_ref, v_ref, breadth)
@@ -302,7 +305,7 @@
     *pieces, send_ref, mine_ref = refs
     core, chip = lax.axis_index("tm") % 2, lax.axis_index("tm") // 2
     before = jnp.zeros(keep_ref.shape, F32)
-    for m, piece in enumerate(pieces, 1):
+    for m, piece in zip(range(len(pieces), 0, -1), pieces):
         before += jnp.where((chip ^ m) < chip, piece[...].astype(F32), 0.0)
     send_ref[...] = (before + jnp.where(core == 0, keep_ref[...], 0.0)).astype(BF16)
     mine_ref[...] = (before + jnp.where(core == 0, 0.0, got_ref[...].astype(F32))).astype(BF16)
@@ -350,7 +353,7 @@
     )
     got = swap_with(give, "tm", lambda i: i ^ 1)
     (total,) = call(combine_kernel, breadth, [(part, BF16)], (keep, got), name="combine")
-    pieces = [swap_with(total, "tm", lambda i: i ^ (2 * m)) for m in range(1, chips)]
+    pieces = [swap_with(total, "tm", lambda i: i ^ (2 * m)) for m in range(chips - 1, 0, -1)]
     q, lin = call(
         own_kernel,
         breadth,
@@ -381,9 +384,9 @@
         odd_keys_kernel,
         breadth,
         [(block, BF16)] * 2 + [(part, F32)],
-        (x_odd, w, means, keep),
+        (x_odd, w, means, keep, close),
         name="keys",
-        through={3: 2},
+        through={3: 2, 4: None},
     )
     send, mine = call(carry_kernel, breadth, [(part, BF16)] * 2, (keep, got, *pieces), name="carry")
     other = swap_with(send, "tm", lambda i: i ^ 1)

time: 22.1 us -> 21.9 us (level)
  waiting for transfers between devices: 1.72 us -> 2.44 us
  starting transfers between devices: 10.1 us -> 9.55 us
    ppermute x7, waiting for transfers between devices: 1.72 us -> 2.44 us  [swap_with(): return lax.ppermute(value, axis, pairs)]
    ppermute x7, starting transfers between devices: 10.1 us -> 9.55 us  [swap_with(): return lax.ppermute(value, axis, pairs)]
  transfers between devices with their start and end apart: 7 -> 7, of which waited for: 2 -> 3; matrix products, arithmetic and copies ran while one was open for 0% -> 0% of each run, Pallas kernels for 35% -> 34%
where the time goes in v8:
time: 21.9 us; the launch traced here: 21.6 us
  starting transfers between devices  9.55 us (44%)
  Pallas kernels  9.42 us (43%)
  waiting for transfers between devices  2.44 us (11%)
    ppermute x7, starting transfers between devices, swap_with(): return lax.ppermute(value, axis, pairs)  9.55 us
    pallas_call x11, Pallas kernels, call(): pl.pallas_call(functools.partial(kernel, breadth), out_shape=[jax.ShapeDt...  9.42 us
    ppermute x7, waiting for transfers between devices, swap_with(): return lax.ppermute(value, axis, pairs)  2.44 us
  transfers between devices with their start and end apart: 7, of which 3 were waited for; matrix products, arithmetic and copies ran while one was open for 0% of the time, Pallas kernels for 34%

profile of v8, /device:TPU:9, one launch (start us, length us, event | category | flops | bytes accessed | tf_op | source)
XLA Modules:
  0.0 21.6 jit_solution(17939152264497044376)
XLA Ops:
  0.0 4.5 %collective-permute-start.1 = (bf16[4,128,512]{2,1,0:T(8,128)(2,1)}, bf16[4,128,512]{2,1,0:T(8,128)(2,1)S(1)}, u32[]{:S(2)}, u32[]{:S(2)}) collective-permute-start(bf16[4,128,512]{2,1,0:T(8,128)(2,1)} %x_ref.5), channel_id=1, source_target_pairs={{8,16},{16,8},{9,17},{17,9},{10,18},{18,10},{11,19},{19,11},{12,20... | collective-permute-start | bytes 1572872 | tf_op jit(solution)/shard_map/ppermute | solution.py:337
  4.6 1.4 %states.1 = (bf16[4,128,512]{2,1,0:T(8,128)(2,1)S(1)}, bf16[4,128,512]{2,1,0:T(8,128)(2,1)S(1)}, f32[4,64,256]{2,1,0:T(8,128)S(1)}, bf16[4,64,256]{2,1,0:T(8,128)(2,1)S(1)}) custom-call(bf16[4,128,512]{2,1,0:T(8,128)(2,1)S(1)} %copy-done.1, bf16[512,1536]{1,0:T(8,128)(2,1)S(1)} %copy-done, bf16[256,256]{1,0:T(8,128)(2,1)S(1)} %means.1.means_ref), custom_call_target="tpu_custom_call" | custom-call | flops 1000000 | bytes 4096 | tf_op jit(solution)/shard_map/states/pallas_call | solution.py:321
  6.0 0.0 copy-start.3
  6.0 0.0 copy-start.4
  6.0 0.0 copy-start.5
  6.0 1.3 %collective-permute-start = (bf16[4,64,256]{2,1,0:T(8,128)(2,1)S(1)}, bf16[4,64,256]{2,1,0:T(8,128)(2,1)S(1)}, u32[]{:S(2)}, u32[]{:S(2)}) collective-permute-start(bf16[4,64,256]{2,1,0:T(8,128)(2,1)S(1)} %get-tuple-element.23), channel_id=1, source_target_pairs={{0,1},{1,0},{2,3},{3,2},{4,5},{5,4},{6,7},{7,6},{8,9},{9,8},{10,11... | collective-permute-start | bytes 393224 | tf_op jit(solution)/shard_map/ppermute | solution.py:337
  7.3 1.0 %collective-permute-done.got_ref = bf16[4,64,256]{2,1,0:T(8,128)(2,1)S(1)} collective-permute-done((bf16[4,64,256]{2,1,0:T(8,128)(2,1)S(1)}, bf16[4,64,256]{2,1,0:T(8,128)(2,1)S(1)}, u32[]{:S(2)}, u32[]{:S(2)}) %collective-permute-start) | collective-permute-done | bytes 131104 | tf_op jit(solution)/shard_map/ppermute | solution.py:337
  8.3 2.2 %collective-permute-start.3 = (bf16[4,64,256]{2,1,0:T(8,128)(2,1)S(1)}, bf16[4,64,256]{2,1,0:T(8,128)(2,1)S(1)}, u32[]{:S(2)}, u32[]{:S(2)}) collective-permute-start(bf16[4,64,256]{2,1,0:T(8,128)(2,1)S(1)} %combine.1.total_ref), channel_id=1, source_target_pairs={{0,6},{1,7},{2,4},{3,5},{4,2},{5,3},{6,0},{7,1},{8,14},{9,15},{10,... | collective-permute-start | bytes 393224 | tf_op jit(solution)/shard_map/ppermute | solution.py:337
  10.6 0.2 %collective-permute-start.4 = (bf16[4,64,256]{2,1,0:T(8,128)(2,1)S(1)}, bf16[4,64,256]{2,1,0:T(8,128)(2,1)S(1)}, u32[]{:S(2)}, u32[]{:S(2)}) collective-permute-start(bf16[4,64,256]{2,1,0:T(8,128)(2,1)S(1)} %combine.1.total_ref), channel_id=1, source_target_pairs={{0,4},{1,5},{2,6},{3,7},{4,0},{5,1},{6,2},{7,3},{8,12},{9,13},{10,... | collective-permute-start | bytes 393224 | tf_op jit(solution)/shard_map/ppermute | solution.py:337
  10.8 0.3 %collective-permute-start.5 = (bf16[4,64,256]{2,1,0:T(8,128)(2,1)S(1)}, bf16[4,64,256]{2,1,0:T(8,128)(2,1)S(1)}, u32[]{:S(2)}, u32[]{:S(2)}) collective-permute-start(bf16[4,64,256]{2,1,0:T(8,128)(2,1)S(1)} %combine.1.total_ref), channel_id=1, source_target_pairs={{0,2},{1,3},{2,0},{3,1},{4,6},{5,7},{6,4},{7,5},{8,10},{9,11},{10,... | collective-permute-start | bytes 393224 | tf_op jit(solution)/shard_map/ppermute | solution.py:337
  11.0 1.3 %own.1 = (bf16[4,128,512]{2,1,0:T(8,128)(2,1)S(1)}, f32[4,128,512]{2,1,0:T(8,128)S(1)}) custom-call(bf16[4,128,512]{2,1,0:T(8,128)(2,1)S(1)} %copy-done.1, bf16[512,1536]{1,0:T(8,128)(2,1)S(1)} %copy-done, bf16[256,256]{1,0:T(8,128)(2,1)S(1)} %means.1.means_ref, bf16[4,128,512]{2,1,0:T(8,128)(2,1)S(1)} %get-tuple-element.20.k_ref, ...), custom_call_target="tpu_custom_call" | custom-call | flops 1000000 | bytes 4096 | tf_op jit(solution)/shard_map/own/pallas_call | solution.py:321
  12.3 0.2 %masks.1 = (f32[3,128,256]{2,1,0:T(8,128)S(1)}, f32[4,256]{1,0:T(4,128)S(1)}) custom-call(s32[4,8]{1,0:T(4,128)S(1)} %copy-done.3, s32[1,4]{1,0:T(1,128)S(1)} %bitcast.2, f32[1,8]{1,0:T(1,128)S(1)} %bitcast.3, bf16[4,64,256]{2,1,0:T(8,128)(2,1)S(1)} %combine.1.total_ref), custom_call_target="tpu_custom_call" | custom-call | flops 1000000 | bytes 4096 | tf_op jit(solution)/shard_map/masks/pallas_call | solution.py:321
  12.6 0.9 %near.1.acc_ref = f32[4,128,1024]{2,1,0:T(8,128)S(1)} custom-call(bf16[4,128,512]{2,1,0:T(8,128)(2,1)S(1)} %get-tuple-element.20.k_ref, bf16[4,128,512]{2,1,0:T(8,128)(2,1)S(1)} %get-tuple-element.21.v_ref, bf16[4,128,512]{2,1,0:T(8,128)(2,1)S(1)} %get-tuple-element.24.q_ref, f32[4,256]{1,0:T(4,128)S(1)} %get-tuple-element.26.row_ref, ...), custom_call_target="tpu_custom_call" | custom-call | flops 1000000 | bytes 4096 | tf_op jit(solution)/shard_map/near/pallas_call | solution.py:321
  13.4 0.0 copy-start.2
  13.4 1.7 %even.1 = (f32[4,128,1024]{2,1,0:T(8,128)S(1)}, f32[4,64,256]{2,1,0:T(8,128)S(1)}) custom-call(bf16[4,128,512]{2,1,0:T(8,128)(2,1)S(1)} %collective-permute-done.2.x_ref, bf16[512,1536]{1,0:T(8,128)(2,1)S(1)} %copy-done, bf16[256,256]{1,0:T(8,128)(2,1)S(1)} %means.1.means_ref, ...), custom_call_target="tpu_custom_call", output_to_operand_aliasing={{1}: (7, {})} | custom-call | flops 1000000 | bytes 4096 | tf_op jit(solution)/shard_map/even/pallas_call | solution.py:321
  15.2 0.9 %collective-permute-done.1.x_ref = bf16[4,128,512]{2,1,0:T(8,128)(2,1)S(1)} collective-permute-done((bf16[4,128,512]{2,1,0:T(8,128)(2,1)}, bf16[4,128,512]{2,1,0:T(8,128)(2,1)S(1)}, u32[]{:S(2)}, u32[]{:S(2)}) %collective-permute-start.1) | collective-permute-done | bytes 524320 | tf_op jit(solution)/shard_map/ppermute | solution.py:337
  16.0 0.9 %keys.1 = (bf16[4,128,512]{2,1,0:T(8,128)(2,1)S(1)}, bf16[4,128,512]{2,1,0:T(8,128)(2,1)S(1)}, f32[4,64,256]{2,1,0:T(8,128)S(1)}) custom-call(bf16[4,128,512]{2,1,0:T(8,128)(2,1)S(1)} %collective-permute-done.1.x_ref, bf16[512,1536]{1,0:T(8,128)(2,1)S(1)} %copy-done, bf16[256,256]{1,0:T(8,128)(2,1)S(1)} %means.1.means_ref, ...), custom_call_target="tpu_custom_call", output_to_operand_aliasing={{2}: (3, {})} | custom-call | flops 1000000 | bytes 4096 | tf_op jit(solution)/shard_map/keys/pallas_call | solution.py:321
  16.9 0.0 collective-permute-done.3.refs_0_
  16.9 0.6 %collective-permute-done.4.refs_1_ = bf16[4,64,256]{2,1,0:T(8,128)(2,1)S(1)} collective-permute-done((bf16[4,64,256]{2,1,0:T(8,128)(2,1)S(1)}, bf16[4,64,256]{2,1,0:T(8,128)(2,1)S(1)}, u32[]{:S(2)}, u32[]{:S(2)}) %collective-permute-start.4) | collective-permute-done | bytes 131104 | tf_op jit(solution)/shard_map/ppermute | solution.py:337
  17.5 0.0 collective-permute-done.5.refs_2_
  17.5 0.1 carry.1
  17.6 1.1 %collective-permute-start.6 = (bf16[4,64,256]{2,1,0:T(8,128)(2,1)S(1)}, bf16[4,64,256]{2,1,0:T(8,128)(2,1)S(1)}, u32[]{:S(2)}, u32[]{:S(2)}) collective-permute-start(bf16[4,64,256]{2,1,0:T(8,128)(2,1)S(1)} %get-tuple-element.31), channel_id=1, source_target_pairs={{0,1},{1,0},{2,3},{3,2},{4,5},{5,4},{6,7},{7,6},{8,9},{9,8},{10,11... | collective-permute-start | bytes 393224 | tf_op jit(solution)/shard_map/ppermute | solution.py:337
  18.7 1.0 %odd.1.gathered_ref = bf16[4,128,512]{2,1,0:T(8,128)(2,1)S(1)} custom-call(bf16[4,128,512]{2,1,0:T(8,128)(2,1)S(1)} %get-tuple-element.32.k_ref, bf16[4,128,512]{2,1,0:T(8,128)(2,1)S(1)} %get-tuple-element.33.v_ref, bf16[4,128,512]{2,1,0:T(8,128)(2,1)S(1)} %get-tuple-element.24.q_ref, f32[4,256]{1,0:T(4,128)S(1)} %get-tuple-element.26.row_ref, ...), custom_call_target="tpu_custom_call" | custom-call | flops 1000000 | bytes 4096 | tf_op jit(solution)/shard_map/odd/pallas_call | solution.py:321
  19.8 1.9 %closing.1 = bf16[4,128,512]{2,1,0:T(8,128)(2,1)} custom-call(bf16[4,128,512]{2,1,0:T(8,128)(2,1)S(1)} %get-tuple-element.24.q_ref, f32[4,128,512]{2,1,0:T(8,128)S(1)} %get-tuple-element.25.lin_ref, bf16[4,64,256]{2,1,0:T(8,128)(2,1)S(1)} %get-tuple-element.30.mine_ref, bf16[4,64,256]{2,1,0:T(8,128)(2,1)S(1)} %collective-permute-done.6.other_ref, ...), custom_call_target="tpu_custom_call" | custom-call | flops 1000000 | bytes 4096 | tf_op jit(solution)/shard_map/closing/pallas_call | solution.py:321
  (13 shorter events, 0.1 us)
Async XLA Ops:
  0.0 4.5 %copy-start.1 = (bf16[4,128,512]{2,1,0:T(8,128)(2,1)S(1)}, bf16[4,128,512]{2,1,0:T(8,128)(2,1)}, u32[]{:S(2)}) copy-start(bf16[4,128,512]{2,1,0:T(8,128)(2,1)} %x_ref.5) | copy-start | bytes 1572868
  0.0 4.6 %copy-start = (bf16[512,1536]{1,0:T(8,128)(2,1)S(1)}, bf16[512,1536]{1,0:T(8,128)(2,1)}, u32[]{:S(2)}) copy-start(bf16[512,1536]{1,0:T(8,128)(2,1)} %w_ref.7) | copy-start | bytes 4718596
  0.0 13.4 %collective-permute-start.2 = (bf16[4,128,512]{2,1,0:T(8,128)(2,1)}, bf16[4,128,512]{2,1,0:T(8,128)(2,1)S(1)}, u32[]{:S(2)}, u32[]{:S(2)}) collective-permute-start(bf16[4,128,512]{2,1,0:T(8,128)(2,1)} %x_ref.5), channel_id=1, source_target_pairs={{0,8},{8,0},{16,24},{24,16},{1,9},{9,1},{17,25},{25,17},{2,10},{10... | collective-permute-start | bytes 1572872 | tf_op jit(solution)/shard_map/ppermute | solution.py:337
  0.0 16.0 %collective-permute-start.1 = (bf16[4,128,512]{2,1,0:T(8,128)(2,1)}, bf16[4,128,512]{2,1,0:T(8,128)(2,1)S(1)}, u32[]{:S(2)}, u32[]{:S(2)}) collective-permute-start(bf16[4,128,512]{2,1,0:T(8,128)(2,1)} %x_ref.5), channel_id=1, source_target_pairs={{8,16},{16,8},{9,17},{17,9},{10,18},{18,10},{11,19},{19,11},{12,20... | collective-permute-start | bytes 1572872 | tf_op jit(solution)/shard_map/ppermute | solution.py:337
  6.0 6.3 %copy-start.3 = (s32[4,8]{1,0:T(4,128)S(1)}, s32[4,8]{1,0:T(4,128)}, u32[]{:S(2)}) copy-start(s32[4,8]{1,0:T(4,128)} %table_ref.1) | copy-start | bytes 388
  6.0 6.3 %copy-start.4 = (s32[4]{0:T(128)S(1)}, s32[4]{0:T(128)}, u32[]{:S(2)}) copy-start(s32[4]{0:T(128)} %param.11) | copy-start | bytes 52
  6.0 6.3 %copy-start.5 = (f32[8]{0:T(128)S(1)}, f32[8]{0:T(128)}, u32[]{:S(2)}) copy-start(f32[8]{0:T(128)} %param.9) | copy-start | bytes 100
  6.0 2.3 %collective-permute-start = (bf16[4,64,256]{2,1,0:T(8,128)(2,1)S(1)}, bf16[4,64,256]{2,1,0:T(8,128)(2,1)S(1)}, u32[]{:S(2)}, u32[]{:S(2)}) collective-permute-start(bf16[4,64,256]{2,1,0:T(8,128)(2,1)S(1)} %get-tuple-element.23), channel_id=1, source_target_pairs={{0,1},{1,0},{2,3},{3,2},{4,5},{5,4},{6,7},{7,6},{8,9},{9,8},{10,11... | collective-permute-start | bytes 393224 | tf_op jit(solution)/shard_map/ppermute | solution.py:337
  8.3 8.6 %collective-permute-start.3 = (bf16[4,64,256]{2,1,0:T(8,128)(2,1)S(1)}, bf16[4,64,256]{2,1,0:T(8,128)(2,1)S(1)}, u32[]{:S(2)}, u32[]{:S(2)}) collective-permute-start(bf16[4,64,256]{2,1,0:T(8,128)(2,1)S(1)} %combine.1.total_ref), channel_id=1, source_target_pairs={{0,6},{1,7},{2,4},{3,5},{4,2},{5,3},{6,0},{7,1},{8,14},{9,15},{10,... | collective-permute-start | bytes 393224 | tf_op jit(solution)/shard_map/ppermute | solution.py:337
  10.6 7.0 %collective-permute-start.4 = (bf16[4,64,256]{2,1,0:T(8,128)(2,1)S(1)}, bf16[4,64,256]{2,1,0:T(8,128)(2,1)S(1)}, u32[]{:S(2)}, u32[]{:S(2)}) collective-permute-start(bf16[4,64,256]{2,1,0:T(8,128)(2,1)S(1)} %combine.1.total_ref), channel_id=1, source_target_pairs={{0,4},{1,5},{2,6},{3,7},{4,0},{5,1},{6,2},{7,3},{8,12},{9,13},{10,... | collective-permute-start | bytes 393224 | tf_op jit(solution)/shard_map/ppermute | solution.py:337
  10.8 6.7 %collective-permute-start.5 = (bf16[4,64,256]{2,1,0:T(8,128)(2,1)S(1)}, bf16[4,64,256]{2,1,0:T(8,128)(2,1)S(1)}, u32[]{:S(2)}, u32[]{:S(2)}) collective-permute-start(bf16[4,64,256]{2,1,0:T(8,128)(2,1)S(1)} %combine.1.total_ref), channel_id=1, source_target_pairs={{0,2},{1,3},{2,0},{3,1},{4,6},{5,7},{6,4},{7,5},{8,10},{9,11},{10,... | collective-permute-start | bytes 393224 | tf_op jit(solution)/shard_map/ppermute | solution.py:337
  13.4 2.6 %copy-start.2 = (bf16[1024,512]{1,0:T(8,128)(2,1)S(1)}, bf16[1024,512]{1,0:T(8,128)(2,1)}, u32[]{:S(2)}) copy-start(bf16[1024,512]{1,0:T(8,128)(2,1)} %close_ref.3) | copy-start | bytes 3145732
  17.6 2.1 %collective-permute-start.6 = (bf16[4,64,256]{2,1,0:T(8,128)(2,1)S(1)}, bf16[4,64,256]{2,1,0:T(8,128)(2,1)S(1)}, u32[]{:S(2)}, u32[]{:S(2)}) collective-permute-start(bf16[4,64,256]{2,1,0:T(8,128)(2,1)S(1)} %get-tuple-element.31), channel_id=1, source_target_pairs={{0,1},{1,0},{2,3},{3,2},{4,5},{5,4},{6,7},{7,6},{8,9},{9,8},{10,11... | collective-permute-start | bytes 393224 | tf_op jit(solution)/shard_map/ppermute | solution.py:337

commit v9 on v7

--- a/solution.py
+++ b/solution.py
@@ -48,6 +48,13 @@
     return (values * lax.rsqrt(dot(square, means) + epsilon)).astype(BF16)
 
 
+def exact_head_norm(values, means, epsilon):
+    square = values * values
+    high = square.astype(BF16)
+    low = (square - high.astype(F32)).astype(BF16)
+    return (values * lax.rsqrt(dot(high, means) + dot(low, means) + epsilon)).astype(BF16)
+
+
 def own_head(values, j, breadth):
     ids = head_ids(values.shape, 1, breadth)
     return jnp.where(ids == j, values, jnp.zeros_like(values))
@@ -70,7 +77,7 @@
     return [dot(normed, w_ref[:, first + h * HALF : first + (h + 1) * HALF]) for h in range(count)]
 
 
-def keys_values(x_ref, w_ref, means_ref, k_ref, v_ref, breadth):
+def keys_values(x_ref, w_ref, means_ref, k_ref, v_ref, breadth, norm=head_norm):
     groups, patches, width = x_ref.shape
     halves = width // HALF
     means = means_ref[...]
@@ -80,7 +87,7 @@
     for h in range(halves):
         at = slice(h * HALF, (h + 1) * HALF)
         v_ref[:, :, at] = values[h].astype(BF16).reshape(groups, patches, HALF)
-        k_ref[:, :, at] = head_norm(keys[h], means, 1e-06).reshape(groups, patches, HALF)
+        k_ref[:, :, at] = norm(keys[h], means, 1e-06).reshape(groups, patches, HALF)
 
 
 def staggered(items, *stages):
@@ -151,7 +158,7 @@
 def states_kernel(breadth, x_ref, w_ref, means_ref, k_ref, v_ref, keep_ref, give_ref):
     groups, patches, width = x_ref.shape
     core = lax.axis_index("tm") % 2
-    keys_values(x_ref, w_ref, means_ref, k_ref, v_ref, breadth)
+    keys_values(x_ref, w_ref, means_ref, k_ref, v_ref, breadth, exact_head_norm)
     for h in range(width // HALF):
         states = []
         for g in range(groups):
@@ -181,7 +188,7 @@
     causal = lax.broadcasted_iota(jnp.int32, wide, 0) >= lax.broadcasted_iota(jnp.int32, wide, 1) % patches
     queries = project(row_norm(x_ref[...].reshape(groups * patches, width)), w_ref, 0, halves)
     for h in range(halves):
-        q = head_norm(queries[h], means, 1e-06)
+        q = exact_head_norm(queries[h], means, 1e-06)
         q_ref[:, :, h * HALF : (h + 1) * HALF] = q.reshape(groups, patches, HALF)
 
     def score(h, g):
@@ -229,7 +236,7 @@
     return (partner >= 0) & (partner < lax.axis_size("stations"))
 
 
-def odd_keys_kernel(breadth, x_ref, w_ref, means_ref, keep_ref, k_ref, v_ref, kept_ref):
+def odd_keys_kernel(breadth, x_ref, w_ref, means_ref, keep_ref, close_ref, k_ref, v_ref, kept_ref):
     @pl.when(odd_partner())
     def _():
         keys_values(x_ref, w_ref, means_ref, k_ref, v_ref, breadth)
@@ -381,9 +388,9 @@
         odd_keys_kernel,
         breadth,
         [(block, BF16)] * 2 + [(part, F32)],
-        (x_odd, w, means, keep),
+        (x_odd, w, means, keep, close),
         name="keys",
-        through={3: 2},
+        through={3: 2, 4: None},
     )
     send, mine = call(carry_kernel, breadth, [(part, BF16)] * 2, (keep, got, *pieces), name="carry")
     other = swap_with(send, "tm", lambda i: i ^ 1)

time: 22.1 us -> 22 us (level)
  waiting for transfers between devices: 1.72 us -> 1.4 us
  Pallas kernels: 9.62 us -> 9.93 us
    ppermute x7, waiting for transfers between devices: 1.72 us -> 1.4 us  [swap_with(): return lax.ppermute(value, axis, pairs)]
    pallas_call x11, Pallas kernels: 9.62 us -> 9.93 us  [call(): pl.pallas_call(functools.partial(kernel, breadth), out_shape=[jax.ShapeDt...]
  transfers between devices with their start and end apart: 7 -> 7, of which waited for: 2 -> 2; matrix products, arithmetic and copies ran while one was open for 0% -> 0% of each run, Pallas kernels for 35% -> 37%
where the time goes in v9:
time: 22 us; the launch traced here: 21.7 us
  starting transfers between devices  10.1 us (46%)
  Pallas kernels  9.93 us (45%)
  waiting for transfers between devices  1.4 us (6%)
    ppermute x7, starting transfers between devices, swap_with(): return lax.ppermute(value, axis, pairs)  10.1 us
    pallas_call x11, Pallas kernels, call(): pl.pallas_call(functools.partial(kernel, breadth), out_shape=[jax.ShapeDt...  9.93 us
    ppermute x7, waiting for transfers between devices, swap_with(): return lax.ppermute(value, axis, pairs)  1.4 us
  transfers between devices with their start and end apart: 7, of which 2 were waited for; matrix products, arithmetic and copies ran while one was open for 0% of the time, Pallas kernels for 37%

profile of v9, /device:TPU:9, one launch (start us, length us, event | category | flops | bytes accessed | tf_op | source)
XLA Modules:
  0.0 21.7 jit_solution(867245460195733233)
XLA Ops:
  0.0 0.0 collective-permute-start.2
  0.0 4.5 %collective-permute-start.1 = (bf16[4,128,512]{2,1,0:T(8,128)(2,1)}, bf16[4,128,512]{2,1,0:T(8,128)(2,1)S(1)}, u32[]{:S(2)}, u32[]{:S(2)}) collective-permute-start(bf16[4,128,512]{2,1,0:T(8,128)(2,1)} %x_ref.5), channel_id=1, source_target_pairs={{8,16},{16,8},{9,17},{17,9},{10,18},{18,10},{11,19},{19,11},{12,20... | collective-permute-start | bytes 1572872 | tf_op jit(solution)/shard_map/ppermute | solution.py:341
  4.6 1.6 %states.1 = (bf16[4,128,512]{2,1,0:T(8,128)(2,1)S(1)}, bf16[4,128,512]{2,1,0:T(8,128)(2,1)S(1)}, f32[4,64,256]{2,1,0:T(8,128)S(1)}, bf16[4,64,256]{2,1,0:T(8,128)(2,1)S(1)}) custom-call(bf16[4,128,512]{2,1,0:T(8,128)(2,1)S(1)} %copy-done.1, bf16[512,1536]{1,0:T(8,128)(2,1)S(1)} %copy-done, bf16[256,256]{1,0:T(8,128)(2,1)S(1)} %means.1.means_ref), custom_call_target="tpu_custom_call" | custom-call | flops 1000000 | bytes 4096 | tf_op jit(solution)/shard_map/states/pallas_call | solution.py:325
  6.2 0.0 copy-start.3
  6.2 0.0 copy-start.4
  6.2 0.0 copy-start.5
  6.2 1.3 %collective-permute-start = (bf16[4,64,256]{2,1,0:T(8,128)(2,1)S(1)}, bf16[4,64,256]{2,1,0:T(8,128)(2,1)S(1)}, u32[]{:S(2)}, u32[]{:S(2)}) collective-permute-start(bf16[4,64,256]{2,1,0:T(8,128)(2,1)S(1)} %get-tuple-element.23), channel_id=1, source_target_pairs={{0,1},{1,0},{2,3},{3,2},{4,5},{5,4},{6,7},{7,6},{8,9},{9,8},{10,11... | collective-permute-start | bytes 393224 | tf_op jit(solution)/shard_map/ppermute | solution.py:341
  7.5 1.0 %collective-permute-done.got_ref = bf16[4,64,256]{2,1,0:T(8,128)(2,1)S(1)} collective-permute-done((bf16[4,64,256]{2,1,0:T(8,128)(2,1)S(1)}, bf16[4,64,256]{2,1,0:T(8,128)(2,1)S(1)}, u32[]{:S(2)}, u32[]{:S(2)}) %collective-permute-start) | collective-permute-done | bytes 131104 | tf_op jit(solution)/shard_map/ppermute | solution.py:341
  8.5 1.3 %collective-permute-start.3 = (bf16[4,64,256]{2,1,0:T(8,128)(2,1)S(1)}, bf16[4,64,256]{2,1,0:T(8,128)(2,1)S(1)}, u32[]{:S(2)}, u32[]{:S(2)}) collective-permute-start(bf16[4,64,256]{2,1,0:T(8,128)(2,1)S(1)} %combine.1.total_ref), channel_id=1, source_target_pairs={{0,2},{1,3},{2,0},{3,1},{4,6},{5,7},{6,4},{7,5},{8,10},{9,11},{10,... | collective-permute-start | bytes 393224 | tf_op jit(solution)/shard_map/ppermute | solution.py:341
  9.8 1.2 %collective-permute-start.4 = (bf16[4,64,256]{2,1,0:T(8,128)(2,1)S(1)}, bf16[4,64,256]{2,1,0:T(8,128)(2,1)S(1)}, u32[]{:S(2)}, u32[]{:S(2)}) collective-permute-start(bf16[4,64,256]{2,1,0:T(8,128)(2,1)S(1)} %combine.1.total_ref), channel_id=1, source_target_pairs={{0,4},{1,5},{2,6},{3,7},{4,0},{5,1},{6,2},{7,3},{8,12},{9,13},{10,... | collective-permute-start | bytes 393224 | tf_op jit(solution)/shard_map/ppermute | solution.py:341
  11.0 0.2 collective-permute-start.5
  11.2 1.4 %own.1 = (bf16[4,128,512]{2,1,0:T(8,128)(2,1)S(1)}, f32[4,128,512]{2,1,0:T(8,128)S(1)}) custom-call(bf16[4,128,512]{2,1,0:T(8,128)(2,1)S(1)} %copy-done.1, bf16[512,1536]{1,0:T(8,128)(2,1)S(1)} %copy-done, bf16[256,256]{1,0:T(8,128)(2,1)S(1)} %means.1.means_ref, bf16[4,128,512]{2,1,0:T(8,128)(2,1)S(1)} %get-tuple-element.20.k_ref, ...), custom_call_target="tpu_custom_call" | custom-call | flops 1000000 | bytes 4096 | tf_op jit(solution)/shard_map/own/pallas_call | solution.py:325
  12.7 0.2 %masks.1 = (f32[3,128,256]{2,1,0:T(8,128)S(1)}, f32[4,256]{1,0:T(4,128)S(1)}) custom-call(s32[4,8]{1,0:T(4,128)S(1)} %copy-done.3, s32[1,4]{1,0:T(1,128)S(1)} %bitcast.2, f32[1,8]{1,0:T(1,128)S(1)} %bitcast.3, bf16[4,64,256]{2,1,0:T(8,128)(2,1)S(1)} %combine.1.total_ref), custom_call_target="tpu_custom_call" | custom-call | flops 1000000 | bytes 4096 | tf_op jit(solution)/shard_map/masks/pallas_call | solution.py:325
  13.0 0.8 %near.1.acc_ref = f32[4,128,1024]{2,1,0:T(8,128)S(1)} custom-call(bf16[4,128,512]{2,1,0:T(8,128)(2,1)S(1)} %get-tuple-element.20.k_ref, bf16[4,128,512]{2,1,0:T(8,128)(2,1)S(1)} %get-tuple-element.21.v_ref, bf16[4,128,512]{2,1,0:T(8,128)(2,1)S(1)} %get-tuple-element.24.q_ref, f32[4,256]{1,0:T(4,128)S(1)} %get-tuple-element.26.row_ref, ...), custom_call_target="tpu_custom_call" | custom-call | flops 1000000 | bytes 4096 | tf_op jit(solution)/shard_map/near/pallas_call | solution.py:325
  13.8 0.0 copy-start.2
  13.8 0.0 collective-permute-done.2.x_ref
  13.8 1.8 %even.1 = (f32[4,128,1024]{2,1,0:T(8,128)S(1)}, f32[4,64,256]{2,1,0:T(8,128)S(1)}) custom-call(bf16[4,128,512]{2,1,0:T(8,128)(2,1)S(1)} %collective-permute-done.2.x_ref, bf16[512,1536]{1,0:T(8,128)(2,1)S(1)} %copy-done, bf16[256,256]{1,0:T(8,128)(2,1)S(1)} %means.1.means_ref, ...), custom_call_target="tpu_custom_call", output_to_operand_aliasing={{1}: (7, {})} | custom-call | flops 1000000 | bytes 4096 | tf_op jit(solution)/shard_map/even/pallas_call | solution.py:325
  15.6 0.4 %collective-permute-done.1.x_ref = bf16[4,128,512]{2,1,0:T(8,128)(2,1)S(1)} collective-permute-done((bf16[4,128,512]{2,1,0:T(8,128)(2,1)}, bf16[4,128,512]{2,1,0:T(8,128)(2,1)S(1)}, u32[]{:S(2)}, u32[]{:S(2)}) %collective-permute-start.1) | collective-permute-done | bytes 524320 | tf_op jit(solution)/shard_map/ppermute | solution.py:341
  16.0 0.9 %keys.1 = (bf16[4,128,512]{2,1,0:T(8,128)(2,1)S(1)}, bf16[4,128,512]{2,1,0:T(8,128)(2,1)S(1)}, f32[4,64,256]{2,1,0:T(8,128)S(1)}) custom-call(bf16[4,128,512]{2,1,0:T(8,128)(2,1)S(1)} %collective-permute-done.1.x_ref, bf16[512,1536]{1,0:T(8,128)(2,1)S(1)} %copy-done, bf16[256,256]{1,0:T(8,128)(2,1)S(1)} %means.1.means_ref, ...), custom_call_target="tpu_custom_call", output_to_operand_aliasing={{2}: (3, {})} | custom-call | flops 1000000 | bytes 4096 | tf_op jit(solution)/shard_map/keys/pallas_call | solution.py:325
  17.0 0.0 collective-permute-done.3.refs_0_
  17.0 0.1 carry.1
  17.1 1.6 %collective-permute-start.6 = (bf16[4,64,256]{2,1,0:T(8,128)(2,1)S(1)}, bf16[4,64,256]{2,1,0:T(8,128)(2,1)S(1)}, u32[]{:S(2)}, u32[]{:S(2)}) collective-permute-start(bf16[4,64,256]{2,1,0:T(8,128)(2,1)S(1)} %get-tuple-element.31), channel_id=1, source_target_pairs={{0,1},{1,0},{2,3},{3,2},{4,5},{5,4},{6,7},{7,6},{8,9},{9,8},{10,11... | collective-permute-start | bytes 393224 | tf_op jit(solution)/shard_map/ppermute | solution.py:341
  18.8 1.0 %odd.1.gathered_ref = bf16[4,128,512]{2,1,0:T(8,128)(2,1)S(1)} custom-call(bf16[4,128,512]{2,1,0:T(8,128)(2,1)S(1)} %get-tuple-element.32.k_ref, bf16[4,128,512]{2,1,0:T(8,128)(2,1)S(1)} %get-tuple-element.33.v_ref, bf16[4,128,512]{2,1,0:T(8,128)(2,1)S(1)} %get-tuple-element.24.q_ref, f32[4,256]{1,0:T(4,128)S(1)} %get-tuple-element.26.row_ref, ...), custom_call_target="tpu_custom_call" | custom-call | flops 1000000 | bytes 4096 | tf_op jit(solution)/shard_map/odd/pallas_call | solution.py:325
  19.8 1.9 %closing.1 = bf16[4,128,512]{2,1,0:T(8,128)(2,1)} custom-call(bf16[4,128,512]{2,1,0:T(8,128)(2,1)S(1)} %get-tuple-element.24.q_ref, f32[4,128,512]{2,1,0:T(8,128)S(1)} %get-tuple-element.25.lin_ref, bf16[4,64,256]{2,1,0:T(8,128)(2,1)S(1)} %get-tuple-element.30.mine_ref, bf16[4,64,256]{2,1,0:T(8,128)(2,1)S(1)} %collective-permute-done.6.other_ref, ...), custom_call_target="tpu_custom_call" | custom-call | flops 1000000 | bytes 4096 | tf_op jit(solution)/shard_map/closing/pallas_call | solution.py:325
  (13 shorter events, 0.1 us)
Async XLA Ops:
  0.0 4.5 %copy-start.1 = (bf16[4,128,512]{2,1,0:T(8,128)(2,1)S(1)}, bf16[4,128,512]{2,1,0:T(8,128)(2,1)}, u32[]{:S(2)}) copy-start(bf16[4,128,512]{2,1,0:T(8,128)(2,1)} %x_ref.5) | copy-start | bytes 1572868
  0.0 4.6 %copy-start = (bf16[512,1536]{1,0:T(8,128)(2,1)S(1)}, bf16[512,1536]{1,0:T(8,128)(2,1)}, u32[]{:S(2)}) copy-start(bf16[512,1536]{1,0:T(8,128)(2,1)} %w_ref.7) | copy-start | bytes 4718596
  0.0 13.8 %collective-permute-start.2 = (bf16[4,128,512]{2,1,0:T(8,128)(2,1)}, bf16[4,128,512]{2,1,0:T(8,128)(2,1)S(1)}, u32[]{:S(2)}, u32[]{:S(2)}) collective-permute-start(bf16[4,128,512]{2,1,0:T(8,128)(2,1)} %x_ref.5), channel_id=1, source_target_pairs={{0,8},{8,0},{16,24},{24,16},{1,9},{9,1},{17,25},{25,17},{2,10},{10... | collective-permute-start | bytes 1572872 | tf_op jit(solution)/shard_map/ppermute | solution.py:341
  0.0 16.0 %collective-permute-start.1 = (bf16[4,128,512]{2,1,0:T(8,128)(2,1)}, bf16[4,128,512]{2,1,0:T(8,128)(2,1)S(1)}, u32[]{:S(2)}, u32[]{:S(2)}) collective-permute-start(bf16[4,128,512]{2,1,0:T(8,128)(2,1)} %x_ref.5), channel_id=1, source_target_pairs={{8,16},{16,8},{9,17},{17,9},{10,18},{18,10},{11,19},{19,11},{12,20... | collective-permute-start | bytes 1572872 | tf_op jit(solution)/shard_map/ppermute | solution.py:341
  6.2 6.5 %copy-start.3 = (s32[4,8]{1,0:T(4,128)S(1)}, s32[4,8]{1,0:T(4,128)}, u32[]{:S(2)}) copy-start(s32[4,8]{1,0:T(4,128)} %table_ref.1) | copy-start | bytes 388
  6.2 6.5 %copy-start.4 = (s32[4]{0:T(128)S(1)}, s32[4]{0:T(128)}, u32[]{:S(2)}) copy-start(s32[4]{0:T(128)} %param.11) | copy-start | bytes 52
  6.2 6.5 %copy-start.5 = (f32[8]{0:T(128)S(1)}, f32[8]{0:T(128)}, u32[]{:S(2)}) copy-start(f32[8]{0:T(128)} %param.9) | copy-start | bytes 100
  6.2 2.3 %collective-permute-start = (bf16[4,64,256]{2,1,0:T(8,128)(2,1)S(1)}, bf16[4,64,256]{2,1,0:T(8,128)(2,1)S(1)}, u32[]{:S(2)}, u32[]{:S(2)}) collective-permute-start(bf16[4,64,256]{2,1,0:T(8,128)(2,1)S(1)} %get-tuple-element.23), channel_id=1, source_target_pairs={{0,1},{1,0},{2,3},{3,2},{4,5},{5,4},{6,7},{7,6},{8,9},{9,8},{10,11... | collective-permute-start | bytes 393224 | tf_op jit(solution)/shard_map/ppermute | solution.py:341
  8.5 8.4 %collective-permute-start.3 = (bf16[4,64,256]{2,1,0:T(8,128)(2,1)S(1)}, bf16[4,64,256]{2,1,0:T(8,128)(2,1)S(1)}, u32[]{:S(2)}, u32[]{:S(2)}) collective-permute-start(bf16[4,64,256]{2,1,0:T(8,128)(2,1)S(1)} %combine.1.total_ref), channel_id=1, source_target_pairs={{0,2},{1,3},{2,0},{3,1},{4,6},{5,7},{6,4},{7,5},{8,10},{9,11},{10,... | collective-permute-start | bytes 393224 | tf_op jit(solution)/shard_map/ppermute | solution.py:341
  9.8 7.2 %collective-permute-start.4 = (bf16[4,64,256]{2,1,0:T(8,128)(2,1)S(1)}, bf16[4,64,256]{2,1,0:T(8,128)(2,1)S(1)}, u32[]{:S(2)}, u32[]{:S(2)}) collective-permute-start(bf16[4,64,256]{2,1,0:T(8,128)(2,1)S(1)} %combine.1.total_ref), channel_id=1, source_target_pairs={{0,4},{1,5},{2,6},{3,7},{4,0},{5,1},{6,2},{7,3},{8,12},{9,13},{10,... | collective-permute-start | bytes 393224 | tf_op jit(solution)/shard_map/ppermute | solution.py:341
  11.0 5.9 %collective-permute-start.5 = (bf16[4,64,256]{2,1,0:T(8,128)(2,1)S(1)}, bf16[4,64,256]{2,1,0:T(8,128)(2,1)S(1)}, u32[]{:S(2)}, u32[]{:S(2)}) collective-permute-start(bf16[4,64,256]{2,1,0:T(8,128)(2,1)S(1)} %combine.1.total_ref), channel_id=1, source_target_pairs={{0,6},{1,7},{2,4},{3,5},{4,2},{5,3},{6,0},{7,1},{8,14},{9,15},{10,... | collective-permute-start | bytes 393224 | tf_op jit(solution)/shard_map/ppermute | solution.py:341
  13.8 2.2 %copy-start.2 = (bf16[1024,512]{1,0:T(8,128)(2,1)S(1)}, bf16[1024,512]{1,0:T(8,128)(2,1)}, u32[]{:S(2)}) copy-start(bf16[1024,512]{1,0:T(8,128)(2,1)} %close_ref.3) | copy-start | bytes 3145732
  17.1 2.7 %collective-permute-start.6 = (bf16[4,64,256]{2,1,0:T(8,128)(2,1)S(1)}, bf16[4,64,256]{2,1,0:T(8,128)(2,1)S(1)}, u32[]{:S(2)}, u32[]{:S(2)}) collective-permute-start(bf16[4,64,256]{2,1,0:T(8,128)(2,1)S(1)} %get-tuple-element.31), channel_id=1, source_target_pairs={{0,1},{1,0},{2,3},{3,2},{4,5},{5,4},{6,7},{7,6},{8,9},{9,8},{10,11... | collective-permute-start | bytes 393224 | tf_op jit(solution)/shard_map/ppermute | solution.py:341

commit v10 on v9

--- a/solution.py
+++ b/solution.py
@@ -219,54 +219,42 @@
     neighbours(breadth, q_ref, [(k_ref, v_ref, mask_ref.at[0])], row_ref, emit)
 
 
-def even_kernel(breadth, x_ref, w_ref, means_ref, q_ref, row_ref, mask_ref, acc_ref, keep_ref, sum_ref, kept_ref, k_ref, v_ref):
-    groups = x_ref.shape[0]
-    keys_values(x_ref, w_ref, means_ref, k_ref, v_ref, breadth)
-
-    def emit(c, u, total):
-        at = (slice(None), slice(c * T, (c + 1) * T), slice(u * 2 * PAIR, (u + 1) * 2 * PAIR))
-        sum_ref[at] = acc_ref[at] + total.reshape(groups, T, 2 * PAIR)
-
-    neighbours(breadth, q_ref, [(k_ref, v_ref, mask_ref.at[1])], row_ref, emit)
-
-
 def odd_partner():
     station = lax.axis_index("stations")
     partner = station + 2 * (station % 2) - 1
     return (partner >= 0) & (partner < lax.axis_size("stations"))
 
 
-def odd_keys_kernel(breadth, x_ref, w_ref, means_ref, keep_ref, close_ref, k_ref, v_ref, kept_ref):
+def odd_keys_kernel(breadth, x_ref, w_ref, means_ref, keep_ref, close_ref, acc_ref, k_ref, v_ref, kept_ref):
     @pl.when(odd_partner())
     def _():
         keys_values(x_ref, w_ref, means_ref, k_ref, v_ref, breadth)
 
 
-def odd_kernel(breadth, k_ref, v_ref, q_ref, row_ref, mask_ref, acc_ref, gathered_ref):
-    groups, patches, width = q_ref.shape
-    there = odd_partner()
-
-    def part(c, u):
-        return (slice(None), slice(c * T, (c + 1) * T), slice(u * 2 * PAIR, (u + 1) * 2 * PAIR))
-
-    def finish(c, u, total):
+def even_keys_kernel(breadth, x_ref, w_ref, means_ref, mine_ref, k_ref, v_ref):
+    keys_values(x_ref, w_ref, means_ref, k_ref, v_ref, breadth)
+
+
+def halo_kernel(breadth, ke_ref, ve_ref, ko_ref, vo_ref, q_ref, row_ref, mask_ref, acc_ref, gathered_ref):
+    groups = q_ref.shape[0]
+    even = (ke_ref, ve_ref, mask_ref.at[1])
+    odd = (ko_ref, vo_ref, mask_ref.at[2])
+
+    def emit(c, u, total):
+        span = slice(c * T, (c + 1) * T)
+        total = acc_ref[:, span, u * 2 * PAIR : (u + 1) * 2 * PAIR] + total.reshape(groups, T, 2 * PAIR)
         share, weight = total[:, :, :PAIR], total[:, :, PAIR:]
         near = pl.reciprocal(weight, approx=True)
         share = share * (near * (2.0 - weight * near))
-        gathered_ref[:, c * T : (c + 1) * T, u * PAIR : (u + 1) * PAIR] = share.astype(BF16)
-
-    @pl.when(there)
+        gathered_ref[:, span, u * PAIR : (u + 1) * PAIR] = share.astype(BF16)
+
+    @pl.when(odd_partner())
     def _():
-        def emit(c, u, total):
-            finish(c, u, acc_ref[part(c, u)] + total.reshape(groups, T, 2 * PAIR))
-
-        neighbours(breadth, q_ref, [(k_ref, v_ref, mask_ref.at[2])], row_ref, emit)
-
-    @pl.when(jnp.logical_not(there))
+        neighbours(breadth, q_ref, [even, odd], row_ref, emit)
+
+    @pl.when(jnp.logical_not(odd_partner()))
     def _():
-        for u in range(width // PAIR):
-            for c in range(patches // T):
-                finish(c, u, acc_ref[part(c, u)])
+        neighbours(breadth, q_ref, [even], row_ref, emit)
 
 
 def closing_kernel(breadth, q_ref, lin_ref, mine_ref, other_ref, means_ref, close_ref, x_ref, gathered_ref, out_hbm, out_ref, sem):
@@ -375,26 +363,27 @@
         through={3: None},
     )
     (acc,) = call(near_kernel, breadth, [(sums, F32)], (k, v, q, rows, masks), name="near")
-    acc, keep = call(
-        even_kernel,
-        breadth,
-        [(sums, F32), (part, F32)],
-        (x_even, w, means, q, rows, masks, acc, keep),
-        [(block, BF16)] * 2,
-        name="even",
-        through={7: 1},
-    )
     k_odd, v_odd, keep = call(
         odd_keys_kernel,
         breadth,
         [(block, BF16)] * 2 + [(part, F32)],
-        (x_odd, w, means, keep, close),
-        name="keys",
-        through={3: 2, 4: None},
+        (x_odd, w, means, keep, close, acc),
+        name="odd",
+        through={3: 2, 4: None, 5: None},
     )
     send, mine = call(carry_kernel, breadth, [(part, BF16)] * 2, (keep, got, *pieces), name="carry")
     other = swap_with(send, "tm", lambda i: i ^ 1)
-    (gathered,) = call(odd_kernel, breadth, [(block, BF16)], (k_odd, v_odd, q, rows, masks, acc), name="odd")
+    k_even, v_even = call(
+        even_keys_kernel,
+        breadth,
+        [(block, BF16)] * 2,
+        (x_even, w, means, mine),
+        name="even",
+        through={3: None},
+    )
+    (gathered,) = call(
+        halo_kernel, breadth, [(block, BF16)], (k_even, v_even, k_odd, v_odd, q, rows, masks, acc), name="halo"
+    )
     (out,) = call(
         closing_kernel,
         breadth,

time: 22 us -> 23.7 us (1.077)
  the two profiles are of different devices: /device:TPU:9 before, /device:TPU:1 now
where the time goes in v10:
time: 23.7 us; the launch traced here: 23.6 us
  starting transfers between devices  11.2 us (47%)
  Pallas kernels  8.08 us (34%)
  waiting for transfers between devices  3.97 us (17%)
    ppermute x7, starting transfers between devices, swap_with(): return lax.ppermute(value, axis, pairs)  11.2 us
    pallas_call x11, Pallas kernels, call(): pl.pallas_call(functools.partial(kernel, breadth), out_shape=[jax.ShapeDt...  8.08 us
    ppermute x7, waiting for transfers between devices, swap_with(): return lax.ppermute(value, axis, pairs)  3.97 us
  transfers between devices with their start and end apart: 7, of which 3 were waited for; matrix products, arithmetic and copies ran while one was open for 0% of the time, Pallas kernels for 27%

profile of v10, /device:TPU:1, one launch (start us, length us, event | category | flops | bytes accessed | tf_op | source)
XLA Modules:
  0.0 23.6 jit_solution(16000279673000022032)
XLA Ops:
  0.0 0.8 %collective-permute-start.1 = (bf16[4,128,512]{2,1,0:T(8,128)(2,1)}, bf16[4,128,512]{2,1,0:T(8,128)(2,1)S(1)}, u32[]{:S(2)}, u32[]{:S(2)}) collective-permute-start(bf16[4,128,512]{2,1,0:T(8,128)(2,1)} %x_ref.5), channel_id=1, source_target_pairs={{8,16},{16,8},{9,17},{17,9},{10,18},{18,10},{11,19},{19,11},{12,20... | collective-permute-start | bytes 1572872 | tf_op jit(solution)/shard_map/ppermute | solution.py:329
  0.8 4.7 %collective-permute-start.6 = (bf16[4,128,512]{2,1,0:T(8,128)(2,1)}, bf16[4,128,512]{2,1,0:T(8,128)(2,1)S(1)}, u32[]{:S(2)}, u32[]{:S(2)}) collective-permute-start(bf16[4,128,512]{2,1,0:T(8,128)(2,1)} %x_ref.5), channel_id=1, source_target_pairs={{0,8},{8,0},{16,24},{24,16},{1,9},{9,1},{17,25},{25,17},{2,10},{10... | collective-permute-start | bytes 1572872 | tf_op jit(solution)/shard_map/ppermute | solution.py:329
  5.6 1.6 %states.1 = (bf16[4,128,512]{2,1,0:T(8,128)(2,1)S(1)}, bf16[4,128,512]{2,1,0:T(8,128)(2,1)S(1)}, f32[4,64,256]{2,1,0:T(8,128)S(1)}, bf16[4,64,256]{2,1,0:T(8,128)(2,1)S(1)}) custom-call(bf16[4,128,512]{2,1,0:T(8,128)(2,1)S(1)} %copy-done.1, bf16[512,1536]{1,0:T(8,128)(2,1)S(1)} %copy-done, bf16[256,256]{1,0:T(8,128)(2,1)S(1)} %means.1.means_ref), custom_call_target="tpu_custom_call" | custom-call | flops 1000000 | bytes 4096 | tf_op jit(solution)/shard_map/states/pallas_call | solution.py:313
  7.2 0.0 copy-start.3
  7.2 0.0 copy-start.4
  7.2 0.0 copy-start.5
  7.2 1.3 %collective-permute-start = (bf16[4,64,256]{2,1,0:T(8,128)(2,1)S(1)}, bf16[4,64,256]{2,1,0:T(8,128)(2,1)S(1)}, u32[]{:S(2)}, u32[]{:S(2)}) collective-permute-start(bf16[4,64,256]{2,1,0:T(8,128)(2,1)S(1)} %get-tuple-element.23), channel_id=1, source_target_pairs={{0,1},{1,0},{2,3},{3,2},{4,5},{5,4},{6,7},{7,6},{8,9},{9,8},{10,11... | collective-permute-start | bytes 393224 | tf_op jit(solution)/shard_map/ppermute | solution.py:329
  8.5 1.0 %collective-permute-done.got_ref = bf16[4,64,256]{2,1,0:T(8,128)(2,1)S(1)} collective-permute-done((bf16[4,64,256]{2,1,0:T(8,128)(2,1)S(1)}, bf16[4,64,256]{2,1,0:T(8,128)(2,1)S(1)}, u32[]{:S(2)}, u32[]{:S(2)}) %collective-permute-start) | collective-permute-done | bytes 131104 | tf_op jit(solution)/shard_map/ppermute | solution.py:329
  9.6 1.3 %collective-permute-start.2 = (bf16[4,64,256]{2,1,0:T(8,128)(2,1)S(1)}, bf16[4,64,256]{2,1,0:T(8,128)(2,1)S(1)}, u32[]{:S(2)}, u32[]{:S(2)}) collective-permute-start(bf16[4,64,256]{2,1,0:T(8,128)(2,1)S(1)} %combine.1.total_ref), channel_id=1, source_target_pairs={{0,2},{1,3},{2,0},{3,1},{4,6},{5,7},{6,4},{7,5},{8,10},{9,11},{10,... | collective-permute-start | bytes 393224 | tf_op jit(solution)/shard_map/ppermute | solution.py:329
  10.8 1.2 %collective-permute-start.3 = (bf16[4,64,256]{2,1,0:T(8,128)(2,1)S(1)}, bf16[4,64,256]{2,1,0:T(8,128)(2,1)S(1)}, u32[]{:S(2)}, u32[]{:S(2)}) collective-permute-start(bf16[4,64,256]{2,1,0:T(8,128)(2,1)S(1)} %combine.1.total_ref), channel_id=1, source_target_pairs={{0,4},{1,5},{2,6},{3,7},{4,0},{5,1},{6,2},{7,3},{8,12},{9,13},{10,... | collective-permute-start | bytes 393224 | tf_op jit(solution)/shard_map/ppermute | solution.py:329
  12.1 0.2 collective-permute-start.4
  12.3 1.4 %own.1 = (bf16[4,128,512]{2,1,0:T(8,128)(2,1)S(1)}, f32[4,128,512]{2,1,0:T(8,128)S(1)}) custom-call(bf16[4,128,512]{2,1,0:T(8,128)(2,1)S(1)} %copy-done.1, bf16[512,1536]{1,0:T(8,128)(2,1)S(1)} %copy-done, bf16[256,256]{1,0:T(8,128)(2,1)S(1)} %means.1.means_ref, bf16[4,128,512]{2,1,0:T(8,128)(2,1)S(1)} %get-tuple-element.20.k_ref, ...), custom_call_target="tpu_custom_call" | custom-call | flops 1000000 | bytes 4096 | tf_op jit(solution)/shard_map/own/pallas_call | solution.py:313
  13.7 0.0 copy-start.2
  13.7 0.2 masks.1
  14.0 0.9 %near.1.acc_ref = f32[4,128,1024]{2,1,0:T(8,128)S(1)} custom-call(bf16[4,128,512]{2,1,0:T(8,128)(2,1)S(1)} %get-tuple-element.20.k_ref, bf16[4,128,512]{2,1,0:T(8,128)(2,1)S(1)} %get-tuple-element.21.v_ref, bf16[4,128,512]{2,1,0:T(8,128)(2,1)S(1)} %get-tuple-element.24.q_ref, f32[4,256]{1,0:T(4,128)S(1)} %get-tuple-element.26.row_ref, ...), custom_call_target="tpu_custom_call" | custom-call | flops 1000000 | bytes 4096 | tf_op jit(solution)/shard_map/near/pallas_call | solution.py:313
  14.8 0.1 copy-done.2
  15.0 0.0 collective-permute-done.2.refs_0_
  15.0 0.3 %collective-permute-done.3.refs_1_ = bf16[4,64,256]{2,1,0:T(8,128)(2,1)S(1)} collective-permute-done((bf16[4,64,256]{2,1,0:T(8,128)(2,1)S(1)}, bf16[4,64,256]{2,1,0:T(8,128)(2,1)S(1)}, u32[]{:S(2)}, u32[]{:S(2)}) %collective-permute-start.3) | collective-permute-done | bytes 131104 | tf_op jit(solution)/shard_map/ppermute | solution.py:329
  15.2 2.7 %collective-permute-done.4.refs_2_ = bf16[4,64,256]{2,1,0:T(8,128)(2,1)S(1)} collective-permute-done((bf16[4,64,256]{2,1,0:T(8,128)(2,1)S(1)}, bf16[4,64,256]{2,1,0:T(8,128)(2,1)S(1)}, u32[]{:S(2)}, u32[]{:S(2)}) %collective-permute-start.4) | collective-permute-done | bytes 131104 | tf_op jit(solution)/shard_map/ppermute | solution.py:329
  17.9 0.1 carry.1
  18.1 1.7 %collective-permute-start.5 = (bf16[4,64,256]{2,1,0:T(8,128)(2,1)S(1)}, bf16[4,64,256]{2,1,0:T(8,128)(2,1)S(1)}, u32[]{:S(2)}, u32[]{:S(2)}) collective-permute-start(bf16[4,64,256]{2,1,0:T(8,128)(2,1)S(1)} %get-tuple-element.30), channel_id=1, source_target_pairs={{0,1},{1,0},{2,3},{3,2},{4,5},{5,4},{6,7},{7,6},{8,9},{9,8},{10,11... | collective-permute-start | bytes 393224 | tf_op jit(solution)/shard_map/ppermute | solution.py:329
  19.8 0.9 %even.1 = (bf16[4,128,512]{2,1,0:T(8,128)(2,1)S(1)}, bf16[4,128,512]{2,1,0:T(8,128)(2,1)S(1)}) custom-call(bf16[4,128,512]{2,1,0:T(8,128)(2,1)S(1)} %collective-permute-done.6.x_ref, bf16[512,1536]{1,0:T(8,128)(2,1)S(1)} %copy-done, bf16[256,256]{1,0:T(8,128)(2,1)S(1)} %means.1.means_ref, bf16[4,64,256]{2,1,0:T(8,128)(2,1)S(1)} %get-tuple-element.29.mine_ref), custom_call_target="tpu_custom_call" | custom-call | flops 1000000 | bytes 4096 | tf_op jit(solution)/shard_map/even/pallas_call | solution.py:313
  20.7 1.0 %halo.1.gathered_ref = bf16[4,128,512]{2,1,0:T(8,128)(2,1)S(1)} custom-call(bf16[4,128,512]{2,1,0:T(8,128)(2,1)S(1)} %get-tuple-element.31.ke_ref, bf16[4,128,512]{2,1,0:T(8,128)(2,1)S(1)} %get-tuple-element.32.ve_ref, bf16[4,128,512]{2,1,0:T(8,128)(2,1)S(1)} %get-tuple-element.33.ko_ref, bf16[4,128,512]{2,1,0:T(8,128)(2,1)S(1)} %get-tuple-element.34.vo_ref, ...), custom_call_target="tpu_custom_call" | custom-call | flops 1000000 | bytes 4096 | tf_op jit(solution)/shard_map/halo/pallas_call | solution.py:313
  21.8 1.8 %closing.1 = bf16[4,128,512]{2,1,0:T(8,128)(2,1)} custom-call(bf16[4,128,512]{2,1,0:T(8,128)(2,1)S(1)} %get-tuple-element.24.q_ref, f32[4,128,512]{2,1,0:T(8,128)S(1)} %get-tuple-element.25.lin_ref, bf16[4,64,256]{2,1,0:T(8,128)(2,1)S(1)} %get-tuple-element.29.mine_ref, bf16[4,64,256]{2,1,0:T(8,128)(2,1)S(1)} %collective-permute-done.5.other_ref, ...), custom_call_target="tpu_custom_call" | custom-call | flops 1000000 | bytes 4096 | tf_op jit(solution)/shard_map/closing/pallas_call | solution.py:313
  (13 shorter events, 0.1 us)
Async XLA Ops:
  0.0 5.6 %copy-start.1 = (bf16[4,128,512]{2,1,0:T(8,128)(2,1)S(1)}, bf16[4,128,512]{2,1,0:T(8,128)(2,1)}, u32[]{:S(2)}) copy-start(bf16[4,128,512]{2,1,0:T(8,128)(2,1)} %x_ref.5) | copy-start | bytes 1572868
  0.0 5.6 %copy-start = (bf16[512,1536]{1,0:T(8,128)(2,1)S(1)}, bf16[512,1536]{1,0:T(8,128)(2,1)}, u32[]{:S(2)}) copy-start(bf16[512,1536]{1,0:T(8,128)(2,1)} %w_ref.7) | copy-start | bytes 4718596
  0.0 14.8 %collective-permute-start.1 = (bf16[4,128,512]{2,1,0:T(8,128)(2,1)}, bf16[4,128,512]{2,1,0:T(8,128)(2,1)S(1)}, u32[]{:S(2)}, u32[]{:S(2)}) collective-permute-start(bf16[4,128,512]{2,1,0:T(8,128)(2,1)} %x_ref.5), channel_id=1, source_target_pairs={{8,16},{16,8},{9,17},{17,9},{10,18},{18,10},{11,19},{19,11},{12,20... | collective-permute-start | bytes 1572872 | tf_op jit(solution)/shard_map/ppermute | solution.py:329
  0.8 18.9 %collective-permute-start.6 = (bf16[4,128,512]{2,1,0:T(8,128)(2,1)}, bf16[4,128,512]{2,1,0:T(8,128)(2,1)S(1)}, u32[]{:S(2)}, u32[]{:S(2)}) collective-permute-start(bf16[4,128,512]{2,1,0:T(8,128)(2,1)} %x_ref.5), channel_id=1, source_target_pairs={{0,8},{8,0},{16,24},{24,16},{1,9},{9,1},{17,25},{25,17},{2,10},{10... | collective-permute-start | bytes 1572872 | tf_op jit(solution)/shard_map/ppermute | solution.py:329
  7.2 6.5 %copy-start.3 = (s32[4,8]{1,0:T(4,128)S(1)}, s32[4,8]{1,0:T(4,128)}, u32[]{:S(2)}) copy-start(s32[4,8]{1,0:T(4,128)} %table_ref.1) | copy-start | bytes 388
  7.2 6.5 %copy-start.4 = (s32[4]{0:T(128)S(1)}, s32[4]{0:T(128)}, u32[]{:S(2)}) copy-start(s32[4]{0:T(128)} %param.11) | copy-start | bytes 52
  7.2 6.5 %copy-start.5 = (f32[8]{0:T(128)S(1)}, f32[8]{0:T(128)}, u32[]{:S(2)}) copy-start(f32[8]{0:T(128)} %param.9) | copy-start | bytes 100
  7.2 2.3 %collective-permute-start = (bf16[4,64,256]{2,1,0:T(8,128)(2,1)S(1)}, bf16[4,64,256]{2,1,0:T(8,128)(2,1)S(1)}, u32[]{:S(2)}, u32[]{:S(2)}) collective-permute-start(bf16[4,64,256]{2,1,0:T(8,128)(2,1)S(1)} %get-tuple-element.23), channel_id=1, source_target_pairs={{0,1},{1,0},{2,3},{3,2},{4,5},{5,4},{6,7},{7,6},{8,9},{9,8},{10,11... | collective-permute-start | bytes 393224 | tf_op jit(solution)/shard_map/ppermute | solution.py:329
  9.6 5.4 %collective-permute-start.2 = (bf16[4,64,256]{2,1,0:T(8,128)(2,1)S(1)}, bf16[4,64,256]{2,1,0:T(8,128)(2,1)S(1)}, u32[]{:S(2)}, u32[]{:S(2)}) collective-permute-start(bf16[4,64,256]{2,1,0:T(8,128)(2,1)S(1)} %combine.1.total_ref), channel_id=1, source_target_pairs={{0,2},{1,3},{2,0},{3,1},{4,6},{5,7},{6,4},{7,5},{8,10},{9,11},{10,... | collective-permute-start | bytes 393224 | tf_op jit(solution)/shard_map/ppermute | solution.py:329
  10.8 4.4 %collective-permute-start.3 = (bf16[4,64,256]{2,1,0:T(8,128)(2,1)S(1)}, bf16[4,64,256]{2,1,0:T(8,128)(2,1)S(1)}, u32[]{:S(2)}, u32[]{:S(2)}) collective-permute-start(bf16[4,64,256]{2,1,0:T(8,128)(2,1)S(1)} %combine.1.total_ref), channel_id=1, source_target_pairs={{0,4},{1,5},{2,6},{3,7},{4,0},{5,1},{6,2},{7,3},{8,12},{9,13},{10,... | collective-permute-start | bytes 393224 | tf_op jit(solution)/shard_map/ppermute | solution.py:329
  12.1 5.9 %collective-permute-start.4 = (bf16[4,64,256]{2,1,0:T(8,128)(2,1)S(1)}, bf16[4,64,256]{2,1,0:T(8,128)(2,1)S(1)}, u32[]{:S(2)}, u32[]{:S(2)}) collective-permute-start(bf16[4,64,256]{2,1,0:T(8,128)(2,1)S(1)} %combine.1.total_ref), channel_id=1, source_target_pairs={{0,6},{1,7},{2,4},{3,5},{4,2},{5,3},{6,0},{7,1},{8,14},{9,15},{10,... | collective-permute-start | bytes 393224 | tf_op jit(solution)/shard_map/ppermute | solution.py:329
  13.7 1.2 %copy-start.2 = (bf16[1024,512]{1,0:T(8,128)(2,1)S(1)}, bf16[1024,512]{1,0:T(8,128)(2,1)}, u32[]{:S(2)}) copy-start(bf16[1024,512]{1,0:T(8,128)(2,1)} %close_ref.3) | copy-start | bytes 3145732
  18.1 3.7 %collective-permute-start.5 = (bf16[4,64,256]{2,1,0:T(8,128)(2,1)S(1)}, bf16[4,64,256]{2,1,0:T(8,128)(2,1)S(1)}, u32[]{:S(2)}, u32[]{:S(2)}) collective-permute-start(bf16[4,64,256]{2,1,0:T(8,128)(2,1)S(1)} %get-tuple-element.30), channel_id=1, source_target_pairs={{0,1},{1,0},{2,3},{3,2},{4,5},{5,4},{6,7},{7,6},{8,9},{9,8},{10,11... | collective-permute-start | bytes 393224 | tf_op jit(solution)/shard_map/ppermute | solution.py:329

commit v11 on v9

--- a/solution.py
+++ b/solution.py
@@ -32,6 +32,11 @@
 def row_norm(x):
     xf = x.astype(F32)
     return (xf * lax.rsqrt(jnp.mean(xf * xf, axis=-1, keepdims=True) + 1e-06)).astype(BF16)
+
+
+def row_scale(x):
+    xf = x.astype(F32)
+    return lax.rsqrt(jnp.mean(xf * xf, axis=-1, keepdims=True) + 1e-06)
 
 
 def head_ids(shape, axis, breadth):
@@ -88,6 +93,20 @@
         at = slice(h * HALF, (h + 1) * HALF)
         v_ref[:, :, at] = values[h].astype(BF16).reshape(groups, patches, HALF)
         k_ref[:, :, at] = norm(keys[h], means, 1e-06).reshape(groups, patches, HALF)
+
+
+def halo_keys_values(x_ref, w_ref, means_ref, k_ref, v_ref, breadth):
+    groups, patches, width = x_ref.shape
+    halves = width // HALF
+    means = means_ref[...]
+    rows = x_ref[...].reshape(groups * patches, width)
+    keys = project(rows, w_ref, width, halves)
+    values = project(rows, w_ref, 2 * width, halves)
+    scale = row_scale(rows)
+    for h in range(halves):
+        at = slice(h * HALF, (h + 1) * HALF)
+        v_ref[:, :, at] = (values[h] * scale).astype(BF16).reshape(groups, patches, HALF)
+        k_ref[:, :, at] = head_norm(keys[h] * scale, means, 1e-06).reshape(groups, patches, HALF)
 
 
 def staggered(items, *stages):
@@ -221,7 +240,7 @@
 
 def even_kernel(breadth, x_ref, w_ref, means_ref, q_ref, row_ref, mask_ref, acc_ref, keep_ref, sum_ref, kept_ref, k_ref, v_ref):
     groups = x_ref.shape[0]
-    keys_values(x_ref, w_ref, means_ref, k_ref, v_ref, breadth)
+    halo_keys_values(x_ref, w_ref, means_ref, k_ref, v_ref, breadth)
 
     def emit(c, u, total):
         at = (slice(None), slice(c * T, (c + 1) * T), slice(u * 2 * PAIR, (u + 1) * 2 * PAIR))
@@ -239,7 +258,7 @@
 def odd_keys_kernel(breadth, x_ref, w_ref, means_ref, keep_ref, close_ref, k_ref, v_ref, kept_ref):
     @pl.when(odd_partner())
     def _():
-        keys_values(x_ref, w_ref, means_ref, k_ref, v_ref, breadth)
+        halo_keys_values(x_ref, w_ref, means_ref, k_ref, v_ref, breadth)
 
 
 def odd_kernel(breadth, k_ref, v_ref, q_ref, row_ref, mask_ref, acc_ref, gathered_ref):

time: 22 us -> 21.9 us (level)
  transfers between devices with their start and end apart: 7 -> 7, of which waited for: 2 -> 2; matrix products, arithmetic and copies ran while one was open for 0% -> 0% of each run, Pallas kernels for 37% -> 36%
where the time goes in v11:
time: 21.9 us; the launch traced here: 21.7 us
  starting transfers between devices  10.1 us (46%)
  Pallas kernels  9.83 us (45%)
  waiting for transfers between devices  1.45 us (7%)
    ppermute x7, starting transfers between devices, swap_with(): return lax.ppermute(value, axis, pairs)  10.1 us
    pallas_call x11, Pallas kernels, call(): pl.pallas_call(functools.partial(kernel, breadth), out_shape=[jax.ShapeDt...  9.83 us
    ppermute x7, waiting for transfers between devices, swap_with(): return lax.ppermute(value, axis, pairs)  1.45 us
  transfers between devices with their start and end apart: 7, of which 2 were waited for; matrix products, arithmetic and copies ran while one was open for 0% of the time, Pallas kernels for 36%

profile of v11, /device:TPU:9, one launch (start us, length us, event | category | flops | bytes accessed | tf_op | source)
XLA Modules:
  0.0 21.7 jit_solution(2418099468286078737)
XLA Ops:
  0.0 4.5 %collective-permute-start.1 = (bf16[4,128,512]{2,1,0:T(8,128)(2,1)}, bf16[4,128,512]{2,1,0:T(8,128)(2,1)S(1)}, u32[]{:S(2)}, u32[]{:S(2)}) collective-permute-start(bf16[4,128,512]{2,1,0:T(8,128)(2,1)} %x_ref.5), channel_id=1, source_target_pairs={{8,16},{16,8},{9,17},{17,9},{10,18},{18,10},{11,19},{19,11},{12,20... | collective-permute-start | bytes 1572872 | tf_op jit(solution)/shard_map/ppermute | solution.py:360
  4.6 1.6 %states.1 = (bf16[4,128,512]{2,1,0:T(8,128)(2,1)S(1)}, bf16[4,128,512]{2,1,0:T(8,128)(2,1)S(1)}, f32[4,64,256]{2,1,0:T(8,128)S(1)}, bf16[4,64,256]{2,1,0:T(8,128)(2,1)S(1)}) custom-call(bf16[4,128,512]{2,1,0:T(8,128)(2,1)S(1)} %copy-done.1, bf16[512,1536]{1,0:T(8,128)(2,1)S(1)} %copy-done, bf16[256,256]{1,0:T(8,128)(2,1)S(1)} %means.1.means_ref), custom_call_target="tpu_custom_call" | custom-call | flops 1000000 | bytes 4096 | tf_op jit(solution)/shard_map/states/pallas_call | solution.py:344
  6.2 0.0 copy-start.3
  6.2 0.0 copy-start.4
  6.2 0.0 copy-start.5
  6.2 1.3 %collective-permute-start = (bf16[4,64,256]{2,1,0:T(8,128)(2,1)S(1)}, bf16[4,64,256]{2,1,0:T(8,128)(2,1)S(1)}, u32[]{:S(2)}, u32[]{:S(2)}) collective-permute-start(bf16[4,64,256]{2,1,0:T(8,128)(2,1)S(1)} %get-tuple-element.23), channel_id=1, source_target_pairs={{0,1},{1,0},{2,3},{3,2},{4,5},{5,4},{6,7},{7,6},{8,9},{9,8},{10,11... | collective-permute-start | bytes 393224 | tf_op jit(solution)/shard_map/ppermute | solution.py:360
  7.5 1.0 %collective-permute-done.got_ref = bf16[4,64,256]{2,1,0:T(8,128)(2,1)S(1)} collective-permute-done((bf16[4,64,256]{2,1,0:T(8,128)(2,1)S(1)}, bf16[4,64,256]{2,1,0:T(8,128)(2,1)S(1)}, u32[]{:S(2)}, u32[]{:S(2)}) %collective-permute-start) | collective-permute-done | bytes 131104 | tf_op jit(solution)/shard_map/ppermute | solution.py:360
  8.5 1.3 %collective-permute-start.3 = (bf16[4,64,256]{2,1,0:T(8,128)(2,1)S(1)}, bf16[4,64,256]{2,1,0:T(8,128)(2,1)S(1)}, u32[]{:S(2)}, u32[]{:S(2)}) collective-permute-start(bf16[4,64,256]{2,1,0:T(8,128)(2,1)S(1)} %combine.1.total_ref), channel_id=1, source_target_pairs={{0,2},{1,3},{2,0},{3,1},{4,6},{5,7},{6,4},{7,5},{8,10},{9,11},{10,... | collective-permute-start | bytes 393224 | tf_op jit(solution)/shard_map/ppermute | solution.py:360
  9.8 1.2 %collective-permute-start.4 = (bf16[4,64,256]{2,1,0:T(8,128)(2,1)S(1)}, bf16[4,64,256]{2,1,0:T(8,128)(2,1)S(1)}, u32[]{:S(2)}, u32[]{:S(2)}) collective-permute-start(bf16[4,64,256]{2,1,0:T(8,128)(2,1)S(1)} %combine.1.total_ref), channel_id=1, source_target_pairs={{0,4},{1,5},{2,6},{3,7},{4,0},{5,1},{6,2},{7,3},{8,12},{9,13},{10,... | collective-permute-start | bytes 393224 | tf_op jit(solution)/shard_map/ppermute | solution.py:360
  11.0 0.2 collective-permute-start.5
  11.2 1.4 %own.1 = (bf16[4,128,512]{2,1,0:T(8,128)(2,1)S(1)}, f32[4,128,512]{2,1,0:T(8,128)S(1)}) custom-call(bf16[4,128,512]{2,1,0:T(8,128)(2,1)S(1)} %copy-done.1, bf16[512,1536]{1,0:T(8,128)(2,1)S(1)} %copy-done, bf16[256,256]{1,0:T(8,128)(2,1)S(1)} %means.1.means_ref, bf16[4,128,512]{2,1,0:T(8,128)(2,1)S(1)} %get-tuple-element.20.k_ref, ...), custom_call_target="tpu_custom_call" | custom-call | flops 1000000 | bytes 4096 | tf_op jit(solution)/shard_map/own/pallas_call | solution.py:344
  12.7 0.2 %masks.1 = (f32[3,128,256]{2,1,0:T(8,128)S(1)}, f32[4,256]{1,0:T(4,128)S(1)}) custom-call(s32[4,8]{1,0:T(4,128)S(1)} %copy-done.3, s32[1,4]{1,0:T(1,128)S(1)} %bitcast.2, f32[1,8]{1,0:T(1,128)S(1)} %bitcast.3, bf16[4,64,256]{2,1,0:T(8,128)(2,1)S(1)} %combine.1.total_ref), custom_call_target="tpu_custom_call" | custom-call | flops 1000000 | bytes 4096 | tf_op jit(solution)/shard_map/masks/pallas_call | solution.py:344
  13.0 0.8 %near.1.acc_ref = f32[4,128,1024]{2,1,0:T(8,128)S(1)} custom-call(bf16[4,128,512]{2,1,0:T(8,128)(2,1)S(1)} %get-tuple-element.20.k_ref, bf16[4,128,512]{2,1,0:T(8,128)(2,1)S(1)} %get-tuple-element.21.v_ref, bf16[4,128,512]{2,1,0:T(8,128)(2,1)S(1)} %get-tuple-element.24.q_ref, f32[4,256]{1,0:T(4,128)S(1)} %get-tuple-element.26.row_ref, ...), custom_call_target="tpu_custom_call" | custom-call | flops 1000000 | bytes 4096 | tf_op jit(solution)/shard_map/near/pallas_call | solution.py:344
  13.8 0.0 copy-start.2
  13.8 1.7 %even.1 = (f32[4,128,1024]{2,1,0:T(8,128)S(1)}, f32[4,64,256]{2,1,0:T(8,128)S(1)}) custom-call(bf16[4,128,512]{2,1,0:T(8,128)(2,1)S(1)} %collective-permute-done.2.x_ref, bf16[512,1536]{1,0:T(8,128)(2,1)S(1)} %copy-done, bf16[256,256]{1,0:T(8,128)(2,1)S(1)} %means.1.means_ref, ...), custom_call_target="tpu_custom_call", output_to_operand_aliasing={{1}: (7, {})} | custom-call | flops 1000000 | bytes 4096 | tf_op jit(solution)/shard_map/even/pallas_call | solution.py:344
  15.6 0.5 %collective-permute-done.1.x_ref = bf16[4,128,512]{2,1,0:T(8,128)(2,1)S(1)} collective-permute-done((bf16[4,128,512]{2,1,0:T(8,128)(2,1)}, bf16[4,128,512]{2,1,0:T(8,128)(2,1)S(1)}, u32[]{:S(2)}, u32[]{:S(2)}) %collective-permute-start.1) | collective-permute-done | bytes 524320 | tf_op jit(solution)/shard_map/ppermute | solution.py:360
  16.0 0.9 %keys.1 = (bf16[4,128,512]{2,1,0:T(8,128)(2,1)S(1)}, bf16[4,128,512]{2,1,0:T(8,128)(2,1)S(1)}, f32[4,64,256]{2,1,0:T(8,128)S(1)}) custom-call(bf16[4,128,512]{2,1,0:T(8,128)(2,1)S(1)} %collective-permute-done.1.x_ref, bf16[512,1536]{1,0:T(8,128)(2,1)S(1)} %copy-done, bf16[256,256]{1,0:T(8,128)(2,1)S(1)} %means.1.means_ref, ...), custom_call_target="tpu_custom_call", output_to_operand_aliasing={{2}: (3, {})} | custom-call | flops 1000000 | bytes 4096 | tf_op jit(solution)/shard_map/keys/pallas_call | solution.py:344
  16.9 0.0 collective-permute-done.3.refs_0_
  16.9 0.0 collective-permute-done.5.refs_2_
  16.9 0.1 carry.1
  17.1 1.6 %collective-permute-start.6 = (bf16[4,64,256]{2,1,0:T(8,128)(2,1)S(1)}, bf16[4,64,256]{2,1,0:T(8,128)(2,1)S(1)}, u32[]{:S(2)}, u32[]{:S(2)}) collective-permute-start(bf16[4,64,256]{2,1,0:T(8,128)(2,1)S(1)} %get-tuple-element.31), channel_id=1, source_target_pairs={{0,1},{1,0},{2,3},{3,2},{4,5},{5,4},{6,7},{7,6},{8,9},{9,8},{10,11... | collective-permute-start | bytes 393224 | tf_op jit(solution)/shard_map/ppermute | solution.py:360
  18.7 1.0 %odd.1.gathered_ref = bf16[4,128,512]{2,1,0:T(8,128)(2,1)S(1)} custom-call(bf16[4,128,512]{2,1,0:T(8,128)(2,1)S(1)} %get-tuple-element.32.k_ref, bf16[4,128,512]{2,1,0:T(8,128)(2,1)S(1)} %get-tuple-element.33.v_ref, bf16[4,128,512]{2,1,0:T(8,128)(2,1)S(1)} %get-tuple-element.24.q_ref, f32[4,256]{1,0:T(4,128)S(1)} %get-tuple-element.26.row_ref, ...), custom_call_target="tpu_custom_call" | custom-call | flops 1000000 | bytes 4096 | tf_op jit(solution)/shard_map/odd/pallas_call | solution.py:344
  19.8 0.0 collective-permute-done.6.other_ref
  19.8 1.9 %closing.1 = bf16[4,128,512]{2,1,0:T(8,128)(2,1)} custom-call(bf16[4,128,512]{2,1,0:T(8,128)(2,1)S(1)} %get-tuple-element.24.q_ref, f32[4,128,512]{2,1,0:T(8,128)S(1)} %get-tuple-element.25.lin_ref, bf16[4,64,256]{2,1,0:T(8,128)(2,1)S(1)} %get-tuple-element.30.mine_ref, bf16[4,64,256]{2,1,0:T(8,128)(2,1)S(1)} %collective-permute-done.6.other_ref, ...), custom_call_target="tpu_custom_call" | custom-call | flops 1000000 | bytes 4096 | tf_op jit(solution)/shard_map/closing/pallas_call | solution.py:344
  (13 shorter events, 0.1 us)
Async XLA Ops:
  0.0 4.5 %copy-start.1 = (bf16[4,128,512]{2,1,0:T(8,128)(2,1)S(1)}, bf16[4,128,512]{2,1,0:T(8,128)(2,1)}, u32[]{:S(2)}) copy-start(bf16[4,128,512]{2,1,0:T(8,128)(2,1)} %x_ref.5) | copy-start | bytes 1572868
  0.0 4.6 %copy-start = (bf16[512,1536]{1,0:T(8,128)(2,1)S(1)}, bf16[512,1536]{1,0:T(8,128)(2,1)}, u32[]{:S(2)}) copy-start(bf16[512,1536]{1,0:T(8,128)(2,1)} %w_ref.7) | copy-start | bytes 4718596
  0.0 13.8 %collective-permute-start.2 = (bf16[4,128,512]{2,1,0:T(8,128)(2,1)}, bf16[4,128,512]{2,1,0:T(8,128)(2,1)S(1)}, u32[]{:S(2)}, u32[]{:S(2)}) collective-permute-start(bf16[4,128,512]{2,1,0:T(8,128)(2,1)} %x_ref.5), channel_id=1, source_target_pairs={{0,8},{8,0},{16,24},{24,16},{1,9},{9,1},{17,25},{25,17},{2,10},{10... | collective-permute-start | bytes 1572872 | tf_op jit(solution)/shard_map/ppermute | solution.py:360
  0.0 16.0 %collective-permute-start.1 = (bf16[4,128,512]{2,1,0:T(8,128)(2,1)}, bf16[4,128,512]{2,1,0:T(8,128)(2,1)S(1)}, u32[]{:S(2)}, u32[]{:S(2)}) collective-permute-start(bf16[4,128,512]{2,1,0:T(8,128)(2,1)} %x_ref.5), channel_id=1, source_target_pairs={{8,16},{16,8},{9,17},{17,9},{10,18},{18,10},{11,19},{19,11},{12,20... | collective-permute-start | bytes 1572872 | tf_op jit(solution)/shard_map/ppermute | solution.py:360
  6.2 6.5 %copy-start.3 = (s32[4,8]{1,0:T(4,128)S(1)}, s32[4,8]{1,0:T(4,128)}, u32[]{:S(2)}) copy-start(s32[4,8]{1,0:T(4,128)} %table_ref.1) | copy-start | bytes 388
  6.2 6.5 %copy-start.4 = (s32[4]{0:T(128)S(1)}, s32[4]{0:T(128)}, u32[]{:S(2)}) copy-start(s32[4]{0:T(128)} %param.11) | copy-start | bytes 52
  6.2 6.5 %copy-start.5 = (f32[8]{0:T(128)S(1)}, f32[8]{0:T(128)}, u32[]{:S(2)}) copy-start(f32[8]{0:T(128)} %param.9) | copy-start | bytes 100
  6.2 2.3 %collective-permute-start = (bf16[4,64,256]{2,1,0:T(8,128)(2,1)S(1)}, bf16[4,64,256]{2,1,0:T(8,128)(2,1)S(1)}, u32[]{:S(2)}, u32[]{:S(2)}) collective-permute-start(bf16[4,64,256]{2,1,0:T(8,128)(2,1)S(1)} %get-tuple-element.23), channel_id=1, source_target_pairs={{0,1},{1,0},{2,3},{3,2},{4,5},{5,4},{6,7},{7,6},{8,9},{9,8},{10,11... | collective-permute-start | bytes 393224 | tf_op jit(solution)/shard_map/ppermute | solution.py:360
  8.5 8.4 %collective-permute-start.3 = (bf16[4,64,256]{2,1,0:T(8,128)(2,1)S(1)}, bf16[4,64,256]{2,1,0:T(8,128)(2,1)S(1)}, u32[]{:S(2)}, u32[]{:S(2)}) collective-permute-start(bf16[4,64,256]{2,1,0:T(8,128)(2,1)S(1)} %combine.1.total_ref), channel_id=1, source_target_pairs={{0,2},{1,3},{2,0},{3,1},{4,6},{5,7},{6,4},{7,5},{8,10},{9,11},{10,... | collective-permute-start | bytes 393224 | tf_op jit(solution)/shard_map/ppermute | solution.py:360
  9.8 7.1 %collective-permute-start.4 = (bf16[4,64,256]{2,1,0:T(8,128)(2,1)S(1)}, bf16[4,64,256]{2,1,0:T(8,128)(2,1)S(1)}, u32[]{:S(2)}, u32[]{:S(2)}) collective-permute-start(bf16[4,64,256]{2,1,0:T(8,128)(2,1)S(1)} %combine.1.total_ref), channel_id=1, source_target_pairs={{0,4},{1,5},{2,6},{3,7},{4,0},{5,1},{6,2},{7,3},{8,12},{9,13},{10,... | collective-permute-start | bytes 393224 | tf_op jit(solution)/shard_map/ppermute | solution.py:360
  11.0 5.9 %collective-permute-start.5 = (bf16[4,64,256]{2,1,0:T(8,128)(2,1)S(1)}, bf16[4,64,256]{2,1,0:T(8,128)(2,1)S(1)}, u32[]{:S(2)}, u32[]{:S(2)}) collective-permute-start(bf16[4,64,256]{2,1,0:T(8,128)(2,1)S(1)} %combine.1.total_ref), channel_id=1, source_target_pairs={{0,6},{1,7},{2,4},{3,5},{4,2},{5,3},{6,0},{7,1},{8,14},{9,15},{10,... | collective-permute-start | bytes 393224 | tf_op jit(solution)/shard_map/ppermute | solution.py:360
  13.8 2.2 %copy-start.2 = (bf16[1024,512]{1,0:T(8,128)(2,1)S(1)}, bf16[1024,512]{1,0:T(8,128)(2,1)}, u32[]{:S(2)}) copy-start(bf16[1024,512]{1,0:T(8,128)(2,1)} %close_ref.3) | copy-start | bytes 3145732
  17.1 2.7 %collective-permute-start.6 = (bf16[4,64,256]{2,1,0:T(8,128)(2,1)S(1)}, bf16[4,64,256]{2,1,0:T(8,128)(2,1)S(1)}, u32[]{:S(2)}, u32[]{:S(2)}) collective-permute-start(bf16[4,64,256]{2,1,0:T(8,128)(2,1)S(1)} %get-tuple-element.31), channel_id=1, source_target_pairs={{0,1},{1,0},{2,3},{3,2},{4,5},{5,4},{6,7},{7,6},{8,9},{9,8},{10,11... | collective-permute-start | bytes 393224 | tf_op jit(solution)/shard_map/ppermute | solution.py:360
